TPU v7x, 32 devices: a whole 2x2x4 slice. The times are simulated.
32 devices in a mesh: lat: 8 (over y, x, core), lon: 4 (over z).
Axes of the slice: x: 2, y: 2, z: 4, core: 2. Of those that a mesh axis runs over, the one named last changes fastest.
Arguments:
- fields: bfloat16 [192, 512, 128], P('lat', 'lon'), may hold values from -6 to 6
- req_block: int32 [8, 4, 3, 1280], P('lat', 'lon'), may hold values from 0 to 191
- req_stencil: int32 [8, 4, 3, 4, 1280], P('lat', 'lon'), may hold values from 0 to 15
- req_frac: int32 [8, 4, 3, 2, 1280], P('lat', 'lon'), may hold values from 0 to 15
- req_count: int32 [8, 4, 3], P('lat', 'lon'), may hold values from 597 to 1280, as said below
- legendre: bfloat16 [1536, 192, 768], P(('lon', 'lat')), may hold values from -0.4375 to 0.4375
Outputs:
- spectral: float32 [1536, 768, 128], P(('lon', 'lat'))
Inputs may be any that keep to these rules, and one draw needn't show every extreme that they name: `req_count`: the three counts of a tile sum to 3072; positions j at or beyond a slot's count are unused. In every latitude band some tile receives 1280 points from each of the three tiles whose slots reach it, and every tile fills one slot to 1280.
All inputs are finite; a program needn't handle non-finite values.
Results may differ from a plain program's by a relative error of at most 0.0048.
Values may be sent and summed in bfloat16 or wider, within the bound.
No kernel may reach another device: no remote copies, remote signals or barrier semaphores. Data moves between devices by JAX's collectives and lax.ppermute only.
A program may use at most 128 MiB of HBM per device.

v0:
```python
import math

import jax
import jax.numpy as jnp
from jax import lax
from jax.sharding import PartitionSpec as P

KF = 1536
NN = 768
BLK = 16
FRAC = 16
COLS = 3072


def padded(cells, sides, width):
    for axis, dim in sides:
        count = lax.axis_size(axis)
        head = lax.slice_in_dim(cells, 0, width, axis=dim)
        tail = lax.slice_in_dim(cells, cells.shape[dim] - width, cells.shape[dim], axis=dim)
        cells = jnp.concatenate(
            [
                lax.ppermute(tail, axis, [(i, (i + 1) % count) for i in range(count)]),
                cells,
                lax.ppermute(head, axis, [((i + 1) % count, i) for i in range(count)]),
            ],
            axis=dim,
        )
    return cells


def hartley_table(lon_total):
    wave_index = jnp.arange(KF, dtype=jnp.int32)
    lon_index = jnp.arange(lon_total, dtype=jnp.int32)
    phase_index = wave_index[:, None] * lon_index[None, :] % lon_total
    phase_angle = 2.0 * math.pi / lon_total * phase_index.astype(jnp.float32)
    return ((jnp.cos(phase_angle) + jnp.sin(phase_angle)) / math.sqrt(lon_total)).astype(
        jnp.bfloat16
    )


def interpolate(own_tile, packed):
    cell_rows = packed[0][None, :] * BLK + packed[1:5]
    picked = jnp.take(own_tile, cell_rows.reshape(-1), axis=0).astype(jnp.float32)
    picked = picked.reshape(4, cell_rows.shape[1], own_tile.shape[1])
    frac_lat = (packed[5].astype(jnp.float32) + 0.5) / FRAC
    frac_lon = (packed[6].astype(jnp.float32) + 0.5) / FRAC
    weights = jnp.stack(
        [
            (1.0 - frac_lat) * (1.0 - frac_lon),
            frac_lat * (1.0 - frac_lon),
            (1.0 - frac_lat) * frac_lon,
            frac_lat * frac_lon,
        ]
    )
    return jnp.sum(weights[:, :, None] * picked, axis=0).astype(jnp.bfloat16)


def place_columns(values, counts):
    slot_ends = jnp.cumsum(counts)
    starts = slot_ends - counts
    column = jnp.arange(COLS, dtype=jnp.int32)
    slot_index = jnp.sum((slot_ends[None, :] <= column[:, None]).astype(jnp.int32), axis=1)
    onehot = slot_index[:, None] == jnp.arange(3, dtype=jnp.int32)[None, :]
    offset = column - jnp.sum(jnp.where(onehot, starts[None, :], 0), axis=1)
    flat_index = slot_index * values.shape[1] + offset
    return jnp.take(values.reshape(-1, values.shape[-1]), flat_index, axis=0)


def local(fields, req_block, req_stencil, req_frac, req_count, legendre):
    lat_rows, lon_cols, channels = fields.shape
    packed = jnp.concatenate(
        [req_block[0, 0][:, None, :], req_stencil[0, 0], req_frac[0, 0]], axis=1
    )
    counts = req_count[0, 0]
    widened = padded(fields, (("lon", 1),), lon_cols)
    slot_values = []
    for slot_index in range(3):
        owner_tile = widened[:, slot_index * lon_cols : (slot_index + 1) * lon_cols, :].reshape(
            -1, channels
        )
        slot_values.append(interpolate(owner_tile, packed[slot_index]))
    departed = place_columns(jnp.stack(slot_values), counts).reshape(lat_rows, lon_cols, channels)
    lon_total = lon_cols * lax.axis_size("lon")
    hartley = hartley_table(lon_total)
    spectra = jnp.einsum(
        "kx,yxc->ykc",
        hartley,
        lax.all_to_all(departed, "lon", split_axis=0, concat_axis=1, tiled=True),
        preferred_element_type=jnp.float32,
    )
    fourier = lax.all_to_all(
        spectra.astype(jnp.bfloat16), "lon", split_axis=1, concat_axis=0, tiled=True
    )
    gathered = lax.all_to_all(fourier, "lat", split_axis=1, concat_axis=0, tiled=True)
    projected = jnp.einsum("kyn,ykc->knc", legendre, gathered, preferred_element_type=jnp.float32)
    degree = jnp.arange(legendre.shape[2], dtype=jnp.float32)
    factor = 1.0 / (1.0 + 4.0 * degree * (degree + 1.0) / (NN * (NN + 1)))
    return projected * factor[None, :, None]


def solution(mesh):
    return jax.shard_map(
        local,
        mesh=mesh,
        in_specs=(
            P("lat", "lon", None),
            P("lat", "lon", None, None),
            P("lat", "lon", None, None, None),
            P("lat", "lon", None, None, None),
            P("lat", "lon", None),
            P(("lon", "lat"), None, None),
        ),
        out_specs=P(("lon", "lat"), None, None),
        check_vma=False,
    )
```

profile of v0, /device:TPU:0, one launch (start us, length us, event | category | flops | bytes accessed | tf_op | source)
XLA Modules:
  0.0 265.8 jit_solution(12394244312858558745)
XLA Ops:
  0.0 0.0 copy-start
  0.0 3.0 %collective-permute-start = (bf16[24,128,128]{2,1,0:T(8,128)(2,1)}, bf16[24,128,128]{2,1,0:T(8,128)(2,1)S(1)}, u32[]{:S(2)}, u32[]{:S(2)}) collective-permute-start(bf16[24,128,128]{2,1,0:T(8,128)(2,1)} %param.8), channel_id=1, source_target_pairs={{0,1},{1,2},{2,3},{3,0},{4,5},{5,6},{6,7},{7,4},{8,9},{9,10},{10,1... | collective-permute-start | bytes 2359304 | tf_op jit(solution)/shard_map/ppermute | solution.py:22
  3.0 2.1 collective-permute-start.1
  5.1 0.8 subtract_multiply_fusion.6
  5.9 0.8 subtract_multiply_fusion.7
  6.8 0.8 multiply_reduce_fusion.2
  7.6 0.8 fusion.48
  8.4 0.8 reduce-window.7
  9.2 0.7 bitcast_subtract_fusion.1
  9.9 0.1 convert_reduce_fusion
  10.0 0.1 select_reduce_fusion
  10.3 0.0 copy-done
  10.3 18.8 %gather_fusion.2 = bf16[5120,128]{1,0:T(8,128)(2,1)} fusion(bf16[3072,128]{1,0:T(8,128)(2,1)S(1)} %bitcast.124, s32[5120]{0:T(1024)S(1)} %broadcast_clamp_fusion.1), kind=kCustom, calls=%fused_computation.1.clone | custom fusion | bytes 2641920 | tf_op jit(solution)/shard_map/jit(_take)/gather | solution.py:43
  29.1 3.7 %broadcast_select_fusion.1 = bf16[5120,128]{1,0:T(8,128)(2,1)S(1)} fusion(bf16[5120,128]{1,0:T(8,128)(2,1)} %gather_fusion.2, pred[5120]{0:T(1024)(128)(4,1)S(1)} %compare_and_fusion.1), kind=kLoop, calls=%fused_computation.30 | loop fusion | flops 655360 | bytes 2626560 | tf_op jit(solution)/shard_map/jit(_take)/select_n | solution.py:43
  32.9 0.9 fusion.8
  33.9 0.0 collective-permute-done
  33.9 15.1 %gather_fusion.1 = bf16[5120,128]{1,0:T(8,128)(2,1)S(1)} fusion(bf16[3072,128]{1,0:T(8,128)(2,1)S(1)} %bitcast.126, s32[5120]{0:T(1024)S(1)} %broadcast_clamp_fusion.2), kind=kCustom, calls=%fused_computation.clone | custom fusion | bytes 2641920 | tf_op jit(solution)/shard_map/jit(_take)/gather | solution.py:43
  49.0 2.7 %broadcast_select_fusion.2 = bf16[5120,128]{1,0:T(8,128)(2,1)S(1)} fusion(bf16[5120,128]{1,0:T(8,128)(2,1)S(1)} %gather_fusion.1, pred[5120]{0:T(1024)(128)(4,1)S(1)} %compare_and_fusion.2), kind=kLoop, calls=%fused_computation.31 | loop fusion | flops 655360 | bytes 2626560 | tf_op jit(solution)/shard_map/jit(_take)/select_n | solution.py:43
  51.7 0.9 fusion.9
  52.6 0.0 collective-permute-done.1
  52.6 15.1 %gather_fusion.3 = bf16[5120,128]{1,0:T(8,128)(2,1)S(1)} fusion(bf16[3072,128]{1,0:T(8,128)(2,1)S(1)} %bitcast.125, s32[5120]{0:T(1024)S(1)} %broadcast_clamp_fusion), kind=kCustom, calls=%fused_computation.2.clone | custom fusion | bytes 2641920 | tf_op jit(solution)/shard_map/jit(_take)/gather | solution.py:43
  67.7 2.7 %broadcast_select_fusion = bf16[5120,128]{1,0:T(8,128)(2,1)S(1)} fusion(bf16[5120,128]{1,0:T(8,128)(2,1)S(1)} %gather_fusion.3, pred[5120]{0:T(1024)(128)(4,1)S(1)} %compare_and_fusion), kind=kLoop, calls=%fused_computation.29 | loop fusion | flops 655360 | bytes 2626560 | tf_op jit(solution)/shard_map/jit(_take)/select_n | solution.py:43
  70.4 0.9 fusion.7
  71.3 0.1 pad_maximum_fusion
  71.4 9.2 %gather_fusion = bf16[3072,128]{1,0:T(8,128)(2,1)S(1)} fusion(bf16[3840,128]{1,0:T(8,128)(2,1)S(1)} %bitcast.127, s32[3072]{0:T(1024)S(1)} %broadcast_clamp_fusion.3), kind=kCustom, calls=%fused_computation.3 | custom fusion | bytes 1585152 | tf_op jit(solution)/shard_map/jit(_take)/gather | solution.py:66
  80.6 0.6 broadcast_select_fusion.3
  81.2 22.6 %all_to_all.54 = bf16[24,128,128]{2,1,0:T(8,128)(2,1)S(1)} all-to-all(bf16[24,128,128]{2,1,0:T(8,128)(2,1)S(1)} %broadcast_select_fusion.3), channel_id=1, replica_groups=mesh['lat'=8,'lon'=4] {'lon'}, dimensions={0} | all-to-all | bytes 1572864 | tf_op jit(solution)/shard_map/all_to_all | solution.py:88
  103.8 0.6 copy.26
  104.4 0.3 all_to_all.42
  104.7 17.4 %fusion.6 = bf16[6,1536,128]{1,2,0:T(8,128)(2,1)} fusion(bf16[6,512,128]{1,2,0:T(8,128)(2,1)S(1)} %all_to_all.42), kind=kOutput, calls=%fused_computation.16 | convolution fusion | flops 1222508544 | bytes 3145728 | tf_op jit(solution)/shard_map/kx,yxc->ykc/dot_general | solution.py:85
  122.1 3.7 %copy.27 = bf16[6,1536,128]{2,0,1:T(8,128)(2,1)S(1)} copy(bf16[6,1536,128]{1,2,0:T(8,128)(2,1)} %fusion.6) | data formatting | bytes 4718592 | tf_op jit(solution)/shard_map/convert_element_type | solution.py:92
  125.8 69.9 %all_to_all.55 = bf16[6,1536,128]{2,0,1:T(8,128)(2,1)S(1)} all-to-all(bf16[6,1536,128]{2,0,1:T(8,128)(2,1)S(1)} %copy.27), channel_id=1, replica_groups=mesh['lat'=8,'lon'=4] {'lon'}, dimensions={1} | all-to-all | bytes 4718592 | tf_op jit(solution)/shard_map/all_to_all | solution.py:91
  195.7 0.5 copy.29
  196.2 2.9 %copy.30 = bf16[24,384,128]{2,0,1:T(8,128)(2,1)} copy(bf16[24,384,128]{2,1,0:T(8,128)(2,1)S(1)} %bitcast.131) | data formatting | bytes 4718592 | tf_op jit(solution)/shard_map/all_to_all | solution.py:91
  199.1 3.8 %all-to-all-start.2 = ((bf16[24,384,128]{2,0,1:T(8,128)(2,1)}), bf16[24,384,128]{2,0,1:T(8,128)(2,1)S(1)}, u32[]{:S(2)}, u32[]{:S(2)}) async-start(bf16[24,384,128]{2,0,1:T(8,128)(2,1)} %copy.30), calls=%async_computation.2 | async-start | bytes 4718592 | tf_op jit(solution)/shard_map/all_to_all | solution.py:94
  203.0 29.4 %all-to-all-done.2 = bf16[24,384,128]{2,0,1:T(8,128)(2,1)S(1)} async-done(((bf16[24,384,128]{2,0,1:T(8,128)(2,1)}), bf16[24,384,128]{2,0,1:T(8,128)(2,1)S(1)}, u32[]{:S(2)}, u32[]{:S(2)}) %all-to-all-start.2) | async-done | bytes 2359328 | tf_op jit(solution)/shard_map/all_to_all | solution.py:94
  232.3 0.7 copy.32
  233.0 14.2 %multiply_bitcast_fusion = f32[48,768,128]{1,2,0:T(8,128)} fusion(f32[768]{0:T(1024)S(1)} %fusion.39, bf16[192,48,128]{2,0,1:T(8,128)(2,1)S(1)} %bitcast.128, bf16[48,192,768]{2,1,0:T(8,128)(2,1)} %param.13), kind=kOutput, calls=%fused_computation.4 | convolution fusion | flops 1816657920 | bytes 35392512 | tf_op jit(solution)/shard_map/kyn,ykc->knc/dot_general | solution.py:95
  247.2 18.6 %copy.33 = f32[48,768,128]{2,1,0:T(8,128)} copy(f32[48,768,128]{1,2,0:T(8,128)} %multiply_bitcast_fusion) | data formatting | bytes 37748736 | tf_op jit(solution)/shard_map/mul | solution.py:98
  (22 shorter events, 0.3 us)
Async XLA Ops:
  0.0 10.3 %copy-start = (bf16[24,128,128]{2,1,0:T(8,128)(2,1)S(1)}, bf16[24,128,128]{2,1,0:T(8,128)(2,1)}, u32[]{:S(2)}) copy-start(bf16[24,128,128]{2,1,0:T(8,128)(2,1)} %param.8) | copy-start | bytes 2359300
  0.0 33.9 %collective-permute-start = (bf16[24,128,128]{2,1,0:T(8,128)(2,1)}, bf16[24,128,128]{2,1,0:T(8,128)(2,1)S(1)}, u32[]{:S(2)}, u32[]{:S(2)}) collective-permute-start(bf16[24,128,128]{2,1,0:T(8,128)(2,1)} %param.8), channel_id=1, source_target_pairs={{0,1},{1,2},{2,3},{3,0},{4,5},{5,6},{6,7},{7,4},{8,9},{9,10},{10,1... | collective-permute-start | bytes 2359304 | tf_op jit(solution)/shard_map/ppermute | solution.py:22
  3.0 49.6 %collective-permute-start.1 = (bf16[24,128,128]{2,1,0:T(8,128)(2,1)}, bf16[24,128,128]{2,1,0:T(8,128)(2,1)S(1)}, u32[]{:S(2)}, u32[]{:S(2)}) collective-permute-start(bf16[24,128,128]{2,1,0:T(8,128)(2,1)} %param.8), channel_id=1, source_target_pairs={{1,0},{2,1},{3,2},{0,3},{5,4},{6,5},{7,6},{4,7},{9,8},{10,9},{11,1... | collective-permute-start | bytes 2359304 | tf_op jit(solution)/shard_map/ppermute | solution.py:24
  199.1 33.2 %all-to-all-start.2 = ((bf16[24,384,128]{2,0,1:T(8,128)(2,1)}), bf16[24,384,128]{2,0,1:T(8,128)(2,1)S(1)}, u32[]{:S(2)}, u32[]{:S(2)}) async-start(bf16[24,384,128]{2,0,1:T(8,128)(2,1)} %copy.30), calls=%async_computation.2 | async-start | bytes 4718592 | tf_op jit(solution)/shard_map/all_to_all | solution.py:94
where the time goes:
time: 267 us; the launch traced here: 266 us
  blocking collectives  92.5 us (35%)
  local copies, waits for them, and re-layouts  86.3 us (32%)
  matrix products  31.6 us (12%)
  waiting for transfers between devices  29.4 us (11%)
  other arithmetic  16.8 us (6%)
  starting transfers between devices  8.9 us (3%)
    all_to_all x1, blocking collectives, local(): lax.all_to_all(spectra.astype(jnp.bfloat16), 'lon', split_axis=1, concat_...  69.9 us
    gather x3, local copies, waits for them, and re-layouts, interpolate(): jnp.take(own_tile, cell_rows.reshape(-1), axis=0).astype(jnp.float32)  49 us
    all_to_all x1, waiting for transfers between devices, local(): lax.all_to_all(fourier, 'lat', split_axis=1, concat_axis=0, tiled=True)  29.4 us
    all_to_all x1, blocking collectives, local(): lax.all_to_all(departed, 'lon', split_axis=0, concat_axis=1, tiled=True)  22.6 us
    mul x1, local copies, waits for them, and re-layouts, local(): return projected * factor[None, :, None]  18.6 us
    dot_general x1, matrix products, local(): jnp.einsum('kx,yxc->ykc', hartley, lax.all_to_all(departed, 'lon', split_...  17.4 us
    dot_general x1, matrix products, local(): jnp.einsum('kyn,ykc->knc', legendre, gathered, preferred_element_type=jnp...  14.2 us
    gather x1, local copies, waits for them, and re-layouts, place_columns(): return jnp.take(values.reshape(-1, values.shape[-1]), flat_index, axis=0)  9.16 us
  transfers between devices with their start and end apart: 3, of which 1 were waited for; matrix products, arithmetic and copies ran while one was open for 18% of the time, Pallas kernels for 0%

commit v1 on v0

v1 whole, which is shorter than its diff:
```python
import functools
import math

import jax
import jax.numpy as jnp
from jax import lax
from jax.experimental import pallas as pl
from jax.experimental.pallas import tpu as pltpu
from jax.sharding import PartitionSpec as P

BLK = 16
FRAC = 16
SLOTS = 3
LANES = 128
SPAN = 2 * LANES
F32 = jnp.float32
BF16 = jnp.bfloat16


def hartley_table(waves, lon_total):
    wave_index = jnp.arange(waves, dtype=jnp.int32)
    lon_index = jnp.arange(lon_total, dtype=jnp.int32)
    phase_index = wave_index[:, None] * lon_index[None, :] % lon_total
    phase_angle = 2.0 * math.pi / lon_total * phase_index.astype(F32)
    return ((jnp.cos(phase_angle) + jnp.sin(phase_angle)) / math.sqrt(lon_total)).astype(BF16)


def chunk_list(channels):
    half = channels // 2
    return ((0, half), (half, half // 2), (half + half // 2, half // 2))


def pack_body(chunks, blocks, counts, fields, block, stencil, frac, *rest):
    outs, wide = rest[:-1], rest[-1]
    cells = blocks * BLK
    cap = block.shape[1]
    wide[...] = fields[...].astype(F32)
    lane = lax.broadcasted_iota(jnp.int32, (blocks, LANES), 1)
    for out, (first, width) in zip(outs, chunks, strict=True):
        groups = LANES // width
        planes = BLK // groups
        for plane in range(planes):
            total = None
            for group in range(groups):
                rows = wide[pl.ds(group * planes + plane, blocks, stride=BLK), :]
                shift = (group * width - first) % LANES
                if shift:
                    rows = pltpu.roll(rows, shift, 1)
                total = rows if total is None else jnp.where(lane >= group * width, rows, total)
            out[plane * blocks : (plane + 1) * blocks, :] = total.astype(BF16)
    starts = (0, counts[0], counts[0] + counts[1])
    column = lax.broadcasted_iota(jnp.int32, (8, cells), 1)
    row = lax.broadcasted_iota(jnp.int32, (8, cells), 0)
    slot = (column >= starts[1]).astype(jnp.int32) + (column >= starts[2]).astype(jnp.int32)
    placed = slot.astype(F32)
    for index in range(SLOTS):
        listed = jnp.concatenate(
            [
                block[index : index + 1, :].astype(F32),
                stencil[index].astype(F32),
                frac[index].astype(F32),
                jnp.zeros((1, cap), F32),
            ],
            axis=0,
        )
        listed = jnp.concatenate([listed, jnp.zeros((8, cells - cap), F32)], axis=1)
        if index:
            listed = pltpu.roll(listed, starts[index], 1)
        placed = jnp.where((slot == index) & (row < 7), listed, placed)
    base = outs[0].shape[0] - cells // LANES * 8
    for span in range(cells // SPAN):
        pair = jnp.concatenate(
            [
                placed[:, span * SPAN : span * SPAN + LANES],
                placed[:, span * SPAN + LANES : (span + 1) * SPAN],
            ],
            axis=0,
        )
        outs[0][base + span * 16 : base + (span + 1) * 16, :] = pair.astype(BF16)


def interp_body(count, width, blocks, lead, here, *rest):
    if lead:
        tiles, (table, out, params, ends, flipped, grid) = rest[: 2 * count - 1], rest[2 * count - 1 :]
    else:
        ends, params, *rest = rest
        tiles, (table, out, flipped, grid) = rest[: 2 * count - 1], rest[2 * count - 1 :]
    me = here[0]
    groups = LANES // width
    planes = BLK // groups
    spans = blocks * BLK // SPAN

    def take(tile, owner):
        for plane in range(planes):
            rows = tile[plane * blocks : (plane + 1) * blocks, :]
            flipped[owner, plane * LANES : (plane + 1) * LANES, :] = rows.T
        if lead:
            params[owner] = tile[planes * blocks :, :]

    take(tiles[0], me)
    for away in range(1, count):

        @pl.when(me >= away)
        def _(away=away):
            take(tiles[away], me - away)

        @pl.when(me + away < count)
        def _(away=away):
            take(tiles[count - 1 + away], me + away)

    if lead:
        for tile in range(count):
            rows = params[tile].astype(F32)
            which = lax.broadcasted_iota(jnp.int32, rows.shape, 0) % 8 == 7
            ends[tile, 0] = 0
            for index in range(SLOTS):
                listed = jnp.where(which & (rows <= index), 1.0, 0.0)
                ends[tile, index + 1] = jnp.sum(listed).astype(jnp.int32)

    grid[...] = jnp.zeros_like(grid)
    block_row = lax.broadcasted_iota(jnp.int32, (blocks, SPAN), 0).astype(F32)
    cell_row = lax.broadcasted_iota(jnp.int32, (BLK, SPAN), 0).astype(F32)

    def job(number, _):
        owner = number // SLOTS
        index = number % SLOTS
        target = lax.rem(owner - index + 1 + count, count)
        low = ends[target, index]
        high = ends[target, index + 1]
        place = pl.multiple_of(target * LANES, LANES)

        def span_step(span, _):
            both = params[target, pl.ds(pl.multiple_of(span * 16, 16), 16), :].astype(F32)

            def line(i):
                return jnp.concatenate([both[i : i + 1, :], both[8 + i : 9 + i, :]], axis=1)

            key = jnp.where(line(7) == index.astype(F32), line(0), -1.0)
            onehot = jnp.where(block_row == key, 1.0, 0.0).astype(BF16)
            f_lat = (line(5) + 0.5) / FRAC
            f_lon = (line(6) + 0.5) / FRAC
            corners = (
                (1.0 - f_lat) * (1.0 - f_lon),
                f_lat * (1.0 - f_lon),
                (1.0 - f_lat) * f_lon,
                f_lat * f_lon,
            )
            weight = jnp.zeros((BLK, SPAN), F32)
            for corner in range(4):
                weight += jnp.where(cell_row == line(1 + corner), corners[corner], 0.0)
            total = jnp.zeros((width, SPAN), F32)
            for plane in range(planes):
                picked = jnp.dot(
                    flipped[owner, plane * LANES : (plane + 1) * LANES, :],
                    onehot,
                    preferred_element_type=F32,
                )
                for group in range(groups):
                    cell = group * planes + plane
                    total += (
                        weight[cell : cell + 1, :] * picked[group * width : (group + 1) * width, :]
                    )
            total = total.astype(BF16)
            for half in range(2):
                rows = pl.ds(pl.multiple_of((2 * span + half) * width, width), width)
                grid[rows, pl.ds(place, LANES)] += total[:, half * LANES : (half + 1) * LANES]
            return 0

        first = low // SPAN
        last = jnp.where(high > low, (high + SPAN - 1) // SPAN, first)
        lax.fori_loop(first, last, span_step, 0)
        return 0

    lax.fori_loop(0, count * SLOTS, job, 0)
    spectra = lax.dot_general(
        table[...], grid[...], (((1,), (1,)), ((), ())), preferred_element_type=F32
    )
    out[...] = spectra.astype(BF16)


def final_body(chunks, lat_rows, per_step, legendre, *rest):
    parts, (out, gathered, factor) = rest[: len(chunks)], rest[len(chunks) :]
    sources, waves, _ = parts[0].shape
    degrees = legendre.shape[2]

    @pl.when(pl.program_id(0) == 0)
    def _():
        degree = lax.broadcasted_iota(jnp.int32, factor.shape, 0).astype(F32)
        factor[...] = 1.0 / (1.0 + 4.0 * degree * (degree + 1.0) / (degrees * (degrees + 1)))
        lane = lax.broadcasted_iota(jnp.int32, (waves, LANES), 1)

        def gather(source, _):
            for row in range(lat_rows):
                total = None
                for part, (first, width) in zip(parts, chunks, strict=True):
                    groups = LANES // width
                    tile, group = row // groups, row % groups
                    values = part[source, :, tile * LANES : (tile + 1) * LANES].astype(F32)
                    shift = (first - group * width) % LANES
                    if shift:
                        values = pltpu.roll(values, shift, 1)
                    total = values if total is None else jnp.where(lane >= first, values, total)
                start = pl.multiple_of((source * lat_rows + row) * waves, 8)
                gathered[pl.ds(start, waves), :] = total
            return 0

        lax.fori_loop(0, sources, gather, 0)

    for step in range(per_step):
        wave = pl.program_id(0) * per_step + step
        column = gathered[pl.ds(wave, sources * lat_rows, stride=waves), :].astype(BF16)
        projected = lax.dot_general(
            legendre[step], column, (((0,), (0,)), ((), ())), preferred_element_type=F32
        )
        out[step] = projected * factor[...]


def whole(shape):
    return pl.BlockSpec(shape, lambda *_: (0,) * len(shape))


VMEM = pl.BlockSpec(memory_space=pltpu.VMEM)
SMEM = pl.BlockSpec(memory_space=pltpu.SMEM)
LIMIT = pltpu.CompilerParams(vmem_limit_bytes=56 * 2**20)


def gathering(fields, req_block, req_stencil, req_frac, req_count, legendre):
    lat_rows, lon_cols, channels = fields.shape
    waves, lat_total, degrees = legendre.shape
    count, bands = lax.axis_size("lon"), lax.axis_size("lat")
    cells = lat_rows * lon_cols
    blocks = cells // BLK
    lon_total = lon_cols * count
    sector_waves = waves * bands
    chunks = chunk_list(channels)
    me = lax.axis_index("lon")
    here = jnp.full((1,), me, jnp.int32)

    table = hartley_table(sector_waves * count, lon_total)
    table = lax.dynamic_slice_in_dim(table, me * sector_waves, sector_waves, axis=0)

    tile_rows = [blocks * BLK * width // LANES for _, width in chunks]
    tile_rows[0] += cells // LANES * 8
    packed = pl.pallas_call(
        functools.partial(pack_body, chunks, blocks),
        out_shape=[jax.ShapeDtypeStruct((rows, LANES), BF16) for rows in tile_rows],
        in_specs=[SMEM, VMEM, VMEM, VMEM, VMEM],
        out_specs=[VMEM] * len(chunks),
        scratch_shapes=[pltpu.VMEM((cells, channels), F32)],
        compiler_params=LIMIT,
    )(req_count[0, 0], fields.reshape(cells, channels), req_block[0, 0], req_stencil[0, 0], req_frac[0, 0])

    parts = []
    ends = params = None
    for number, (first, width) in enumerate(chunks):
        below, above = [packed[number]], [packed[number]]
        for away in range(1, count):
            below.append(lax.ppermute(below[-1], "lon", [(i, i + 1) for i in range(away - 1, count - 1)]))
            above.append(lax.ppermute(above[-1], "lon", [(i + 1, i) for i in range(count - away)]))
        tiles = below + above[1:]
        lead = number == 0
        out_shape = [jax.ShapeDtypeStruct((sector_waves, lat_rows * width), BF16)]
        out_specs = [VMEM]
        given = [here]
        if lead:
            out_shape += [
                jax.ShapeDtypeStruct((count, cells // LANES * 8, LANES), BF16),
                jax.ShapeDtypeStruct((count, SLOTS + 1), jnp.int32),
            ]
            out_specs += [VMEM, SMEM]
        else:
            given += [ends, params]
        results = pl.pallas_call(
            functools.partial(interp_body, count, width, blocks, lead),
            out_shape=out_shape,
            in_specs=[SMEM] + ([] if lead else [SMEM, VMEM]) + [VMEM] * (len(tiles) + 1),
            out_specs=out_specs,
            scratch_shapes=[
                pltpu.VMEM((count, BLK * width, blocks), BF16),
                pltpu.VMEM((lat_rows * width, lon_total), BF16),
            ],
            compiler_params=LIMIT,
            cost_estimate=pl.CostEstimate(flops=width * 10**7, bytes_accessed=10**6, transcendentals=0),
        )(*given, *tiles, table)
        if lead:
            fourier, params, ends = results
        else:
            (fourier,) = results
        fourier = fourier.reshape(bands, waves, lat_rows * width)
        parts.append(lax.all_to_all(fourier, "lat", split_axis=0, concat_axis=0, tiled=True))

    per_step = math.gcd(waves, 4)
    return pl.pallas_call(
        functools.partial(final_body, chunks, lat_rows, per_step),
        grid=(waves // per_step,),
        out_shape=jax.ShapeDtypeStruct((waves, degrees, channels), F32),
        in_specs=[pl.BlockSpec((per_step, lat_total, degrees), lambda i: (i, 0, 0))]
        + [whole(part.shape) for part in parts],
        out_specs=pl.BlockSpec((per_step, degrees, channels), lambda i: (i, 0, 0)),
        scratch_shapes=[
            pltpu.VMEM((lat_total * waves, channels), F32),
            pltpu.VMEM((degrees, channels), F32),
        ],
        compiler_params=LIMIT,
    )(legendre, *parts)


def padded(cells, sides, width):
    for axis, dim in sides:
        count = lax.axis_size(axis)
        head = lax.slice_in_dim(cells, 0, width, axis=dim)
        tail = lax.slice_in_dim(cells, cells.shape[dim] - width, cells.shape[dim], axis=dim)
        cells = jnp.concatenate(
            [
                lax.ppermute(tail, axis, [(i, (i + 1) % count) for i in range(count)]),
                cells,
                lax.ppermute(head, axis, [((i + 1) % count, i) for i in range(count)]),
            ],
            axis=dim,
        )
    return cells


def interpolate(own_tile, packed):
    cell_rows = packed[0][None, :] * BLK + packed[1:5]
    picked = jnp.take(own_tile, cell_rows.reshape(-1), axis=0).astype(F32)
    picked = picked.reshape(4, cell_rows.shape[1], own_tile.shape[1])
    frac_lat = (packed[5].astype(F32) + 0.5) / FRAC
    frac_lon = (packed[6].astype(F32) + 0.5) / FRAC
    weights = jnp.stack(
        [
            (1.0 - frac_lat) * (1.0 - frac_lon),
            frac_lat * (1.0 - frac_lon),
            (1.0 - frac_lat) * frac_lon,
            frac_lat * frac_lon,
        ]
    )
    return jnp.sum(weights[:, :, None] * picked, axis=0).astype(BF16)


def place_columns(values, counts, columns):
    slot_ends = jnp.cumsum(counts)
    starts = slot_ends - counts
    column = jnp.arange(columns, dtype=jnp.int32)
    slot_index = jnp.sum((slot_ends[None, :] <= column[:, None]).astype(jnp.int32), axis=1)
    onehot = slot_index[:, None] == jnp.arange(SLOTS, dtype=jnp.int32)[None, :]
    offset = column - jnp.sum(jnp.where(onehot, starts[None, :], 0), axis=1)
    flat_index = slot_index * values.shape[1] + offset
    return jnp.take(values.reshape(-1, values.shape[-1]), flat_index, axis=0)


def exchanging(fields, req_block, req_stencil, req_frac, req_count, legendre):
    lat_rows, lon_cols, channels = fields.shape
    count = lax.axis_size("lon")
    waves_total = legendre.shape[0] * count * lax.axis_size("lat")
    packed = jnp.concatenate(
        [req_block[0, 0][:, None, :], req_stencil[0, 0], req_frac[0, 0]], axis=1
    )
    counts = req_count[0, 0]
    widened = padded(fields, (("lon", 1),), lon_cols)
    slot_values = []
    for slot_index in range(SLOTS):
        owner_tile = widened[:, slot_index * lon_cols : (slot_index + 1) * lon_cols, :].reshape(
            -1, channels
        )
        slot_values.append(interpolate(owner_tile, packed[slot_index]))
    departed = place_columns(jnp.stack(slot_values), counts, lat_rows * lon_cols)
    departed = departed.reshape(lat_rows, lon_cols, channels)
    lon_total = lon_cols * count
    spectra = jnp.einsum(
        "kx,yxc->ykc",
        hartley_table(waves_total, lon_total),
        lax.all_to_all(departed, "lon", split_axis=0, concat_axis=1, tiled=True),
        preferred_element_type=F32,
    )
    fourier = lax.all_to_all(spectra.astype(BF16), "lon", split_axis=1, concat_axis=0, tiled=True)
    gathered = lax.all_to_all(fourier, "lat", split_axis=1, concat_axis=0, tiled=True)
    projected = jnp.einsum("kyn,ykc->knc", legendre, gathered, preferred_element_type=F32)
    degrees = legendre.shape[2]
    degree = jnp.arange(degrees, dtype=F32)
    factor = 1.0 / (1.0 + 4.0 * degree * (degree + 1.0) / (degrees * (degrees + 1)))
    return projected * factor[None, :, None]


def local(fields, req_block, req_stencil, req_frac, req_count, legendre):
    count = lax.axis_size("lon")
    lon_cols = fields.shape[1]
    sector_waves = legendre.shape[0] * lax.axis_size("lat")
    plan = gathering if count * lon_cols <= lon_cols + sector_waves else exchanging
    return plan(fields, req_block, req_stencil, req_frac, req_count, legendre)


def solution(mesh):
    return jax.shard_map(
        local,
        mesh=mesh,
        in_specs=(
            P("lat", "lon", None),
            P("lat", "lon", None, None),
            P("lat", "lon", None, None, None),
            P("lat", "lon", None, None, None),
            P("lat", "lon", None),
            P(("lon", "lat"), None, None),
        ),
        out_specs=P(("lon", "lat"), None, None),
        check_vma=False,
    )
```

time: 267 us -> 199 us (0.75)
  local copies, waits for them, and re-layouts: 86.3 us -> 2.68 us
  Pallas kernels: 0 us -> 78.9 us
  blocking collectives: 92.5 us -> 34.5 us
  matrix products: 31.6 us -> 0 us
  starting transfers between devices: 8.9 us -> 39.1 us
  other arithmetic: 16.8 us -> 4.84 us
  waiting for transfers between devices: 29.4 us -> 37.2 us
    pallas_call x0 -> x5, Pallas kernels: none -> 78.9 us  [the longest x3 54.9 us: gathering(): pl.pallas_call(functools.partial(interp_body, count, width, blocks, lead)...]
    gather x4 -> x0, local copies, waits for them, and re-layouts: 58.1 us -> none  [the longest x3 49 us: interpolate(): jnp.take(own_tile, cell_rows.reshape(-1), axis=0).astype(jnp.float32)]
    all_to_all x2, blocking collectives: 92.5 us -> 34.5 us  [gathering(): lax.all_to_all(fourier, 'lat', split_axis=0, concat_axis=0, tiled=True)]
    ppermute x2 -> x18, waiting for transfers between devices: 0.01 us -> 37.2 us  [the longest x9 37.1 us: gathering(): lax.ppermute(above[-1], 'lon', [(i + 1, i) for i in range(count - away)])]
    dot_general x2 -> x0, matrix products: 31.6 us -> none  [the longest x1 17.4 us: local(): jnp.einsum('kx,yxc->ykc', hartley, lax.all_to_all(departed, 'lon', split_...]
    ppermute x2 -> x18, starting transfers between devices: 5.1 us -> 35.2 us  [the longest x9 23.6 us: gathering(): lax.ppermute(below[-1], 'lon', [(i, i + 1) for i in range(away - 1, count...]
    all_to_all x1, waiting for transfers between devices: 29.4 us -> 0.01 us  [gathering(): lax.all_to_all(fourier, 'lat', split_axis=0, concat_axis=0, tiled=True)]
    mul x1 -> x0, local copies, waits for them, and re-layouts: 18.6 us -> none  [local(): return projected * factor[None, :, None]]
  transfers between devices with their start and end apart: 3 -> 19, of which waited for: 1 -> 6; matrix products, arithmetic and copies ran while one was open for 18% -> 2% of each run, Pallas kernels for 0% -> 28%
where the time goes in v1:
time: 199 us; the launch traced here: 197 us
  Pallas kernels  78.9 us (40%)
  starting transfers between devices  39.1 us (20%)
  waiting for transfers between devices  37.2 us (19%)
  blocking collectives  34.5 us (17%)
  other arithmetic  4.84 us (2%)
  local copies, waits for them, and re-layouts  2.68 us (1%)
    pallas_call x3, Pallas kernels, gathering(): pl.pallas_call(functools.partial(interp_body, count, width, blocks, lead)...  54.9 us
    ppermute x9, waiting for transfers between devices, gathering(): lax.ppermute(above[-1], 'lon', [(i + 1, i) for i in range(count - away)])  37.1 us
    all_to_all x2, blocking collectives, gathering(): lax.all_to_all(fourier, 'lat', split_axis=0, concat_axis=0, tiled=True)  34.5 us
    ppermute x9, starting transfers between devices, gathering(): lax.ppermute(below[-1], 'lon', [(i, i + 1) for i in range(away - 1, count...  23.6 us
    pallas_call x1, Pallas kernels, gathering(): pl.pallas_call(functools.partial(final_body, chunks, lat_rows, per_step),...  20.3 us
    ppermute x9, starting transfers between devices, gathering(): lax.ppermute(above[-1], 'lon', [(i + 1, i) for i in range(count - away)])  11.7 us
  transfers between devices with their start and end apart: 19, of which 6 were waited for; matrix products, arithmetic and copies ran while one was open for 2% of the time, Pallas kernels for 28%

profile of v1, /device:TPU:0, one launch (start us, length us, event | category | flops | bytes accessed | tf_op | source)
XLA Modules:
  0.0 197.5 jit_solution(621108298132223153)
XLA Ops:
  0.0 1.3 copy.9
  1.3 3.7 %shard_map.64 = (bf16[1728,128]{1,0:T(8,128)(2,1)}, bf16[768,128]{1,0:T(8,128)(2,1)}, bf16[768,128]{1,0:T(8,128)(2,1)}) custom-call(s32[3]{0:T(128)} %bitcast.18, bf16[3072,128]{1,0:T(8,128)(2,1)} %bitcast.14, s32[3,1280]{1,0:T(4,128)} %bitcast.15, s32[3,4,1280]{2,1,0:T(4,128)} %bitcast.16, s32[3,2,1280]{2,1,0:T(2,128)} %bitcast.17), custom_call_target="tpu_custom_call" | custom-call | tf_op jit(solution)/shard_map/pallas_call | solution.py:244
  5.0 1.4 collective-permute-start.3
  6.4 5.6 %collective-permute-start = (bf16[1728,128]{1,0:T(8,128)(2,1)}, bf16[1728,128]{1,0:T(8,128)(2,1)S(1)}, u32[]{:S(2)}, u32[]{:S(2)}) collective-permute-start(bf16[1728,128]{1,0:T(8,128)(2,1)} %get-tuple-element.11.rest_0_), channel_id=1, source_target_pairs={{0,1},{1,2},{2,3},{4,5},{5,6},{6,7},{8,9},{9,10},{10,11},{12,13},{... | collective-permute-start | bytes 1327112 | tf_op jit(solution)/shard_map/ppermute | solution.py:258
  12.0 8.4 %collective-permute-done.3.rest_4_ = bf16[1728,128]{1,0:T(8,128)(2,1)S(1)} collective-permute-done((bf16[1728,128]{1,0:T(8,128)(2,1)}, bf16[1728,128]{1,0:T(8,128)(2,1)S(1)}, u32[]{:S(2)}, u32[]{:S(2)}) %collective-permute-start.3) | collective-permute-done | bytes 442400 | tf_op jit(solution)/shard_map/ppermute | solution.py:259
  20.4 1.3 collective-permute-start.4
  21.7 0.0 collective-permute-done.rest_1_
  21.8 1.5 collective-permute-start.1
  23.2 1.3 collective-permute-start.15
  24.5 8.9 %collective-permute-start.12 = (bf16[768,128]{1,0:T(8,128)(2,1)}, bf16[768,128]{1,0:T(8,128)(2,1)S(1)}, u32[]{:S(2)}, u32[]{:S(2)}) collective-permute-start(bf16[768,128]{1,0:T(8,128)(2,1)} %get-tuple-element.16.rest_2_), channel_id=1, source_target_pairs={{0,1},{1,2},{2,3},{4,5},{5,6},{6,7},{8,9},{9,10},{10,11},{12,13},{... | collective-permute-start | bytes 589832 | tf_op jit(solution)/shard_map/ppermute | solution.py:258
  33.4 4.5 %collective-permute-done.15.rest_6_ = bf16[768,128]{1,0:T(8,128)(2,1)S(1)} collective-permute-done((bf16[768,128]{1,0:T(8,128)(2,1)}, bf16[768,128]{1,0:T(8,128)(2,1)S(1)}, u32[]{:S(2)}, u32[]{:S(2)}) %collective-permute-start.15) | collective-permute-done | bytes 196640 | tf_op jit(solution)/shard_map/ppermute | solution.py:259
  37.9 1.3 collective-permute-start.16
  39.2 0.0 collective-permute-done.12.rest_3_
  39.2 1.4 collective-permute-start.13
  40.6 0.0 collective-permute-done.4.rest_5_
  40.6 1.3 collective-permute-start.5
  41.9 1.3 collective-permute-start.9
  43.2 2.4 %collective-permute-done.16.rest_7_ = bf16[768,128]{1,0:T(8,128)(2,1)} collective-permute-done((bf16[768,128]{1,0:T(8,128)(2,1)S(1)}, bf16[768,128]{1,0:T(8,128)(2,1)}, u32[]{:S(2)}, u32[]{:S(2)}) %collective-permute-start.16) | collective-permute-done | bytes 196640 | tf_op jit(solution)/shard_map/ppermute | solution.py:259
  45.6 1.3 collective-permute-start.17
  46.9 0.0 collective-permute-done.13.rest_4_
  46.9 1.4 collective-permute-start.14
  48.2 1.4 collective-permute-start.2
  49.7 1.3 add_select_fusion
  51.0 8.2 %collective-permute-done.5.rest_6_ = bf16[1728,128]{1,0:T(8,128)(2,1)} collective-permute-done((bf16[1728,128]{1,0:T(8,128)(2,1)}, bf16[1728,128]{1,0:T(8,128)(2,1)}, u32[]{:S(2)}, u32[]{:S(2)}) %collective-permute-start.5) | collective-permute-done | bytes 442400 | tf_op jit(solution)/shard_map/ppermute | solution.py:259
  59.2 2.1 %collective-permute-start.6 = (bf16[768,128]{1,0:T(8,128)(2,1)S(1)}, bf16[768,128]{1,0:T(8,128)(2,1)}, u32[]{:S(2)}, u32[]{:S(2)}) collective-permute-start(bf16[768,128]{1,0:T(8,128)(2,1)S(1)} %copy-done.4), channel_id=1, source_target_pairs={{0,1},{1,2},{2,3},{4,5},{5,6},{6,7},{8,9},{9,10},{10,11},{12,13},{... | collective-permute-start | bytes 589832 | tf_op jit(solution)/shard_map/ppermute | solution.py:258
  61.3 3.5 %multiply_convert_fusion.rest_7_.rest_9_ = bf16[384,512]{1,0:T(8,128)(2,1)} fusion(s32[1536,512]{1,0:T(8,128)S(1)} %add_select_fusion, s32[]{:T(128)S(6)} %select_n.11), kind=kLoop, calls=%fused_computation.9 | loop fusion | flops 983040 | bytes 1179652 | tf_op jit(solution)/shard_map/convert_element_type | solution.py:25
  64.9 0.0 collective-permute-done.2.rest_3_
  64.9 21.6 %shard_map.65 = (bf16[384,1536]{1,0:T(8,128)(2,1)}, bf16[4,192,128]{2,1,0:T(8,128)(2,1)}, s32[4,4]{1,0:T(4,128)}) custom-call(s32[1]{0:T(128)} %bitcast.here, bf16[1728,128]{1,0:T(8,128)(2,1)} %get-tuple-element.11.rest_0_, bf16[1728,128]{1,0:T(8,128)(2,1)} %copy-done.3, bf16[1728,128]{1,0:T(8,128)(2,1)} %collective-permute-done.1.rest_2_, ...), custom_call_target="tpu_custom_call" | custom-call | flops 640000000 | bytes 1000000 | tf_op jit(solution)/shard_map/pallas_call | solution.py:273
  86.5 0.0 collective-permute-done.17.rest_8_
  86.5 0.0 collective-permute-done.14.rest_5_
  86.5 0.0 copy-start.1
  86.5 16.7 %shard_map.67 = bf16[384,768]{1,0:T(8,128)(2,1)} custom-call(s32[1]{0:T(128)} %bitcast.here, s32[4,4]{1,0:T(4,128)} %get-tuple-element.13.rest_0_, bf16[4,192,128]{2,1,0:T(8,128)(2,1)} %get-tuple-element.14.rest_1_, bf16[768,128]{1,0:T(8,128)(2,1)} %get-tuple-element.16.rest_2_, bf16[768,128]{1,0:T(8,128)(2,1)} %copy-done.7, ...), custom_call_target="tpu_custom_call" | custom-call | flops 320000000 | bytes 1000000 | tf_op jit(solution)/shard_map/pallas_call | solution.py:273
  103.2 3.9 %all-to-all-start.2 = ((bf16[8,48,768]{2,1,0:T(8,128)(2,1)}), bf16[8,48,768]{2,1,0:T(8,128)(2,1)S(1)}, u32[]{:S(2)}, u32[]{:S(2)}) async-start(bf16[8,48,768]{2,1,0:T(8,128)(2,1)} %bitcast.11), calls=%async_computation.2 | async-start | bytes 1179648 | tf_op jit(solution)/shard_map/all_to_all | solution.py:290
  107.1 0.0 collective-permute-done.9.rest_6_
  107.1 1.3 collective-permute-start.10
  108.4 0.7 collective-permute-start.7
  109.1 7.2 %collective-permute-done.10.rest_7_ = bf16[768,128]{1,0:T(8,128)(2,1)S(1)} collective-permute-done((bf16[768,128]{1,0:T(8,128)(2,1)S(1)}, bf16[768,128]{1,0:T(8,128)(2,1)S(1)}, u32[]{:S(2)}, u32[]{:S(2)}) %collective-permute-start.10) | collective-permute-done | bytes 196640 | tf_op jit(solution)/shard_map/ppermute | solution.py:259
  116.3 1.3 collective-permute-start.11
  117.6 0.0 collective-permute-done.7.rest_4_
  117.6 0.7 collective-permute-start.8
  118.3 6.4 %collective-permute-done.11.rest_8_ = bf16[768,128]{1,0:T(8,128)(2,1)S(1)} collective-permute-done((bf16[768,128]{1,0:T(8,128)(2,1)S(1)}, bf16[768,128]{1,0:T(8,128)(2,1)S(1)}, u32[]{:S(2)}, u32[]{:S(2)}) %collective-permute-start.11) | collective-permute-done | bytes 196640 | tf_op jit(solution)/shard_map/ppermute | solution.py:259
  124.7 0.6 copy-done.10
  125.4 0.7 copy-done.11
  126.0 16.6 %shard_map.66 = bf16[384,768]{1,0:T(8,128)(2,1)} custom-call(s32[1]{0:T(128)} %bitcast.here, s32[4,4]{1,0:T(4,128)} %get-tuple-element.13.rest_0_, bf16[4,192,128]{2,1,0:T(8,128)(2,1)} %get-tuple-element.14.rest_1_, bf16[768,128]{1,0:T(8,128)(2,1)} %get-tuple-element.15.rest_2_, bf16[768,128]{1,0:T(8,128)(2,1)} %collective-permute-done.6.rest_3_, ...), custom_call_target="tpu_custom_call" | custom-call | flops 320000000 | bytes 1000000 | tf_op jit(solution)/shard_map/pallas_call | solution.py:273
  142.6 0.0 all-to-all-done.2.rest_2_
  142.6 14.6 %all_to_all.15.rest_1_ = bf16[8,48,768]{2,1,0:T(8,128)(2,1)} all-to-all(bf16[8,48,768]{2,1,0:T(8,128)(2,1)} %bitcast.12), channel_id=1, replica_groups=mesh['lat'=8,'lon'=4] {'lat'}, dimensions={0} | all-to-all | bytes 1179648 | tf_op jit(solution)/shard_map/all_to_all | solution.py:290
  157.3 19.9 %all_to_all.16.rest_0_ = bf16[8,48,1536]{2,1,0:T(8,128)(2,1)} all-to-all(bf16[8,48,1536]{2,1,0:T(8,128)(2,1)S(1)} %bitcast.13), channel_id=1, replica_groups=mesh['lat'=8,'lon'=4] {'lat'}, dimensions={0} | all-to-all | bytes 2359296 | tf_op jit(solution)/shard_map/all_to_all | solution.py:290
  177.1 20.3 %shard_map.68 = f32[48,768,128]{2,1,0:T(8,128)} custom-call(bf16[48,192,768]{2,1,0:T(8,128)(2,1)} %legendre.1, bf16[8,48,1536]{2,1,0:T(8,128)(2,1)} %all_to_all.16.rest_0_, bf16[8,48,768]{2,1,0:T(8,128)(2,1)} %all_to_all.15.rest_1_, bf16[8,48,768]{2,1,0:T(8,128)(2,1)} %copy-done), custom_call_target="tpu_custom_call" | custom-call | tf_op jit(solution)/shard_map/pallas_call | solution.py:293
  (24 shorter events, 0.0 us)
Async XLA Ops:
  5.0 54.2 %copy-start.4 = (bf16[768,128]{1,0:T(8,128)(2,1)S(1)}, bf16[768,128]{1,0:T(8,128)(2,1)}, u32[]{:S(2)}) copy-start(bf16[768,128]{1,0:T(8,128)(2,1)} %get-tuple-element.15.rest_2_) | copy-start | bytes 589828
  5.0 15.4 %collective-permute-start.3 = (bf16[1728,128]{1,0:T(8,128)(2,1)}, bf16[1728,128]{1,0:T(8,128)(2,1)S(1)}, u32[]{:S(2)}, u32[]{:S(2)}) collective-permute-start(bf16[1728,128]{1,0:T(8,128)(2,1)} %get-tuple-element.11.rest_0_), channel_id=1, source_target_pairs={{1,0},{2,1},{3,2},{5,4},{6,5},{7,6},{9,8},{10,9},{11,10},{13,12},{... | collective-permute-start | bytes 1327112 | tf_op jit(solution)/shard_map/ppermute | solution.py:259
  6.4 15.3 %collective-permute-start = (bf16[1728,128]{1,0:T(8,128)(2,1)}, bf16[1728,128]{1,0:T(8,128)(2,1)S(1)}, u32[]{:S(2)}, u32[]{:S(2)}) collective-permute-start(bf16[1728,128]{1,0:T(8,128)(2,1)} %get-tuple-element.11.rest_0_), channel_id=1, source_target_pairs={{0,1},{1,2},{2,3},{4,5},{5,6},{6,7},{8,9},{9,10},{10,11},{12,13},{... | collective-permute-start | bytes 1327112 | tf_op jit(solution)/shard_map/ppermute | solution.py:258
  20.4 27.8 %copy-start.2 = (bf16[1728,128]{1,0:T(8,128)(2,1)}, bf16[1728,128]{1,0:T(8,128)(2,1)S(1)}, u32[]{:S(2)}) copy-start(bf16[1728,128]{1,0:T(8,128)(2,1)S(1)} %collective-permute-done.3.rest_4_) | copy-start | bytes 1327108
  20.4 20.1 %collective-permute-start.4 = (bf16[1728,128]{1,0:T(8,128)(2,1)S(1)}, bf16[1728,128]{1,0:T(8,128)(2,1)}, u32[]{:S(2)}, u32[]{:S(2)}) collective-permute-start(bf16[1728,128]{1,0:T(8,128)(2,1)S(1)} %collective-permute-done.3.rest_4_), channel_id=1, source_target_pairs={{1,0},{2,1},{5,4},{6,5},{9,8},{10,9},{13,12},{14,13},{17,16},{18,1... | collective-permute-start | bytes 1327112 | tf_op jit(solution)/shard_map/ppermute | solution.py:259
  21.7 26.5 %copy-start.3 = (bf16[1728,128]{1,0:T(8,128)(2,1)}, bf16[1728,128]{1,0:T(8,128)(2,1)S(1)}, u32[]{:S(2)}) copy-start(bf16[1728,128]{1,0:T(8,128)(2,1)S(1)} %collective-permute-done.rest_1_) | copy-start | bytes 1327108
  21.8 26.5 %collective-permute-start.1 = (bf16[1728,128]{1,0:T(8,128)(2,1)S(1)}, bf16[1728,128]{1,0:T(8,128)(2,1)}, u32[]{:S(2)}, u32[]{:S(2)}) collective-permute-start(bf16[1728,128]{1,0:T(8,128)(2,1)S(1)} %collective-permute-done.rest_1_), channel_id=1, source_target_pairs={{1,2},{2,3},{5,6},{6,7},{9,10},{10,11},{13,14},{14,15},{17,18},{18... | collective-permute-start | bytes 1327112 | tf_op jit(solution)/shard_map/ppermute | solution.py:258
  23.2 14.7 %collective-permute-start.15 = (bf16[768,128]{1,0:T(8,128)(2,1)}, bf16[768,128]{1,0:T(8,128)(2,1)S(1)}, u32[]{:S(2)}, u32[]{:S(2)}) collective-permute-start(bf16[768,128]{1,0:T(8,128)(2,1)} %get-tuple-element.16.rest_2_), channel_id=1, source_target_pairs={{1,0},{2,1},{3,2},{5,4},{6,5},{7,6},{9,8},{10,9},{11,10},{13,12},{... | collective-permute-start | bytes 589832 | tf_op jit(solution)/shard_map/ppermute | solution.py:259
  24.5 14.7 %collective-permute-start.12 = (bf16[768,128]{1,0:T(8,128)(2,1)}, bf16[768,128]{1,0:T(8,128)(2,1)S(1)}, u32[]{:S(2)}, u32[]{:S(2)}) collective-permute-start(bf16[768,128]{1,0:T(8,128)(2,1)} %get-tuple-element.16.rest_2_), channel_id=1, source_target_pairs={{0,1},{1,2},{2,3},{4,5},{5,6},{6,7},{8,9},{9,10},{10,11},{12,13},{... | collective-permute-start | bytes 589832 | tf_op jit(solution)/shard_map/ppermute | solution.py:258
  37.9 10.3 %copy-start.6 = (bf16[768,128]{1,0:T(8,128)(2,1)}, bf16[768,128]{1,0:T(8,128)(2,1)S(1)}, u32[]{:S(2)}) copy-start(bf16[768,128]{1,0:T(8,128)(2,1)S(1)} %collective-permute-done.15.rest_6_) | copy-start | bytes 589828
  37.9 7.7 %collective-permute-start.16 = (bf16[768,128]{1,0:T(8,128)(2,1)S(1)}, bf16[768,128]{1,0:T(8,128)(2,1)}, u32[]{:S(2)}, u32[]{:S(2)}) collective-permute-start(bf16[768,128]{1,0:T(8,128)(2,1)S(1)} %collective-permute-done.15.rest_6_), channel_id=1, source_target_pairs={{1,0},{2,1},{5,4},{6,5},{9,8},{10,9},{13,12},{14,13},{17,16},{18,1... | collective-permute-start | bytes 589832 | tf_op jit(solution)/shard_map/ppermute | solution.py:259
  39.2 9.0 %copy-start.7 = (bf16[768,128]{1,0:T(8,128)(2,1)}, bf16[768,128]{1,0:T(8,128)(2,1)S(1)}, u32[]{:S(2)}) copy-start(bf16[768,128]{1,0:T(8,128)(2,1)S(1)} %collective-permute-done.12.rest_3_) | copy-start | bytes 589828
  39.2 7.6 %collective-permute-start.13 = (bf16[768,128]{1,0:T(8,128)(2,1)S(1)}, bf16[768,128]{1,0:T(8,128)(2,1)}, u32[]{:S(2)}, u32[]{:S(2)}) collective-permute-start(bf16[768,128]{1,0:T(8,128)(2,1)S(1)} %collective-permute-done.12.rest_3_), channel_id=1, source_target_pairs={{1,2},{2,3},{5,6},{6,7},{9,10},{10,11},{13,14},{14,15},{17,18},{18... | collective-permute-start | bytes 589832 | tf_op jit(solution)/shard_map/ppermute | solution.py:258
  40.6 18.6 %collective-permute-start.5 = (bf16[1728,128]{1,0:T(8,128)(2,1)}, bf16[1728,128]{1,0:T(8,128)(2,1)}, u32[]{:S(2)}, u32[]{:S(2)}) collective-permute-start(bf16[1728,128]{1,0:T(8,128)(2,1)} %collective-permute-done.4.rest_5_), channel_id=1, source_target_pairs={{1,0},{5,4},{9,8},{13,12},{17,16},{21,20},{25,24},{29,28}} | collective-permute-start | bytes 1327112 | tf_op jit(solution)/shard_map/ppermute | solution.py:259
  41.9 65.2 %collective-permute-start.9 = (bf16[768,128]{1,0:T(8,128)(2,1)}, bf16[768,128]{1,0:T(8,128)(2,1)S(1)}, u32[]{:S(2)}, u32[]{:S(2)}) collective-permute-start(bf16[768,128]{1,0:T(8,128)(2,1)} %get-tuple-element.15.rest_2_), channel_id=1, source_target_pairs={{1,0},{2,1},{3,2},{5,4},{6,5},{7,6},{9,8},{10,9},{11,10},{13,12},{... | collective-permute-start | bytes 589832 | tf_op jit(solution)/shard_map/ppermute | solution.py:259
  45.6 40.9 %collective-permute-start.17 = (bf16[768,128]{1,0:T(8,128)(2,1)}, bf16[768,128]{1,0:T(8,128)(2,1)}, u32[]{:S(2)}, u32[]{:S(2)}) collective-permute-start(bf16[768,128]{1,0:T(8,128)(2,1)} %collective-permute-done.16.rest_7_), channel_id=1, source_target_pairs={{1,0},{5,4},{9,8},{13,12},{17,16},{21,20},{25,24},{29,28}} | collective-permute-start | bytes 589832 | tf_op jit(solution)/shard_map/ppermute | solution.py:259
  46.9 39.6 %collective-permute-start.14 = (bf16[768,128]{1,0:T(8,128)(2,1)}, bf16[768,128]{1,0:T(8,128)(2,1)}, u32[]{:S(2)}, u32[]{:S(2)}) collective-permute-start(bf16[768,128]{1,0:T(8,128)(2,1)} %collective-permute-done.13.rest_4_), channel_id=1, source_target_pairs={{2,3},{6,7},{10,11},{14,15},{18,19},{22,23},{26,27},{30,31}} | collective-permute-start | bytes 589832 | tf_op jit(solution)/shard_map/ppermute | solution.py:258
  48.2 16.6 %collective-permute-start.2 = (bf16[1728,128]{1,0:T(8,128)(2,1)}, bf16[1728,128]{1,0:T(8,128)(2,1)}, u32[]{:S(2)}, u32[]{:S(2)}) collective-permute-start(bf16[1728,128]{1,0:T(8,128)(2,1)} %collective-permute-done.1.rest_2_), channel_id=1, source_target_pairs={{2,3},{6,7},{10,11},{14,15},{18,19},{22,23},{26,27},{30,31}} | collective-permute-start | bytes 1327112 | tf_op jit(solution)/shard_map/ppermute | solution.py:258
  59.2 49.2 %collective-permute-start.6 = (bf16[768,128]{1,0:T(8,128)(2,1)S(1)}, bf16[768,128]{1,0:T(8,128)(2,1)}, u32[]{:S(2)}, u32[]{:S(2)}) collective-permute-start(bf16[768,128]{1,0:T(8,128)(2,1)S(1)} %copy-done.4), channel_id=1, source_target_pairs={{0,1},{1,2},{2,3},{4,5},{5,6},{6,7},{8,9},{9,10},{10,11},{12,13},{... | collective-permute-start | bytes 589832 | tf_op jit(solution)/shard_map/ppermute | solution.py:258
  86.5 70.8 %copy-start.1 = (bf16[384,1536]{1,0:T(8,128)(2,1)S(1)}, bf16[384,1536]{1,0:T(8,128)(2,1)}, u32[]{:S(2)}) copy-start(bf16[384,1536]{1,0:T(8,128)(2,1)} %get-tuple-element.12) | copy-start | bytes 3538948
  103.2 39.5 %all-to-all-start.2 = ((bf16[8,48,768]{2,1,0:T(8,128)(2,1)}), bf16[8,48,768]{2,1,0:T(8,128)(2,1)S(1)}, u32[]{:S(2)}, u32[]{:S(2)}) async-start(bf16[8,48,768]{2,1,0:T(8,128)(2,1)} %bitcast.11), calls=%async_computation.2 | async-start | bytes 1179648 | tf_op jit(solution)/shard_map/all_to_all | solution.py:290
  107.1 17.6 %copy-start.5 = (bf16[768,128]{1,0:T(8,128)(2,1)}, bf16[768,128]{1,0:T(8,128)(2,1)S(1)}, u32[]{:S(2)}) copy-start(bf16[768,128]{1,0:T(8,128)(2,1)S(1)} %collective-permute-done.9.rest_6_) | copy-start | bytes 589828
  107.1 9.2 %collective-permute-start.10 = (bf16[768,128]{1,0:T(8,128)(2,1)S(1)}, bf16[768,128]{1,0:T(8,128)(2,1)S(1)}, u32[]{:S(2)}, u32[]{:S(2)}) collective-permute-start(bf16[768,128]{1,0:T(8,128)(2,1)S(1)} %collective-permute-done.9.rest_6_), channel_id=1, source_target_pairs={{1,0},{2,1},{5,4},{6,5},{9,8},{10,9},{13,12},{14,13},{17,16},{18,1... | collective-permute-start | bytes 589832 | tf_op jit(solution)/shard_map/ppermute | solution.py:259
  108.4 9.2 %collective-permute-start.7 = (bf16[768,128]{1,0:T(8,128)(2,1)}, bf16[768,128]{1,0:T(8,128)(2,1)S(1)}, u32[]{:S(2)}, u32[]{:S(2)}) collective-permute-start(bf16[768,128]{1,0:T(8,128)(2,1)} %collective-permute-done.6.rest_3_), channel_id=1, source_target_pairs={{1,2},{2,3},{5,6},{6,7},{9,10},{10,11},{13,14},{14,15},{17,18},{18... | collective-permute-start | bytes 589832 | tf_op jit(solution)/shard_map/ppermute | solution.py:258
  116.3 8.4 %copy-start.8 = (bf16[768,128]{1,0:T(8,128)(2,1)}, bf16[768,128]{1,0:T(8,128)(2,1)S(1)}, u32[]{:S(2)}) copy-start(bf16[768,128]{1,0:T(8,128)(2,1)S(1)} %collective-permute-done.10.rest_7_) | copy-start | bytes 589828
  116.3 8.4 %collective-permute-start.11 = (bf16[768,128]{1,0:T(8,128)(2,1)S(1)}, bf16[768,128]{1,0:T(8,128)(2,1)S(1)}, u32[]{:S(2)}, u32[]{:S(2)}) collective-permute-start(bf16[768,128]{1,0:T(8,128)(2,1)S(1)} %collective-permute-done.10.rest_7_), channel_id=1, source_target_pairs={{1,0},{5,4},{9,8},{13,12},{17,16},{21,20},{25,24},{29,28}} | collective-permute-start | bytes 589832 | tf_op jit(solution)/shard_map/ppermute | solution.py:259
  117.6 7.1 %copy-start.9 = (bf16[768,128]{1,0:T(8,128)(2,1)}, bf16[768,128]{1,0:T(8,128)(2,1)S(1)}, u32[]{:S(2)}) copy-start(bf16[768,128]{1,0:T(8,128)(2,1)S(1)} %collective-permute-done.7.rest_4_) | copy-start | bytes 589828
  117.6 7.1 %collective-permute-start.8 = (bf16[768,128]{1,0:T(8,128)(2,1)S(1)}, bf16[768,128]{1,0:T(8,128)(2,1)S(1)}, u32[]{:S(2)}, u32[]{:S(2)}) collective-permute-start(bf16[768,128]{1,0:T(8,128)(2,1)S(1)} %collective-permute-done.7.rest_4_), channel_id=1, source_target_pairs={{2,3},{6,7},{10,11},{14,15},{18,19},{22,23},{26,27},{30,31}} | collective-permute-start | bytes 589832 | tf_op jit(solution)/shard_map/ppermute | solution.py:258
  124.7 0.7 copy-start.10
  125.4 0.7 copy-start.11
  142.6 34.5 %copy-start = (bf16[8,48,768]{2,1,0:T(8,128)(2,1)}, bf16[8,48,768]{2,1,0:T(8,128)(2,1)S(1)}, u32[]{:S(2)}) copy-start(bf16[8,48,768]{2,1,0:T(8,128)(2,1)S(1)} %all-to-all-done.2.rest_2_) | copy-start | bytes 1769476

commit v2 on v1

--- a/solution.py
+++ b/solution.py
@@ -27,7 +27,7 @@
 
 def chunk_list(channels):
     half = channels // 2
-    return ((0, half), (half, half // 2), (half + half // 2, half // 2))
+    return ((0, half), (half, half))
 
 
 def pack_body(chunks, blocks, counts, fields, block, stencil, frac, *rest):
@@ -79,63 +79,83 @@
         outs[0][base + span * 16 : base + (span + 1) * 16, :] = pair.astype(BF16)
 
 
-def interp_body(count, width, blocks, lead, here, *rest):
+def interp_body(count, width, blocks, lead, late, reach, here, *rest):
+    tiles, rest = rest[: len(reach)], rest[len(reach) :]
+    if not lead:
+        (params, ends), rest = rest[:2], rest[2:]
+    if late:
+        (given, table), rest = rest[:2], rest[2:]
+        (out, *rest), grid = rest[:-1], rest[-1]
+    else:
+        grid, *rest = rest
     if lead:
-        tiles, (table, out, params, ends, flipped, grid) = rest[: 2 * count - 1], rest[2 * count - 1 :]
+        params, ends, flipped = rest
     else:
-        ends, params, *rest = rest
-        tiles, (table, out, flipped, grid) = rest[: 2 * count - 1], rest[2 * count - 1 :]
+        (flipped,) = rest
     me = here[0]
+    far = count - 1
     groups = LANES // width
     planes = BLK // groups
-    spans = blocks * BLK // SPAN
+    sign = 1 - 2 * lax.rem(me, 2)
+    owners = [me + side * sign * away for away, side in reach]
+
+    def present(number):
+        return (owners[number] >= 0) & (owners[number] < count)
 
     def take(tile, owner):
         for plane in range(planes):
             rows = tile[plane * blocks : (plane + 1) * blocks, :]
             flipped[owner, plane * LANES : (plane + 1) * LANES, :] = rows.T
-        if lead:
-            params[owner] = tile[planes * blocks :, :]
-
-    take(tiles[0], me)
-    for away in range(1, count):
-
-        @pl.when(me >= away)
-        def _(away=away):
-            take(tiles[away], me - away)
-
-        @pl.when(me + away < count)
-        def _(away=away):
-            take(tiles[count - 1 + away], me + away)
 
     if lead:
+        for number, tile in enumerate(tiles):
+
+            @pl.when(present(number))
+            def _(number=number, tile=tile):
+                params[owners[number]] = tile[planes * blocks :, :]
+
         for tile in range(count):
-            rows = params[tile].astype(F32)
-            which = lax.broadcasted_iota(jnp.int32, rows.shape, 0) % 8 == 7
             ends[tile, 0] = 0
-            for index in range(SLOTS):
-                listed = jnp.where(which & (rows <= index), 1.0, 0.0)
-                ends[tile, index + 1] = jnp.sum(listed).astype(jnp.int32)
-
-    grid[...] = jnp.zeros_like(grid)
+
+            @pl.when(late | (jnp.abs(me - tile) < far))
+            def _(tile=tile):
+                rows = params[tile].astype(F32)
+                which = lax.broadcasted_iota(jnp.int32, rows.shape, 0) % 8 == 7
+                for index in range(SLOTS):
+                    listed = jnp.where(which & (rows <= index), 1.0, 0.0)
+                    ends[tile, index + 1] = jnp.sum(listed).astype(jnp.int32)
+
+    if late:
+        grid[...] = given[...]
+    else:
+        grid[...] = jnp.zeros_like(grid)
+
     block_row = lax.broadcasted_iota(jnp.int32, (blocks, SPAN), 0).astype(F32)
     cell_row = lax.broadcasted_iota(jnp.int32, (BLK, SPAN), 0).astype(F32)
 
-    def job(number, _):
-        owner = number // SLOTS
-        index = number % SLOTS
+    def wanted(owner, index):
+        target = lax.rem(owner - index + 1 + count, count)
+        if not lead:
+            return jnp.bool_(True)
+        distant = jnp.maximum(jnp.abs(target - me), jnp.abs(owner - me)) == far
+        return distant if late else jnp.logical_not(distant)
+
+    def job(owner, index):
         target = lax.rem(owner - index + 1 + count, count)
         low = ends[target, index]
         high = ends[target, index + 1]
         place = pl.multiple_of(target * LANES, LANES)
-
-        def span_step(span, _):
+        first = low // SPAN
+        last = jnp.where(high > low, (high + SPAN - 1) // SPAN, first)
+
+        def span_step(span, valid):
             both = params[target, pl.ds(pl.multiple_of(span * 16, 16), 16), :].astype(F32)
 
             def line(i):
                 return jnp.concatenate([both[i : i + 1, :], both[8 + i : 9 + i, :]], axis=1)
 
-            key = jnp.where(line(7) == index.astype(F32), line(0), -1.0)
+            mine = line(7) == jnp.where(valid, index, -1).astype(F32)
+            key = jnp.where(mine, line(0), -1.0)
             onehot = jnp.where(block_row == key, 1.0, 0.0).astype(BF16)
             f_lat = (line(5) + 0.5) / FRAC
             f_lon = (line(6) + 0.5) / FRAC
@@ -148,80 +168,127 @@
             weight = jnp.zeros((BLK, SPAN), F32)
             for corner in range(4):
                 weight += jnp.where(cell_row == line(1 + corner), corners[corner], 0.0)
+            picked = jnp.dot(flipped[owner], onehot, preferred_element_type=F32)
             total = jnp.zeros((width, SPAN), F32)
-            for plane in range(planes):
-                picked = jnp.dot(
-                    flipped[owner, plane * LANES : (plane + 1) * LANES, :],
-                    onehot,
-                    preferred_element_type=F32,
-                )
-                for group in range(groups):
-                    cell = group * planes + plane
-                    total += (
-                        weight[cell : cell + 1, :] * picked[group * width : (group + 1) * width, :]
-                    )
-            total = total.astype(BF16)
+            for cell in range(BLK):
+                start = cell % planes * LANES + cell // planes * width
+                total += weight[cell : cell + 1, :] * picked[start : start + width, :]
+            return total.astype(BF16)
+
+        def add(span, total):
             for half in range(2):
                 rows = pl.ds(pl.multiple_of((2 * span + half) * width, width), width)
                 grid[rows, pl.ds(place, LANES)] += total[:, half * LANES : (half + 1) * LANES]
+
+        def pair_step(pair, _):
+            one = first + 2 * pair
+            two = jnp.minimum(one + 1, last - 1)
+            total_one = span_step(one, True)
+            total_two = span_step(two, one + 1 < last)
+            add(one, total_one)
+            add(two, total_two)
             return 0
 
-        first = low // SPAN
-        last = jnp.where(high > low, (high + SPAN - 1) // SPAN, first)
-        lax.fori_loop(first, last, span_step, 0)
+        lax.fori_loop(0, (last - first + 1) // 2, pair_step, 0)
+
+    for number, tile in enumerate(tiles):
+        owner = owners[number]
+        needed = present(number)
+        if lead and late:
+            asked = [wanted(owner, index) for index in range(SLOTS)]
+            needed = needed & functools.reduce(jnp.logical_or, asked)
+
+        @pl.when(needed)
+        def _(tile=tile, owner=owner):
+            take(tile, owner)
+
+            def each(index, _):
+                @pl.when(wanted(owner, index))
+                def _():
+                    job(owner, index)
+
+                return 0
+
+            lax.fori_loop(0, SLOTS, each, 0)
+
+    if late:
+        out[...] = lax.dot_general(
+            table[...], grid[...], (((1,), (1,)), ((), ())), preferred_element_type=F32
+        ).astype(BF16)
+
+
+def collect_body(chunks, lat_rows, *rest):
+    parts, gathered = rest[:-1], rest[-1]
+    bands, waves, _ = parts[0].shape
+    lane = lax.broadcasted_iota(jnp.int32, (waves, LANES), 1)
+
+    def collect(source, _):
+        for row in range(lat_rows):
+            total = None
+            for part, (first, width) in zip(parts, chunks, strict=True):
+                groups = LANES // width
+                tile, group = row // groups, row % groups
+                values = part[source, :, tile * LANES : (tile + 1) * LANES].astype(F32)
+                turn = (first - group * width) % LANES
+                if turn:
+                    values = pltpu.roll(values, turn, 1)
+                total = values if total is None else jnp.where(lane >= first, values, total)
+            start = pl.multiple_of((source * lat_rows + row) * waves, 8)
+            gathered[pl.ds(start, waves), :] = total
         return 0
 
-    lax.fori_loop(0, count * SLOTS, job, 0)
-    spectra = lax.dot_general(
-        table[...], grid[...], (((1,), (1,)), ((), ())), preferred_element_type=F32
-    )
-    out[...] = spectra.astype(BF16)
-
-
-def final_body(chunks, lat_rows, per_step, legendre, *rest):
-    parts, (out, gathered, factor) = rest[: len(chunks)], rest[len(chunks) :]
-    sources, waves, _ = parts[0].shape
-    degrees = legendre.shape[2]
-
-    @pl.when(pl.program_id(0) == 0)
-    def _():
-        degree = lax.broadcasted_iota(jnp.int32, factor.shape, 0).astype(F32)
-        factor[...] = 1.0 / (1.0 + 4.0 * degree * (degree + 1.0) / (degrees * (degrees + 1)))
-        lane = lax.broadcasted_iota(jnp.int32, (waves, LANES), 1)
-
-        def gather(source, _):
-            for row in range(lat_rows):
-                total = None
-                for part, (first, width) in zip(parts, chunks, strict=True):
-                    groups = LANES // width
-                    tile, group = row // groups, row % groups
-                    values = part[source, :, tile * LANES : (tile + 1) * LANES].astype(F32)
-                    shift = (first - group * width) % LANES
-                    if shift:
-                        values = pltpu.roll(values, shift, 1)
-                    total = values if total is None else jnp.where(lane >= first, values, total)
-                start = pl.multiple_of((source * lat_rows + row) * waves, 8)
-                gathered[pl.ds(start, waves), :] = total
-            return 0
-
-        lax.fori_loop(0, sources, gather, 0)
-
-    for step in range(per_step):
-        wave = pl.program_id(0) * per_step + step
-        column = gathered[pl.ds(wave, sources * lat_rows, stride=waves), :].astype(BF16)
-        projected = lax.dot_general(
-            legendre[step], column, (((0,), (0,)), ((), ())), preferred_element_type=F32
-        )
-        out[step] = projected * factor[...]
-
-
-def whole(shape):
-    return pl.BlockSpec(shape, lambda *_: (0,) * len(shape))
+    lax.fori_loop(0, bands, collect, 0)
+
+
+def final_body(last, lat_rows, per_step, legendre, early, part, out, gathered, factor, staged, done):
+    waves, lat_total, degrees = legendre.shape
+    bands = part.shape[0]
+    first, width = last
+    degree = lax.broadcasted_iota(jnp.int32, factor.shape, 0).astype(F32)
+    factor[...] = 1.0 / (1.0 + 4.0 * degree * (degree + 1.0) / (degrees * (degrees + 1)))
+    lane = lax.broadcasted_iota(jnp.int32, (waves, LANES), 1)
+    groups = LANES // width
+
+    def collect(source, _):
+        for row in range(lat_rows):
+            tile, group = row // groups, row % groups
+            values = part[source, :, tile * LANES : (tile + 1) * LANES].astype(F32)
+            turn = (first - group * width) % LANES
+            if turn:
+                values = pltpu.roll(values, turn, 1)
+            rows = pl.ds(pl.multiple_of((source * lat_rows + row) * waves, 8), waves)
+            gathered[rows, :] = jnp.where(lane >= first, values, early[rows, :])
+        return 0
+
+    lax.fori_loop(0, bands, collect, 0)
+
+    def step(number, _):
+        for inner in range(per_step):
+            wave = number * per_step + inner
+            column = gathered[pl.ds(wave, lat_total, stride=waves), :].astype(BF16)
+            projected = lax.dot_general(
+                legendre[wave], column, (((0,), (0,)), ((), ())), preferred_element_type=F32
+            )
+            staged[wave] = projected * factor[...]
+        rows = pl.ds(number * per_step, per_step)
+        pltpu.make_async_copy(staged.at[rows], out.at[rows], done).start()
+        return 0
+
+    lax.fori_loop(0, waves // per_step, step, 0)
+    pltpu.make_async_copy(staged, out, done).wait()
 
 
 VMEM = pl.BlockSpec(memory_space=pltpu.VMEM)
 SMEM = pl.BlockSpec(memory_space=pltpu.SMEM)
-LIMIT = pltpu.CompilerParams(vmem_limit_bytes=56 * 2**20)
+ANY = pl.BlockSpec(memory_space=pl.ANY)
+
+
+def limit(mib):
+    return pltpu.CompilerParams(vmem_limit_bytes=mib * 2**20)
+
+
+def cost(flops):
+    return pl.CostEstimate(flops=flops, bytes_accessed=10**6, transcendentals=0)
 
 
 def gathering(fields, req_block, req_stencil, req_frac, req_count, legendre):
@@ -245,64 +312,96 @@
         functools.partial(pack_body, chunks, blocks),
         out_shape=[jax.ShapeDtypeStruct((rows, LANES), BF16) for rows in tile_rows],
         in_specs=[SMEM, VMEM, VMEM, VMEM, VMEM],
-        out_specs=[VMEM] * len(chunks),
+        out_specs=[VMEM] * len(tile_rows),
         scratch_shapes=[pltpu.VMEM((cells, channels), F32)],
-        compiler_params=LIMIT,
+        compiler_params=limit(16),
+        name="pack",
     )(req_count[0, 0], fields.reshape(cells, channels), req_block[0, 0], req_stencil[0, 0], req_frac[0, 0])
 
+    def links(parity, away):
+        up = [(i, i + 1) for i in range(parity, count - 1, 2) if i - away + 1 >= 0]
+        down = [(i + 1, i) for i in range(parity, count - 1, 2) if i + away < count]
+        return up + down
+
+    held = [[(packed[number], 0, 1)] for number in range(len(chunks))]
+    edge = [(tile, tile) for tile in packed]
+    for away in range(1, count):
+        for number in range(len(chunks)):
+            even, odd = edge[number]
+            both = []
+            for parity, tile, side in ((0, odd, 1), (1, even, -1)):
+                pairs = links(parity, away)
+                both.append(lax.ppermute(tile, "lon", pairs) if pairs else None)
+                if pairs:
+                    held[number].append((both[-1], away, side))
+            edge[number] = tuple(both)
+
     parts = []
-    ends = params = None
+    params = ends = None
     for number, (first, width) in enumerate(chunks):
-        below, above = [packed[number]], [packed[number]]
-        for away in range(1, count):
-            below.append(lax.ppermute(below[-1], "lon", [(i, i + 1) for i in range(away - 1, count - 1)]))
-            above.append(lax.ppermute(above[-1], "lon", [(i + 1, i) for i in range(count - away)]))
-        tiles = below + above[1:]
         lead = number == 0
-        out_shape = [jax.ShapeDtypeStruct((sector_waves, lat_rows * width), BF16)]
-        out_specs = [VMEM]
-        given = [here]
+        soon = [one for one in held[number] if one[1] < count - 1]
+        last = held[number] if lead else [one for one in held[number] if one[1] == count - 1]
+        flipped = pltpu.VMEM((count, BLK * width, blocks), BF16)
+        grid = jax.ShapeDtypeStruct((lat_rows * width, lon_total), BF16)
+        listed = [
+            jax.ShapeDtypeStruct((count, cells // LANES * 8, LANES), BF16),
+            jax.ShapeDtypeStruct((count, SLOTS + 1), jnp.int32),
+        ]
+        given = [] if lead else [params, ends]
+        given_specs = [] if lead else [VMEM, SMEM]
+        kept = [pltpu.VMEM(listed[0].shape, BF16), pltpu.SMEM(listed[1].shape, jnp.int32)]
+        grid = pl.pallas_call(
+            functools.partial(interp_body, count, width, blocks, lead, False, [one[1:] for one in soon]),
+            out_shape=grid,
+            in_specs=[SMEM] + [VMEM] * len(soon) + given_specs,
+            out_specs=VMEM,
+            scratch_shapes=(kept if lead else []) + [flipped],
+            compiler_params=limit(24),
+            cost_estimate=cost(width * 10**8),
+            name="early",
+        )(here, *[one[0] for one in soon], *given)
+        fourier, *found = pl.pallas_call(
+            functools.partial(interp_body, count, width, blocks, lead, True, [one[1:] for one in last]),
+            out_shape=[jax.ShapeDtypeStruct((sector_waves, lat_rows * width), BF16)]
+            + (listed if lead else []),
+            in_specs=[SMEM] + [VMEM] * len(last) + given_specs + [VMEM, VMEM],
+            out_specs=[VMEM] + ([VMEM, SMEM] if lead else []),
+            scratch_shapes=[flipped, pltpu.VMEM(grid.shape, BF16)],
+            compiler_params=limit(24),
+            cost_estimate=cost(width * 5 * 10**7),
+            name="late",
+        )(here, *[one[0] for one in last], *given, grid, table)
         if lead:
-            out_shape += [
-                jax.ShapeDtypeStruct((count, cells // LANES * 8, LANES), BF16),
-                jax.ShapeDtypeStruct((count, SLOTS + 1), jnp.int32),
-            ]
-            out_specs += [VMEM, SMEM]
-        else:
-            given += [ends, params]
-        results = pl.pallas_call(
-            functools.partial(interp_body, count, width, blocks, lead),
-            out_shape=out_shape,
-            in_specs=[SMEM] + ([] if lead else [SMEM, VMEM]) + [VMEM] * (len(tiles) + 1),
-            out_specs=out_specs,
-            scratch_shapes=[
-                pltpu.VMEM((count, BLK * width, blocks), BF16),
-                pltpu.VMEM((lat_rows * width, lon_total), BF16),
-            ],
-            compiler_params=LIMIT,
-            cost_estimate=pl.CostEstimate(flops=width * 10**7, bytes_accessed=10**6, transcendentals=0),
-        )(*given, *tiles, table)
-        if lead:
-            fourier, params, ends = results
-        else:
-            (fourier,) = results
+            params, ends = found
         fourier = fourier.reshape(bands, waves, lat_rows * width)
         parts.append(lax.all_to_all(fourier, "lat", split_axis=0, concat_axis=0, tiled=True))
 
-    per_step = math.gcd(waves, 4)
+    gathered = jax.ShapeDtypeStruct((lat_total * waves, channels), F32)
+    early = pl.pallas_call(
+        functools.partial(collect_body, chunks[:-1], lat_rows),
+        out_shape=gathered,
+        in_specs=[VMEM] * (len(chunks) - 1),
+        out_specs=VMEM,
+        compiler_params=limit(16),
+        cost_estimate=cost(10**9),
+        name="collect",
+    )(*parts[:-1])
+    per_step = math.gcd(waves, 8)
     return pl.pallas_call(
-        functools.partial(final_body, chunks, lat_rows, per_step),
-        grid=(waves // per_step,),
+        functools.partial(final_body, chunks[-1], lat_rows, per_step),
         out_shape=jax.ShapeDtypeStruct((waves, degrees, channels), F32),
-        in_specs=[pl.BlockSpec((per_step, lat_total, degrees), lambda i: (i, 0, 0))]
-        + [whole(part.shape) for part in parts],
-        out_specs=pl.BlockSpec((per_step, degrees, channels), lambda i: (i, 0, 0)),
+        in_specs=[VMEM] * 3,
+        out_specs=ANY,
         scratch_shapes=[
-            pltpu.VMEM((lat_total * waves, channels), F32),
+            pltpu.VMEM(gathered.shape, F32),
             pltpu.VMEM((degrees, channels), F32),
+            pltpu.VMEM((waves, degrees, channels), F32),
+            pltpu.SemaphoreType.DMA,
         ],
-        compiler_params=LIMIT,
-    )(legendre, *parts)
+        compiler_params=limit(28),
+        name="final",
+    )(legendre, early, parts[-1])
 
 
 def padded(cells, sides, width):

time: 199 us -> 132 us (0.66)
  blocking collectives: 34.5 us -> 0 us
  Pallas kernels: 78.9 us -> 50.2 us
  starting transfers between devices: 39.1 us -> 24 us
  local copies, waits for them, and re-layouts: 2.68 us -> 15.2 us
    all_to_all x2 -> x0, blocking collectives: 34.5 us -> none  [gathering(): lax.all_to_all(fourier, 'lat', split_axis=0, concat_axis=0, tiled=True)]
    pallas_call x4 -> x6, Pallas kernels: 75.2 us -> 48.5 us  [the longest x4 38.5 us: gathering(): pl.pallas_call(functools.partial(interp_body, count, width, blocks, lead,...]
    ppermute x18 -> x10, starting transfers between devices: 35.2 us -> 16.2 us  [gathering(): both.append(lax.ppermute(tile, 'lon', pairs) if pairs else None)]
    ppermute x18 -> x10, waiting for transfers between devices: 37.2 us -> 23 us  [gathering(): both.append(lax.ppermute(tile, 'lon', pairs) if pairs else None)]
    all_to_all x1 -> x2, waiting for transfers between devices: 0.01 us -> 13.8 us  [gathering(): lax.all_to_all(fourier, 'lat', split_axis=0, concat_axis=0, tiled=True)]
    unnamed x25 -> x19, local copies, waits for them, and re-layouts: 2.68 us -> 15.2 us
    all_to_all x1 -> x2, starting transfers between devices: 3.89 us -> 7.75 us  [gathering(): lax.all_to_all(fourier, 'lat', split_axis=0, concat_axis=0, tiled=True)]
  transfers between devices with their start and end apart: 19 -> 12, of which waited for: 6 -> 5; matrix products, arithmetic and copies ran while one was open for 2% -> 3% of each run, Pallas kernels for 28% -> 30%
where the time goes in v2:
time: 132 us; the launch traced here: 131 us
  Pallas kernels  50.2 us (38%)
  waiting for transfers between devices  36.8 us (28%)
  starting transfers between devices  24 us (18%)
  local copies, waits for them, and re-layouts  15.2 us (12%)
  other arithmetic  4.24 us (3%)
    pallas_call x4, Pallas kernels, gathering(): pl.pallas_call(functools.partial(interp_body, count, width, blocks, lead,...  38.5 us
    ppermute x10, waiting for transfers between devices, gathering(): both.append(lax.ppermute(tile, 'lon', pairs) if pairs else None)  23 us
    ppermute x10, starting transfers between devices, gathering(): both.append(lax.ppermute(tile, 'lon', pairs) if pairs else None)  16.2 us
    unnamed x19, local copies, waits for them, and re-layouts  15.2 us
    all_to_all x2, waiting for transfers between devices, gathering(): lax.all_to_all(fourier, 'lat', split_axis=0, concat_axis=0, tiled=True)  13.8 us
    pallas_call x1, Pallas kernels, gathering(): pl.pallas_call(functools.partial(final_body, chunks[-1], lat_rows, per_st...  9.11 us
    all_to_all x2, starting transfers between devices, gathering(): lax.all_to_all(fourier, 'lat', split_axis=0, concat_axis=0, tiled=True)  7.75 us
    convert_element_type x1, other arithmetic, hartley_table(): ((jnp.cos(phase_angle) + jnp.sin(phase_angle)) / math.sqrt(lon_total)).as...  2.92 us
  transfers between devices with their start and end apart: 12, of which 5 were waited for; matrix products, arithmetic and copies ran while one was open for 3% of the time, Pallas kernels for 30%

profile of v2, /device:TPU:0, one launch (start us, length us, event | category | flops | bytes accessed | tf_op | source)
XLA Modules:
  0.0 130.8 jit_solution(12653940496951994818)
XLA Ops:
  0.0 0.7 copy.9
  0.7 1.1 copy-done.3
  1.9 0.0 copy-start.4
  1.9 0.8 copy-done.4
  2.7 0.0 copy-start.5
  2.7 0.8 copy-done.5
  3.4 0.7 copy-done.6
  4.1 1.8 %pack.1 = (bf16[1728,128]{1,0:T(8,128)(2,1)S(1)}, bf16[1536,128]{1,0:T(8,128)(2,1)S(1)}) custom-call(s32[3]{0:T(128)S(1)} %bitcast.14, bf16[3072,128]{1,0:T(8,128)(2,1)S(1)} %bitcast.10, s32[3,1280]{1,0:T(4,128)S(1)} %bitcast.11, s32[3,4,1280]{2,1,0:T(4,128)S(1)} %bitcast.12, s32[3,2,1280]{2,1,0:T(2,128)S(1)} %bitcast.13), custom_call_target="tpu_custom_call" | custom-call | tf_op jit(solution)/shard_map/pack/pallas_call | solution.py:311
  5.9 0.7 collective-permute-start.1
  6.6 5.9 %collective-permute-start = (bf16[1728,128]{1,0:T(8,128)(2,1)S(1)}, bf16[1728,128]{1,0:T(8,128)(2,1)S(1)}, u32[]{:S(2)}, u32[]{:S(2)}) collective-permute-start(bf16[1728,128]{1,0:T(8,128)(2,1)S(1)} %get-tuple-element.10.rest_0_), channel_id=1, source_target_pairs={{0,1},{2,3},{1,0},{3,2},{4,5},{6,7},{5,4},{7,6},{8,9},{10,11},{9,8... | collective-permute-start | bytes 1327112 | tf_op jit(solution)/shard_map/ppermute | solution.py:334
  12.4 0.7 collective-permute-start.8
  13.1 1.8 %collective-permute-start.5 = (bf16[1536,128]{1,0:T(8,128)(2,1)S(1)}, bf16[1536,128]{1,0:T(8,128)(2,1)S(1)}, u32[]{:S(2)}, u32[]{:S(2)}) collective-permute-start(bf16[1536,128]{1,0:T(8,128)(2,1)S(1)} %get-tuple-element.12.rest_0_), channel_id=1, source_target_pairs={{0,1},{2,3},{1,0},{3,2},{4,5},{6,7},{5,4},{7,6},{8,9},{10,11},{9,8... | collective-permute-start | bytes 1179656 | tf_op jit(solution)/shard_map/ppermute | solution.py:334
  14.9 0.0 collective-permute-done.1.rest_2_
  14.9 1.3 collective-permute-start.2
  16.2 7.3 %collective-permute-done.rest_1_ = bf16[1728,128]{1,0:T(8,128)(2,1)S(1)} collective-permute-done((bf16[1728,128]{1,0:T(8,128)(2,1)S(1)}, bf16[1728,128]{1,0:T(8,128)(2,1)S(1)}, u32[]{:S(2)}, u32[]{:S(2)}) %collective-permute-start) | collective-permute-done | bytes 442400 | tf_op jit(solution)/shard_map/ppermute | solution.py:334
  23.5 0.7 collective-permute-start.3
  24.2 1.3 %add_select_fusion = s32[1536,512]{1,0:T(8,128)S(1)} fusion(), kind=kLoop, calls=%fused_computation | loop fusion | flops 9437184 | bytes 3145728 | tf_op jit(solution)/shard_map/jit(remainder)/select_n | solution.py:23
  25.5 2.9 %multiply_convert_fusion.rest_7_.rest_4_ = bf16[384,512]{1,0:T(8,128)(2,1)S(1)} fusion(s32[1536,512]{1,0:T(8,128)S(1)} %add_select_fusion, s32[]{:T(128)S(6)} %select_n.11), kind=kLoop, calls=%fused_computation.9 | loop fusion | flops 983040 | bytes 1179652 | tf_op jit(solution)/shard_map/convert_element_type | solution.py:25
  28.4 0.0 collective-permute-done.8.rest_2_
  28.4 1.3 collective-permute-start.9
  29.7 2.2 %collective-permute-done.5.rest_1_ = bf16[1536,128]{1,0:T(8,128)(2,1)S(1)} collective-permute-done((bf16[1536,128]{1,0:T(8,128)(2,1)S(1)}, bf16[1536,128]{1,0:T(8,128)(2,1)S(1)}, u32[]{:S(2)}, u32[]{:S(2)}) %collective-permute-start.5) | collective-permute-done | bytes 393248 | tf_op jit(solution)/shard_map/ppermute | solution.py:334
  31.9 1.4 %collective-permute-start.6 = (bf16[1536,128]{1,0:T(8,128)(2,1)S(1)}, bf16[1536,128]{1,0:T(8,128)(2,1)}, u32[]{:S(2)}, u32[]{:S(2)}) collective-permute-start(bf16[1536,128]{1,0:T(8,128)(2,1)S(1)} %collective-permute-done.5.rest_1_), channel_id=1, source_target_pairs={{1,2},{2,1},{5,6},{6,5},{9,10},{10,9},{13,14},{14,13},{17,18},{18,... | collective-permute-start | bytes 1179656 | tf_op jit(solution)/shard_map/ppermute | solution.py:334
  33.3 0.0 collective-permute-done.3.rest_4_
  33.3 1.3 collective-permute-start.4
  34.6 6.8 %collective-permute-done.2.rest_3_ = bf16[1728,128]{1,0:T(8,128)(2,1)S(1)} collective-permute-done((bf16[1728,128]{1,0:T(8,128)(2,1)S(1)}, bf16[1728,128]{1,0:T(8,128)(2,1)S(1)}, u32[]{:S(2)}, u32[]{:S(2)}) %collective-permute-start.2) | collective-permute-done | bytes 442400 | tf_op jit(solution)/shard_map/ppermute | solution.py:334
  41.4 10.0 %early.2.rest_6_ = bf16[1536,512]{1,0:T(8,128)(2,1)S(1)} custom-call(s32[1]{0:T(128)} %bitcast.here, bf16[1728,128]{1,0:T(8,128)(2,1)S(1)} %get-tuple-element.10.rest_0_, bf16[1728,128]{1,0:T(8,128)(2,1)S(1)} %collective-permute-done.rest_1_, bf16[1728,128]{1,0:T(8,128)(2,1)S(1)} %collective-permute-done.1.rest_2_, ...), custom_call_target="tpu_custom_call" | custom-call | flops 6400000000 | bytes 1000000 | tf_op jit(solution)/shard_map/early/pallas_call | solution.py:354
  51.4 6.8 %collective-permute-done.4.rest_5_ = bf16[1728,128]{1,0:T(8,128)(2,1)S(1)} collective-permute-done((bf16[1728,128]{1,0:T(8,128)(2,1)S(1)}, bf16[1728,128]{1,0:T(8,128)(2,1)S(1)}, u32[]{:S(2)}, u32[]{:S(2)}) %collective-permute-start.4) | collective-permute-done | bytes 442400 | tf_op jit(solution)/shard_map/ppermute | solution.py:334
  58.1 9.3 %late.2 = (bf16[384,1536]{1,0:T(8,128)(2,1)}, bf16[4,192,128]{2,1,0:T(8,128)(2,1)S(1)}, s32[4,4]{1,0:T(4,128)S(1)}) custom-call(s32[1]{0:T(128)} %bitcast.here, bf16[1728,128]{1,0:T(8,128)(2,1)S(1)} %get-tuple-element.10.rest_0_, bf16[1728,128]{1,0:T(8,128)(2,1)S(1)} %collective-permute-done.rest_1_, bf16[1728,128]{1,0:T(8,128)(2,1)S(1)} %collective-permute-done.1.rest_2_, ...), custom_call_target="tpu_custom_call" | custom-call | flops 3200000000 | bytes 1000000 | tf_op jit(solution)/shard_map/late/pallas_call | solution.py:364
  67.4 0.0 copy-start.7
  67.4 0.7 copy-done.7
  68.1 3.6 %all-to-all-start = ((bf16[8,48,1536]{2,1,0:T(8,128)(2,1)}), bf16[8,48,1536]{2,1,0:T(8,128)(2,1)S(1)}, u32[]{:S(2)}, u32[]{:S(2)}) async-start(bf16[8,48,1536]{2,1,0:T(8,128)(2,1)} %bitcast.5), calls=%async_computation | async-start | bytes 2359296 | tf_op jit(solution)/shard_map/all_to_all | solution.py:378
  71.7 0.0 collective-permute-done.6.rest_4_
  71.7 1.3 collective-permute-start.7
  73.0 0.0 collective-permute-done.9.rest_3_
  73.0 0.0 copy-start.8
  73.0 0.9 copy-done.8
  73.9 13.0 %early.3.rest_3_ = bf16[1536,512]{1,0:T(8,128)(2,1)S(1)} custom-call(s32[1]{0:T(128)} %bitcast.here, bf16[1536,128]{1,0:T(8,128)(2,1)S(1)} %get-tuple-element.12.rest_0_, bf16[1536,128]{1,0:T(8,128)(2,1)S(1)} %collective-permute-done.5.rest_1_, bf16[1536,128]{1,0:T(8,128)(2,1)S(1)} %collective-permute-done.8.rest_2_, ...), custom_call_target="tpu_custom_call" | custom-call | flops 6400000000 | bytes 1000000 | tf_op jit(solution)/shard_map/early/pallas_call | solution.py:354
  86.9 0.0 collective-permute-done.7.rest_0_
  86.9 6.3 %late.3 = bf16[384,1536]{1,0:T(8,128)(2,1)} custom-call(s32[1]{0:T(128)} %bitcast.here, bf16[1536,128]{1,0:T(8,128)(2,1)S(1)} %collective-permute-done.7.rest_0_, bf16[4,192,128]{2,1,0:T(8,128)(2,1)S(1)} %copy-done.8, s32[4,4]{1,0:T(4,128)S(1)} %get-tuple-element.14.rest_6_.rest_2_, bf16[1536,512]{1,0:T(8,128)(2,1)S(1)} %early.3.rest_3_, ...), custom_call_target="tpu_custom_call" | custom-call | flops 3200000000 | bytes 1000000 | tf_op jit(solution)/shard_map/late/pallas_call | solution.py:364
  93.2 0.0 all-to-all-done.rest_0_
  93.2 4.2 %all-to-all-start.1 = ((bf16[8,48,1536]{2,1,0:T(8,128)(2,1)}), bf16[8,48,1536]{2,1,0:T(8,128)(2,1)S(1)}, u32[]{:S(2)}, u32[]{:S(2)}) async-start(bf16[8,48,1536]{2,1,0:T(8,128)(2,1)} %bitcast.6), calls=%async_computation.1 | async-start | bytes 2359296 | tf_op jit(solution)/shard_map/all_to_all | solution.py:378
  97.4 0.9 collect.1.early
  98.2 0.0 copy-start
  98.3 2.2 %copy-done = f32[9216,128]{1,0:T(8,128)} copy-done((f32[9216,128]{1,0:T(8,128)}, f32[9216,128]{1,0:T(8,128)S(1)}, u32[]{:S(2)}) %copy-start) | copy-done | bytes 4718616
  100.4 13.8 %all-to-all-done.1.part = bf16[8,48,1536]{2,1,0:T(8,128)(2,1)S(1)} async-done(((bf16[8,48,1536]{2,1,0:T(8,128)(2,1)}), bf16[8,48,1536]{2,1,0:T(8,128)(2,1)S(1)}, u32[]{:S(2)}, u32[]{:S(2)}) %all-to-all-start.1) | async-done | bytes 1179680 | tf_op jit(solution)/shard_map/all_to_all | solution.py:378
  114.2 2.3 %copy-done.1 = f32[9216,128]{1,0:T(8,128)S(1)} copy-done((f32[9216,128]{1,0:T(8,128)S(1)}, f32[9216,128]{1,0:T(8,128)}, u32[]{:S(2)}) %copy-start.1) | copy-done | bytes 4718616
  116.5 5.0 %copy-done.2 = bf16[48,192,768]{2,1,0:T(8,128)(2,1)S(1)} copy-done((bf16[48,192,768]{2,1,0:T(8,128)(2,1)S(1)}, bf16[48,192,768]{2,1,0:T(8,128)(2,1)}, u32[]{:S(2)}) %copy-start.2) | copy-done | bytes 14155800
  121.6 9.1 %final.1 = f32[48,768,128]{2,1,0:T(8,128)} custom-call(bf16[48,192,768]{2,1,0:T(8,128)(2,1)S(1)} %copy-done.2, f32[9216,128]{1,0:T(8,128)S(1)} %copy-done.1, bf16[8,48,1536]{2,1,0:T(8,128)(2,1)S(1)} %all-to-all-done.1.part), custom_call_target="tpu_custom_call" | custom-call | tf_op jit(solution)/shard_map/final/pallas_call | solution.py:391
  (4 shorter events, 0.0 us)
Async XLA Ops:
  0.7 1.1 copy-start.3
  1.9 0.8 copy-start.4
  2.7 0.8 copy-start.5
  3.4 0.7 copy-start.6
  5.9 9.0 %collective-permute-start.1 = (bf16[1728,128]{1,0:T(8,128)(2,1)S(1)}, bf16[1728,128]{1,0:T(8,128)(2,1)S(1)}, u32[]{:S(2)}, u32[]{:S(2)}) collective-permute-start(bf16[1728,128]{1,0:T(8,128)(2,1)S(1)} %get-tuple-element.10.rest_0_), channel_id=1, source_target_pairs={{1,2},{2,1},{5,6},{6,5},{9,10},{10,9},{13,14},{14,13},{17,18},{18,... | collective-permute-start | bytes 1327112 | tf_op jit(solution)/shard_map/ppermute | solution.py:334
  6.6 16.9 %collective-permute-start = (bf16[1728,128]{1,0:T(8,128)(2,1)S(1)}, bf16[1728,128]{1,0:T(8,128)(2,1)S(1)}, u32[]{:S(2)}, u32[]{:S(2)}) collective-permute-start(bf16[1728,128]{1,0:T(8,128)(2,1)S(1)} %get-tuple-element.10.rest_0_), channel_id=1, source_target_pairs={{0,1},{2,3},{1,0},{3,2},{4,5},{6,7},{5,4},{7,6},{8,9},{10,11},{9,8... | collective-permute-start | bytes 1327112 | tf_op jit(solution)/shard_map/ppermute | solution.py:334
  12.4 16.0 %collective-permute-start.8 = (bf16[1536,128]{1,0:T(8,128)(2,1)S(1)}, bf16[1536,128]{1,0:T(8,128)(2,1)S(1)}, u32[]{:S(2)}, u32[]{:S(2)}) collective-permute-start(bf16[1536,128]{1,0:T(8,128)(2,1)S(1)} %get-tuple-element.12.rest_0_), channel_id=1, source_target_pairs={{1,2},{2,1},{5,6},{6,5},{9,10},{10,9},{13,14},{14,13},{17,18},{18,... | collective-permute-start | bytes 1179656 | tf_op jit(solution)/shard_map/ppermute | solution.py:334
  13.1 18.8 %collective-permute-start.5 = (bf16[1536,128]{1,0:T(8,128)(2,1)S(1)}, bf16[1536,128]{1,0:T(8,128)(2,1)S(1)}, u32[]{:S(2)}, u32[]{:S(2)}) collective-permute-start(bf16[1536,128]{1,0:T(8,128)(2,1)S(1)} %get-tuple-element.12.rest_0_), channel_id=1, source_target_pairs={{0,1},{2,3},{1,0},{3,2},{4,5},{6,7},{5,4},{7,6},{8,9},{10,11},{9,8... | collective-permute-start | bytes 1179656 | tf_op jit(solution)/shard_map/ppermute | solution.py:334
  14.9 26.5 %collective-permute-start.2 = (bf16[1728,128]{1,0:T(8,128)(2,1)S(1)}, bf16[1728,128]{1,0:T(8,128)(2,1)S(1)}, u32[]{:S(2)}, u32[]{:S(2)}) collective-permute-start(bf16[1728,128]{1,0:T(8,128)(2,1)S(1)} %collective-permute-done.1.rest_2_), channel_id=1, source_target_pairs={{2,3},{1,0},{6,7},{5,4},{10,11},{9,8},{14,15},{13,12},{18,19},{17,... | collective-permute-start | bytes 1327112 | tf_op jit(solution)/shard_map/ppermute | solution.py:334
  23.5 9.8 %collective-permute-start.3 = (bf16[1728,128]{1,0:T(8,128)(2,1)S(1)}, bf16[1728,128]{1,0:T(8,128)(2,1)S(1)}, u32[]{:S(2)}, u32[]{:S(2)}) collective-permute-start(bf16[1728,128]{1,0:T(8,128)(2,1)S(1)} %collective-permute-done.rest_1_), channel_id=1, source_target_pairs={{1,2},{2,1},{5,6},{6,5},{9,10},{10,9},{13,14},{14,13},{17,18},{18,... | collective-permute-start | bytes 1327112 | tf_op jit(solution)/shard_map/ppermute | solution.py:334
  28.4 44.6 %collective-permute-start.9 = (bf16[1536,128]{1,0:T(8,128)(2,1)S(1)}, bf16[1536,128]{1,0:T(8,128)(2,1)}, u32[]{:S(2)}, u32[]{:S(2)}) collective-permute-start(bf16[1536,128]{1,0:T(8,128)(2,1)S(1)} %collective-permute-done.8.rest_2_), channel_id=1, source_target_pairs={{2,3},{1,0},{6,7},{5,4},{10,11},{9,8},{14,15},{13,12},{18,19},{17,... | collective-permute-start | bytes 1179656 | tf_op jit(solution)/shard_map/ppermute | solution.py:334
  31.9 39.8 %collective-permute-start.6 = (bf16[1536,128]{1,0:T(8,128)(2,1)S(1)}, bf16[1536,128]{1,0:T(8,128)(2,1)}, u32[]{:S(2)}, u32[]{:S(2)}) collective-permute-start(bf16[1536,128]{1,0:T(8,128)(2,1)S(1)} %collective-permute-done.5.rest_1_), channel_id=1, source_target_pairs={{1,2},{2,1},{5,6},{6,5},{9,10},{10,9},{13,14},{14,13},{17,18},{18,... | collective-permute-start | bytes 1179656 | tf_op jit(solution)/shard_map/ppermute | solution.py:334
  33.3 24.8 %collective-permute-start.4 = (bf16[1728,128]{1,0:T(8,128)(2,1)S(1)}, bf16[1728,128]{1,0:T(8,128)(2,1)S(1)}, u32[]{:S(2)}, u32[]{:S(2)}) collective-permute-start(bf16[1728,128]{1,0:T(8,128)(2,1)S(1)} %collective-permute-done.3.rest_4_), channel_id=1, source_target_pairs={{2,3},{1,0},{6,7},{5,4},{10,11},{9,8},{14,15},{13,12},{18,19},{17,... | collective-permute-start | bytes 1327112 | tf_op jit(solution)/shard_map/ppermute | solution.py:334
  67.4 0.7 copy-start.7
  68.1 25.1 %all-to-all-start = ((bf16[8,48,1536]{2,1,0:T(8,128)(2,1)}), bf16[8,48,1536]{2,1,0:T(8,128)(2,1)S(1)}, u32[]{:S(2)}, u32[]{:S(2)}) async-start(bf16[8,48,1536]{2,1,0:T(8,128)(2,1)} %bitcast.5), calls=%async_computation | async-start | bytes 2359296 | tf_op jit(solution)/shard_map/all_to_all | solution.py:378
  71.7 15.2 %collective-permute-start.7 = (bf16[1536,128]{1,0:T(8,128)(2,1)}, bf16[1536,128]{1,0:T(8,128)(2,1)S(1)}, u32[]{:S(2)}, u32[]{:S(2)}) collective-permute-start(bf16[1536,128]{1,0:T(8,128)(2,1)} %collective-permute-done.6.rest_4_), channel_id=1, source_target_pairs={{2,3},{1,0},{6,7},{5,4},{10,11},{9,8},{14,15},{13,12},{18,19},{17,... | collective-permute-start | bytes 1179656 | tf_op jit(solution)/shard_map/ppermute | solution.py:334
  73.0 0.9 copy-start.8
  93.2 21.0 %all-to-all-start.1 = ((bf16[8,48,1536]{2,1,0:T(8,128)(2,1)}), bf16[8,48,1536]{2,1,0:T(8,128)(2,1)S(1)}, u32[]{:S(2)}, u32[]{:S(2)}) async-start(bf16[8,48,1536]{2,1,0:T(8,128)(2,1)} %bitcast.6), calls=%async_computation.1 | async-start | bytes 2359296 | tf_op jit(solution)/shard_map/all_to_all | solution.py:378
  98.2 2.2 %copy-start = (f32[9216,128]{1,0:T(8,128)}, f32[9216,128]{1,0:T(8,128)S(1)}, u32[]{:S(2)}) copy-start(f32[9216,128]{1,0:T(8,128)S(1)} %collect.1.early) | copy-start | bytes 14155780
  114.2 2.3 %copy-start.1 = (f32[9216,128]{1,0:T(8,128)S(1)}, f32[9216,128]{1,0:T(8,128)}, u32[]{:S(2)}) copy-start(f32[9216,128]{1,0:T(8,128)} %copy-done) | copy-start | bytes 14155780
  116.5 5.0 %copy-start.2 = (bf16[48,192,768]{2,1,0:T(8,128)(2,1)S(1)}, bf16[48,192,768]{2,1,0:T(8,128)(2,1)}, u32[]{:S(2)}) copy-start(bf16[48,192,768]{2,1,0:T(8,128)(2,1)} %legendre.1) | copy-start | bytes 42467332

commit v3 on v2

--- a/solution.py
+++ b/solution.py
@@ -3,6 +3,7 @@
 
 import jax
 import jax.numpy as jnp
+import numpy as np
 from jax import lax
 from jax.experimental import pallas as pl
 from jax.experimental.pallas import tpu as pltpu
@@ -13,6 +14,7 @@
 SLOTS = 3
 LANES = 128
 SPAN = 2 * LANES
+UNROLL = 4
 F32 = jnp.float32
 BF16 = jnp.bfloat16
 
@@ -25,13 +27,29 @@
     return ((jnp.cos(phase_angle) + jnp.sin(phase_angle)) / math.sqrt(lon_total)).astype(BF16)
 
 
+def hartley_constant(waves, lon_total):
+    phase_index = np.arange(waves)[:, None] * np.arange(lon_total)[None, :] % lon_total
+    phase_angle = np.float32(2.0 * math.pi / lon_total) * phase_index.astype(np.float32)
+    table = (np.cos(phase_angle) + np.sin(phase_angle)) / np.float32(math.sqrt(lon_total))
+    return jnp.asarray(table.astype(BF16))
+
+
 def chunk_list(channels):
     half = channels // 2
     return ((0, half), (half, half))
 
 
 def pack_body(chunks, blocks, counts, fields, block, stencil, frac, *rest):
-    outs, wide = rest[:-1], rest[-1]
+    outs, (wide, *held, done) = rest[: len(chunks)], rest[len(chunks) :]
+    copies = [
+        pltpu.make_async_copy(given, kept, done.at[number])
+        for number, (given, kept) in enumerate(zip((counts, fields, block, stencil, frac), held, strict=True))
+    ]
+    for copy in copies:
+        copy.start()
+    for copy in copies:
+        copy.wait()
+    counts, fields, block, stencil, frac = held
     cells = blocks * BLK
     cap = block.shape[1]
     wide[...] = fields[...].astype(F32)
@@ -79,28 +97,30 @@
         outs[0][base + span * 16 : base + (span + 1) * 16, :] = pair.astype(BF16)
 
 
-def interp_body(count, width, blocks, lead, late, reach, here, *rest):
+def interp_body(count, bands, width, blocks, lead, late, far, reach, here, *rest):
     tiles, rest = rest[: len(reach)], rest[len(reach) :]
     if not lead:
         (params, ends), rest = rest[:2], rest[2:]
     if late:
         (given, table), rest = rest[:2], rest[2:]
-        (out, *rest), grid = rest[:-1], rest[-1]
+        outs, rest, (grid, spectra) = rest[:bands], rest[bands:-2], rest[-2:]
     else:
         grid, *rest = rest
     if lead:
-        params, ends, flipped = rest
+        params, ends, flipped, work = rest
     else:
-        (flipped,) = rest
+        flipped, work = rest
     me = here[0]
-    far = count - 1
     groups = LANES // width
     planes = BLK // groups
-    sign = 1 - 2 * lax.rem(me, 2)
-    owners = [me + side * sign * away for away, side in reach]
+    owners = [jnp.bitwise_xor(me, step) for step, _ in reach]
+
+    def distant(other):
+        step = jnp.bitwise_xor(me, other)
+        return functools.reduce(jnp.logical_or, [step == one for one in far], jnp.bool_(False))
 
     def present(number):
-        return (owners[number] >= 0) & (owners[number] < count)
+        return (jnp.abs(me - owners[number]) <= count // 2) == reach[number][1]
 
     def take(tile, owner):
         for plane in range(planes):
@@ -117,7 +137,7 @@
         for tile in range(count):
             ends[tile, 0] = 0
 
-            @pl.when(late | (jnp.abs(me - tile) < far))
+            @pl.when(late | jnp.logical_not(distant(tile)))
             def _(tile=tile):
                 rows = params[tile].astype(F32)
                 which = lax.broadcasted_iota(jnp.int32, rows.shape, 0) % 8 == 7
@@ -137,130 +157,131 @@
         target = lax.rem(owner - index + 1 + count, count)
         if not lead:
             return jnp.bool_(True)
-        distant = jnp.maximum(jnp.abs(target - me), jnp.abs(owner - me)) == far
-        return distant if late else jnp.logical_not(distant)
-
-    def job(owner, index):
-        target = lax.rem(owner - index + 1 + count, count)
-        low = ends[target, index]
-        high = ends[target, index + 1]
-        place = pl.multiple_of(target * LANES, LANES)
-        first = low // SPAN
-        last = jnp.where(high > low, (high + SPAN - 1) // SPAN, first)
-
-        def span_step(span, valid):
-            both = params[target, pl.ds(pl.multiple_of(span * 16, 16), 16), :].astype(F32)
-
-            def line(i):
-                return jnp.concatenate([both[i : i + 1, :], both[8 + i : 9 + i, :]], axis=1)
-
-            mine = line(7) == jnp.where(valid, index, -1).astype(F32)
-            key = jnp.where(mine, line(0), -1.0)
-            onehot = jnp.where(block_row == key, 1.0, 0.0).astype(BF16)
-            f_lat = (line(5) + 0.5) / FRAC
-            f_lon = (line(6) + 0.5) / FRAC
-            corners = (
-                (1.0 - f_lat) * (1.0 - f_lon),
-                f_lat * (1.0 - f_lon),
-                (1.0 - f_lat) * f_lon,
-                f_lat * f_lon,
+        either = distant(target) | distant(owner)
+        return either if late else jnp.logical_not(either)
+
+    spans = blocks * BLK // SPAN
+    entries = jnp.int32(0)
+    for number, tile in enumerate(tiles):
+        owner = owners[number]
+        asked = [present(number) & wanted(owner, index) for index in range(SLOTS)]
+
+        @pl.when(functools.reduce(jnp.logical_or, asked))
+        def _(tile=tile, owner=owner):
+            take(tile, owner)
+
+        for index in range(SLOTS):
+            target = lax.rem(owner - index + 1 + count, count)
+            target = jnp.where(asked[index], target, 0)
+            low = ends[target, index]
+            high = ends[target, index + 1]
+            first = low // SPAN
+            extra = (high + SPAN - 1) // SPAN - first
+            extra = jnp.where(asked[index] & (high > low), extra, 0)
+            code = ((owner * count + target) * SLOTS + index) * spans + first
+
+            def enter(span, _, code=code, entries=entries):
+                work[entries + span] = code + span
+                return 0
+
+            lax.fori_loop(0, extra, enter, 0)
+            entries = entries + extra
+
+    def entry_step(entry):
+        code = work[jnp.minimum(entry, entries - 1)]
+        span = lax.rem(code, spans)
+        code = code // spans
+        index = jnp.where(entry < entries, lax.rem(code, SLOTS), -1)
+        code = code // SLOTS
+        target, owner = lax.rem(code, count), code // count
+        both = params[target, pl.ds(pl.multiple_of(span * 16, 16), 16), :].astype(F32)
+
+        def line(i):
+            return jnp.concatenate([both[i : i + 1, :], both[8 + i : 9 + i, :]], axis=1)
+
+        key = jnp.where(line(7) == index.astype(F32), line(0), -1.0)
+        onehot = jnp.where(block_row == key, 1.0, 0.0).astype(BF16)
+        f_lat = (line(5) + 0.5) / FRAC
+        f_lon = (line(6) + 0.5) / FRAC
+        corners = (
+            (1.0 - f_lat) * (1.0 - f_lon),
+            f_lat * (1.0 - f_lon),
+            (1.0 - f_lat) * f_lon,
+            f_lat * f_lon,
+        )
+        weight = jnp.zeros((BLK, SPAN), F32)
+        for corner in range(4):
+            weight += jnp.where(cell_row == line(1 + corner), corners[corner], 0.0)
+        total = jnp.zeros((width, SPAN), F32)
+        for plane in range(planes):
+            picked = jnp.dot(
+                flipped[owner, plane * LANES : (plane + 1) * LANES, :],
+                onehot,
+                preferred_element_type=F32,
             )
-            weight = jnp.zeros((BLK, SPAN), F32)
-            for corner in range(4):
-                weight += jnp.where(cell_row == line(1 + corner), corners[corner], 0.0)
-            picked = jnp.dot(flipped[owner], onehot, preferred_element_type=F32)
-            total = jnp.zeros((width, SPAN), F32)
-            for cell in range(BLK):
-                start = cell % planes * LANES + cell // planes * width
-                total += weight[cell : cell + 1, :] * picked[start : start + width, :]
-            return total.astype(BF16)
-
-        def add(span, total):
+            for group in range(groups):
+                cell = group * planes + plane
+                total += (
+                    weight[cell : cell + 1, :] * picked[group * width : (group + 1) * width, :]
+                )
+        return span, pl.multiple_of(target * LANES, LANES), total.astype(BF16)
+
+    def step(number, _):
+        found = [entry_step(number * UNROLL + inner) for inner in range(UNROLL)]
+        for span, place, total in found:
             for half in range(2):
                 rows = pl.ds(pl.multiple_of((2 * span + half) * width, width), width)
                 grid[rows, pl.ds(place, LANES)] += total[:, half * LANES : (half + 1) * LANES]
-
-        def pair_step(pair, _):
-            one = first + 2 * pair
-            two = jnp.minimum(one + 1, last - 1)
-            total_one = span_step(one, True)
-            total_two = span_step(two, one + 1 < last)
-            add(one, total_one)
-            add(two, total_two)
-            return 0
-
-        lax.fori_loop(0, (last - first + 1) // 2, pair_step, 0)
-
-    for number, tile in enumerate(tiles):
-        owner = owners[number]
-        needed = present(number)
-        if lead and late:
-            asked = [wanted(owner, index) for index in range(SLOTS)]
-            needed = needed & functools.reduce(jnp.logical_or, asked)
-
-        @pl.when(needed)
-        def _(tile=tile, owner=owner):
-            take(tile, owner)
-
-            def each(index, _):
-                @pl.when(wanted(owner, index))
-                def _():
-                    job(owner, index)
-
-                return 0
-
-            lax.fori_loop(0, SLOTS, each, 0)
+        return 0
+
+    lax.fori_loop(0, (entries + UNROLL - 1) // UNROLL, step, 0)
 
     if late:
-        out[...] = lax.dot_general(
+        spectra[...] = lax.dot_general(
             table[...], grid[...], (((1,), (1,)), ((), ())), preferred_element_type=F32
         ).astype(BF16)
-
-
-def collect_body(chunks, lat_rows, *rest):
-    parts, gathered = rest[:-1], rest[-1]
-    bands, waves, _ = parts[0].shape
+        waves = outs[0].shape[0]
+        for shift, out in enumerate(outs):
+            start = pl.multiple_of(jnp.bitwise_xor(here[1], shift) * waves, 16)
+            out[...] = spectra[pl.ds(start, waves), :]
+
+
+def spread_rows(piece, row, first, width):
+    groups = LANES // width
+    tile, group = row // groups, row % groups
+    values = piece[:, tile * LANES : (tile + 1) * LANES].astype(F32)
+    turn = (first - group * width) % LANES
+    return pltpu.roll(values, turn, 1) if turn else values
+
+
+def collect_body(chunks, bands, lat_rows, here, *rest):
+    pieces, gathered = rest[:-1], rest[-1]
+    waves = pieces[0].shape[0]
     lane = lax.broadcasted_iota(jnp.int32, (waves, LANES), 1)
-
-    def collect(source, _):
+    for shift in range(bands):
+        source = jnp.bitwise_xor(here[1], shift)
         for row in range(lat_rows):
             total = None
-            for part, (first, width) in zip(parts, chunks, strict=True):
-                groups = LANES // width
-                tile, group = row // groups, row % groups
-                values = part[source, :, tile * LANES : (tile + 1) * LANES].astype(F32)
-                turn = (first - group * width) % LANES
-                if turn:
-                    values = pltpu.roll(values, turn, 1)
+            for part, (first, width) in enumerate(chunks):
+                values = spread_rows(pieces[part * bands + shift], row, first, width)
                 total = values if total is None else jnp.where(lane >= first, values, total)
             start = pl.multiple_of((source * lat_rows + row) * waves, 8)
             gathered[pl.ds(start, waves), :] = total
-        return 0
-
-    lax.fori_loop(0, bands, collect, 0)
-
-
-def final_body(last, lat_rows, per_step, legendre, early, part, out, gathered, factor, staged, done):
+
+
+def final_body(last, bands, lat_rows, per_step, here, legendre, early, *rest):
+    pieces, (out, gathered, factor, staged, done) = rest[:bands], rest[bands:]
     waves, lat_total, degrees = legendre.shape
-    bands = part.shape[0]
     first, width = last
     degree = lax.broadcasted_iota(jnp.int32, factor.shape, 0).astype(F32)
     factor[...] = 1.0 / (1.0 + 4.0 * degree * (degree + 1.0) / (degrees * (degrees + 1)))
     lane = lax.broadcasted_iota(jnp.int32, (waves, LANES), 1)
-    groups = LANES // width
-
-    def collect(source, _):
+    for shift in range(bands):
+        source = jnp.bitwise_xor(here[1], shift)
         for row in range(lat_rows):
-            tile, group = row // groups, row % groups
-            values = part[source, :, tile * LANES : (tile + 1) * LANES].astype(F32)
-            turn = (first - group * width) % LANES
-            if turn:
-                values = pltpu.roll(values, turn, 1)
+            values = spread_rows(pieces[shift], row, first, width)
             rows = pl.ds(pl.multiple_of((source * lat_rows + row) * waves, 8), waves)
             gathered[rows, :] = jnp.where(lane >= first, values, early[rows, :])
-        return 0
-
-    lax.fori_loop(0, bands, collect, 0)
 
     def step(number, _):
         for inner in range(per_step):
@@ -301,9 +322,9 @@
     sector_waves = waves * bands
     chunks = chunk_list(channels)
     me = lax.axis_index("lon")
-    here = jnp.full((1,), me, jnp.int32)
-
-    table = hartley_table(sector_waves * count, lon_total)
+    here = jnp.stack([me, lax.axis_index("lat")]).astype(jnp.int32)
+
+    table = hartley_constant(sector_waves * count, lon_total)
     table = lax.dynamic_slice_in_dim(table, me * sector_waves, sector_waves, axis=0)
 
     tile_rows = [blocks * BLK * width // LANES for _, width in chunks]
@@ -311,38 +332,51 @@
     packed = pl.pallas_call(
         functools.partial(pack_body, chunks, blocks),
         out_shape=[jax.ShapeDtypeStruct((rows, LANES), BF16) for rows in tile_rows],
-        in_specs=[SMEM, VMEM, VMEM, VMEM, VMEM],
+        in_specs=[pl.BlockSpec(memory_space=pltpu.HBM)] * 5,
         out_specs=[VMEM] * len(tile_rows),
-        scratch_shapes=[pltpu.VMEM((cells, channels), F32)],
-        compiler_params=limit(16),
+        scratch_shapes=[
+            pltpu.VMEM((cells, channels), F32),
+            pltpu.SMEM(req_count.shape[2:], jnp.int32),
+            pltpu.VMEM((cells, channels), BF16),
+            pltpu.VMEM(req_block.shape[2:], jnp.int32),
+            pltpu.VMEM(req_stencil.shape[2:], jnp.int32),
+            pltpu.VMEM(req_frac.shape[2:], jnp.int32),
+            pltpu.SemaphoreType.DMA((5,)),
+        ],
+        compiler_params=limit(48),
         name="pack",
     )(req_count[0, 0], fields.reshape(cells, channels), req_block[0, 0], req_stencil[0, 0], req_frac[0, 0])
 
-    def links(parity, away):
-        up = [(i, i + 1) for i in range(parity, count - 1, 2) if i - away + 1 >= 0]
-        down = [(i + 1, i) for i in range(parity, count - 1, 2) if i + away < count]
-        return up + down
-
-    held = [[(packed[number], 0, 1)] for number in range(len(chunks))]
-    edge = [(tile, tile) for tile in packed]
-    for away in range(1, count):
-        for number in range(len(chunks)):
-            even, odd = edge[number]
-            both = []
-            for parity, tile, side in ((0, odd, 1), (1, even, -1)):
-                pairs = links(parity, away)
-                both.append(lax.ppermute(tile, "lon", pairs) if pairs else None)
-                if pairs:
-                    held[number].append((both[-1], away, side))
-            edge[number] = tuple(both)
-
+    near = [(i, i ^ step) for step in range(count) for i in range(count) if abs(i - (i ^ step)) <= count // 2]
+
+    def after(tile, others):
+        return lax.optimization_barrier((tile, *others))[0] if others else tile
+
+    def exchange(tile, step, others=()):
+        return lax.ppermute(after(tile, others), "lon", [pair for pair in near if pair[0] ^ pair[1] == step])
+
+    def relay(tile, step):
+        pairs = [(i ^ 1, i) for i in range(count) if (i, i ^ step) not in near]
+        return lax.ppermute(tile, "lon", pairs)
+
+    far = [step for step in range(count) if any((i, i ^ step) not in near for i in range(count))]
     parts = []
     params = ends = None
+    ahead = moved = ()
     for number, (first, width) in enumerate(chunks):
         lead = number == 0
-        soon = [one for one in held[number] if one[1] < count - 1]
-        last = held[number] if lead else [one for one in held[number] if one[1] == count - 1]
-        flipped = pltpu.VMEM((count, BLK * width, blocks), BF16)
+        tile = packed[number]
+        near_tiles = {step: exchange(tile, step, ahead) for step in range(1, count) if step not in far}
+        ahead = tuple(near_tiles.values())
+        far_tiles = [(exchange(tile, step, ahead), step, True) for step in far]
+        passed = [relay(near_tiles[step ^ 1], step) for step in far]
+        far_tiles += [(got, step, False) for got, step in zip(passed, far, strict=True)]
+        soon = [(tile, 0, True)] + [(got, step, True) for step, got in near_tiles.items()]
+        last = soon + far_tiles if lead else far_tiles
+        scratch = [
+            pltpu.VMEM((count, BLK * width, blocks), BF16),
+            pltpu.SMEM((count * SLOTS * (cells // SPAN + 1),), jnp.int32),
+        ]
         grid = jax.ShapeDtypeStruct((lat_rows * width, lon_total), BF16)
         listed = [
             jax.ShapeDtypeStruct((count, cells // LANES * 8, LANES), BF16),
@@ -352,46 +386,56 @@
         given_specs = [] if lead else [VMEM, SMEM]
         kept = [pltpu.VMEM(listed[0].shape, BF16), pltpu.SMEM(listed[1].shape, jnp.int32)]
         grid = pl.pallas_call(
-            functools.partial(interp_body, count, width, blocks, lead, False, [one[1:] for one in soon]),
+            functools.partial(interp_body, count, bands, width, blocks, lead, False, far, [one[1:] for one in soon]),
             out_shape=grid,
             in_specs=[SMEM] + [VMEM] * len(soon) + given_specs,
             out_specs=VMEM,
-            scratch_shapes=(kept if lead else []) + [flipped],
+            scratch_shapes=(kept if lead else []) + scratch,
             compiler_params=limit(24),
-            cost_estimate=cost(width * 10**8),
+            cost_estimate=cost(width * 10**9),
             name="early",
         )(here, *[one[0] for one in soon], *given)
-        fourier, *found = pl.pallas_call(
-            functools.partial(interp_body, count, width, blocks, lead, True, [one[1:] for one in last]),
-            out_shape=[jax.ShapeDtypeStruct((sector_waves, lat_rows * width), BF16)]
+        ahead = (grid, *[got for got, _, _ in far_tiles])
+        grid = after(grid, moved)
+        results = pl.pallas_call(
+            functools.partial(interp_body, count, bands, width, blocks, lead, True, far, [one[1:] for one in last]),
+            out_shape=[jax.ShapeDtypeStruct((waves, lat_rows * width), BF16)] * bands
             + (listed if lead else []),
             in_specs=[SMEM] + [VMEM] * len(last) + given_specs + [VMEM, VMEM],
-            out_specs=[VMEM] + ([VMEM, SMEM] if lead else []),
-            scratch_shapes=[flipped, pltpu.VMEM(grid.shape, BF16)],
+            out_specs=[VMEM] * bands + ([VMEM, SMEM] if lead else []),
+            scratch_shapes=scratch
+            + [
+                pltpu.VMEM(grid.shape, BF16),
+                pltpu.VMEM((sector_waves, lat_rows * width), BF16),
+            ],
             compiler_params=limit(24),
             cost_estimate=cost(width * 5 * 10**7),
             name="late",
         )(here, *[one[0] for one in last], *given, grid, table)
         if lead:
-            params, ends = found
-        fourier = fourier.reshape(bands, waves, lat_rows * width)
-        parts.append(lax.all_to_all(fourier, "lat", split_axis=0, concat_axis=0, tiled=True))
+            params, ends = results[bands:]
+        pieces = [results[0]]
+        for shift in range(1, bands):
+            pieces.append(lax.ppermute(results[shift], "lat", [(i, i ^ shift) for i in range(bands)]))
+        parts.append(pieces)
+        moved = pieces[2:6]
 
     gathered = jax.ShapeDtypeStruct((lat_total * waves, channels), F32)
+    early = [piece for pieces in parts[:-1] for piece in pieces]
     early = pl.pallas_call(
-        functools.partial(collect_body, chunks[:-1], lat_rows),
+        functools.partial(collect_body, chunks[:-1], bands, lat_rows),
         out_shape=gathered,
-        in_specs=[VMEM] * (len(chunks) - 1),
+        in_specs=[SMEM] + [VMEM] * len(early),
         out_specs=VMEM,
         compiler_params=limit(16),
         cost_estimate=cost(10**9),
         name="collect",
-    )(*parts[:-1])
+    )(here, *early)
     per_step = math.gcd(waves, 8)
     return pl.pallas_call(
-        functools.partial(final_body, chunks[-1], lat_rows, per_step),
+        functools.partial(final_body, chunks[-1], bands, lat_rows, per_step),
         out_shape=jax.ShapeDtypeStruct((waves, degrees, channels), F32),
-        in_specs=[VMEM] * 3,
+        in_specs=[SMEM] + [VMEM] * (bands + 2),
         out_specs=ANY,
         scratch_shapes=[
             pltpu.VMEM(gathered.shape, F32),
@@ -401,7 +445,7 @@
         ],
         compiler_params=limit(28),
         name="final",
-    )(legendre, early, parts[-1])
+    )(here, legendre, early, *parts[-1])
 
 
 def padded(cells, sides, width):
@@ -485,7 +529,10 @@
     count = lax.axis_size("lon")
     lon_cols = fields.shape[1]
     sector_waves = legendre.shape[0] * lax.axis_size("lat")
-    plan = gathering if count * lon_cols <= lon_cols + sector_waves else exchanging
+    bands = lax.axis_size("lat")
+    fits = count * lon_cols <= lon_cols + sector_waves
+    fits = fits and bands & (bands - 1) == 0 and count & (count - 1) == 0
+    plan = gathering if fits else exchanging
     return plan(fields, req_block, req_stencil, req_frac, req_count, legendre)
 
 

time: 132 us -> 112 us (0.85)
  local copies, waits for them, and re-layouts: 15.2 us -> 5.13 us
  Pallas kernels: 50.2 us -> 42.4 us
  other arithmetic: 4.24 us -> 0.08 us
  starting transfers between devices: 24 us -> 26.4 us
    all_to_all x2 -> x0, waiting for transfers between devices: 13.8 us -> none  [gathering(): lax.all_to_all(fourier, 'lat', split_axis=0, concat_axis=0, tiled=True)]
    ppermute x10 -> x22, waiting for transfers between devices: 23 us -> 36.7 us  [the longest x6 22.1 us: exchange(): lax.ppermute(after(tile, others), 'lon', [pair for pair in near if pair[0...]
    unnamed x19 -> x17, local copies, waits for them, and re-layouts: 15.2 us -> 4.11 us
    ppermute x10 -> x22, starting transfers between devices: 16.2 us -> 26.4 us  [the longest x14 12.5 us: gathering(): lax.ppermute(results[shift], 'lat', [(i, i ^ shift) for i in range(bands)])]
    pallas_call x6, Pallas kernels: 48.5 us -> 40.7 us  [the longest x4 30.2 us: gathering(): pl.pallas_call(functools.partial(interp_body, count, bands, width, blocks...]
    all_to_all x2 -> x0, starting transfers between devices: 7.75 us -> none  [gathering(): lax.all_to_all(fourier, 'lat', split_axis=0, concat_axis=0, tiled=True)]
    convert_element_type x1 -> x0, other arithmetic: 2.92 us -> none  [hartley_table(): ((jnp.cos(phase_angle) + jnp.sin(phase_angle)) / math.sqrt(lon_total)).as...]
    select_n x1 -> x0, other arithmetic: 1.32 us -> none  [hartley_table(): phase_index = wave_index[:, None] * lon_index[None, :] % lon_total]
  transfers between devices with their start and end apart: 12 -> 22, of which waited for: 5 -> 8; matrix products, arithmetic and copies ran while one was open for 3% -> 1% of each run, Pallas kernels for 30% -> 28%
where the time goes in v3:
time: 112 us; the launch traced here: 111 us
  Pallas kernels  42.4 us (38%)
  waiting for transfers between devices  36.7 us (33%)
  starting transfers between devices  26.4 us (24%)
  local copies, waits for them, and re-layouts  5.13 us (5%)
    pallas_call x4, Pallas kernels, gathering(): pl.pallas_call(functools.partial(interp_body, count, bands, width, blocks...  30.2 us
    ppermute x6, waiting for transfers between devices, exchange(): lax.ppermute(after(tile, others), 'lon', [pair for pair in near if pair[0...  22.1 us
    ppermute x14, starting transfers between devices, gathering(): lax.ppermute(results[shift], 'lat', [(i, i ^ shift) for i in range(bands)])  12.5 us
    ppermute x6, starting transfers between devices, exchange(): lax.ppermute(after(tile, others), 'lon', [pair for pair in near if pair[0...  11.3 us
    ppermute x14, waiting for transfers between devices, gathering(): lax.ppermute(results[shift], 'lat', [(i, i ^ shift) for i in range(bands)])  10.8 us
    pallas_call x1, Pallas kernels, gathering(): pl.pallas_call(functools.partial(final_body, chunks[-1], bands, lat_rows,...  9.43 us
    unnamed x17, local copies, waits for them, and re-layouts  4.11 us
    ppermute x2, waiting for transfers between devices, relay(): return lax.ppermute(tile, 'lon', pairs)  3.83 us
  transfers between devices with their start and end apart: 22, of which 8 were waited for; matrix products, arithmetic and copies ran while one was open for 1% of the time, Pallas kernels for 28%

profile of v3, /device:TPU:0, one launch (start us, length us, event | category | flops | bytes accessed | tf_op | source)
XLA Modules:
  0.0 111.1 jit_solution(434951286302601492)
XLA Ops:
  0.0 0.7 copy.10
  0.7 1.1 %copy-done = bf16[24,128,128]{2,1,0:T(8,128)(2,1)S(1)} copy-done((bf16[24,128,128]{2,1,0:T(8,128)(2,1)S(1)}, bf16[24,128,128]{2,1,0:T(8,128)(2,1)}, u32[]{:S(2)}) %copy-start) | copy-done | bytes 786456
  1.9 0.8 copy-done.1
  2.7 0.8 copy-done.2
  3.4 0.7 copy-done.3
  4.1 1.8 %pack.1 = (bf16[1728,128]{1,0:T(8,128)(2,1)S(1)}, bf16[1536,128]{1,0:T(8,128)(2,1)S(1)}) custom-call(s32[3]{0:T(128)S(1)} %bitcast.15, bf16[3072,128]{1,0:T(8,128)(2,1)S(1)} %bitcast.11, s32[3,1280]{1,0:T(4,128)S(1)} %bitcast.12, s32[3,4,1280]{2,1,0:T(4,128)S(1)} %bitcast.13, s32[3,2,1280]{2,1,0:T(2,128)S(1)} %bitcast.14), custom_call_target="tpu_custom_call" | custom-call | tf_op jit(solution)/shard_map/pack/pallas_call | solution.py:332
  5.9 4.1 %collective-permute-start.1 = (bf16[1728,128]{1,0:T(8,128)(2,1)S(1)}, bf16[1728,128]{1,0:T(8,128)(2,1)S(1)}, u32[]{:S(2)}, u32[]{:S(2)}) collective-permute-start(bf16[1728,128]{1,0:T(8,128)(2,1)S(1)} %get-tuple-element.30.rest_0_), channel_id=1, source_target_pairs={{0,2},{1,3},{2,0},{3,1},{4,6},{5,7},{6,4},{7,5},{8,10},{9,11},{10,... | collective-permute-start | bytes 1327112 | tf_op jit(solution)/shard_map/ppermute | solution.py:356
  10.0 1.6 %collective-permute-start = (bf16[1728,128]{1,0:T(8,128)(2,1)S(1)}, bf16[1728,128]{1,0:T(8,128)(2,1)S(1)}, u32[]{:S(2)}, u32[]{:S(2)}) collective-permute-start(bf16[1728,128]{1,0:T(8,128)(2,1)S(1)} %get-tuple-element.30.rest_0_), channel_id=1, source_target_pairs={{0,1},{1,0},{2,3},{3,2},{4,5},{5,4},{6,7},{7,6},{8,9},{9,8},{10,11... | collective-permute-start | bytes 1327112 | tf_op jit(solution)/shard_map/ppermute | solution.py:356
  11.6 0.1 pad_add_fusion.here
  11.7 1.0 constant_dynamic-slice_fusion.rest_6_.rest_5_
  12.7 17.1 %collective-permute-done.1.rest_2_ = bf16[1728,128]{1,0:T(8,128)(2,1)S(1)} collective-permute-done((bf16[1728,128]{1,0:T(8,128)(2,1)S(1)}, bf16[1728,128]{1,0:T(8,128)(2,1)S(1)}, u32[]{:S(2)}, u32[]{:S(2)}) %collective-permute-start.1) | collective-permute-done | bytes 442400 | tf_op jit(solution)/shard_map/ppermute | solution.py:356
  29.8 0.2 collective-permute-done.rest_1_
  29.9 0.7 collective-permute-start.2
  30.6 1.3 %collective-permute-start.3 = (bf16[1728,128]{1,0:T(8,128)(2,1)S(1)}, bf16[1728,128]{1,0:T(8,128)(2,1)S(1)}, u32[]{:S(2)}, u32[]{:S(2)}) collective-permute-start(bf16[1728,128]{1,0:T(8,128)(2,1)S(1)} %collective-permute-done.1.rest_2_), channel_id=1, source_target_pairs={{1,0},{2,3},{5,4},{6,7},{9,8},{10,11},{13,12},{14,15},{17,16},{18,... | collective-permute-start | bytes 1327112 | tf_op jit(solution)/shard_map/ppermute | solution.py:360
  31.9 8.4 %early.2.rest_5_ = bf16[1536,512]{1,0:T(8,128)(2,1)S(1)} custom-call(s32[2]{0:T(128)S(1)} %pad_add_fusion.here, bf16[1728,128]{1,0:T(8,128)(2,1)S(1)} %get-tuple-element.30.rest_0_, bf16[1728,128]{1,0:T(8,128)(2,1)S(1)} %collective-permute-done.rest_1_, bf16[1728,128]{1,0:T(8,128)(2,1)S(1)} %collective-permute-done.1.rest_2_), custom_call_target="tpu_custom_call" | custom-call | flops 64000000000 | bytes 1000000 | tf_op jit(solution)/shard_map/early/pallas_call | solution.py:388
  40.3 3.8 %collective-permute-done.3.rest_4_ = bf16[1728,128]{1,0:T(8,128)(2,1)S(1)} collective-permute-done((bf16[1728,128]{1,0:T(8,128)(2,1)S(1)}, bf16[1728,128]{1,0:T(8,128)(2,1)S(1)}, u32[]{:S(2)}, u32[]{:S(2)}) %collective-permute-start.3) | collective-permute-done | bytes 442400 | tf_op jit(solution)/shard_map/ppermute | solution.py:360
  44.1 0.0 collective-permute-done.2.rest_3_
  44.1 1.8 %collective-permute-start.12 = (bf16[1536,128]{1,0:T(8,128)(2,1)S(1)}, bf16[1536,128]{1,0:T(8,128)(2,1)S(1)}, u32[]{:S(2)}, u32[]{:S(2)}) collective-permute-start(bf16[1536,128]{1,0:T(8,128)(2,1)S(1)} %get-tuple-element.41.rest_0_), channel_id=1, source_target_pairs={{0,2},{1,3},{2,0},{3,1},{4,6},{5,7},{6,4},{7,5},{8,10},{9,11},{10,... | collective-permute-start | bytes 1179656 | tf_op jit(solution)/shard_map/ppermute | solution.py:356
  45.9 2.5 %collective-permute-start.11 = (bf16[1536,128]{1,0:T(8,128)(2,1)S(1)}, bf16[1536,128]{1,0:T(8,128)(2,1)S(1)}, u32[]{:S(2)}, u32[]{:S(2)}) collective-permute-start(bf16[1536,128]{1,0:T(8,128)(2,1)S(1)} %get-tuple-element.41.rest_0_), channel_id=1, source_target_pairs={{0,1},{1,0},{2,3},{3,2},{4,5},{5,4},{6,7},{7,6},{8,9},{9,8},{10,11... | collective-permute-start | bytes 1179656 | tf_op jit(solution)/shard_map/ppermute | solution.py:356
  48.4 7.4 %late.2 = (bf16[48,1536]{1,0:T(8,128)(2,1)S(1)}, bf16[48,1536]{1,0:T(8,128)(2,1)S(1)}, bf16[48,1536]{1,0:T(8,128)(2,1)S(1)}, bf16[48,1536]{1,0:T(8,128)(2,1)S(1)...) custom-call(s32[2]{0:T(128)S(1)} %pad_add_fusion.here, ...), custom_call_target="tpu_custom_call" | custom-call | flops 3200000000 | bytes 1000000 | tf_op jit(solution)/shard_map/late/pallas_call | solution.py:400
  55.9 0.8 collective-permute-start.5
  56.6 0.0 collective-permute-start.6
  56.6 1.5 %collective-permute-start.7 = (bf16[48,1536]{1,0:T(8,128)(2,1)S(1)}, bf16[48,1536]{1,0:T(8,128)(2,1)S(1)}, u32[]{:S(2)}, u32[]{:S(2)}) collective-permute-start(bf16[48,1536]{1,0:T(8,128)(2,1)S(1)} %get-tuple-element.35), channel_id=1, source_target_pairs={{0,16},{4,20},{8,24},{12,28},{16,0},{20,4},{24,8},{28,12},{1,17},{... | collective-permute-start | bytes 442376 | tf_op jit(solution)/shard_map/ppermute | solution.py:419
  58.2 4.8 %collective-permute-done.12.rest_2_ = bf16[1536,128]{1,0:T(8,128)(2,1)S(1)} collective-permute-done((bf16[1536,128]{1,0:T(8,128)(2,1)S(1)}, bf16[1536,128]{1,0:T(8,128)(2,1)S(1)}, u32[]{:S(2)}, u32[]{:S(2)}) %collective-permute-start.12) | collective-permute-done | bytes 393248 | tf_op jit(solution)/shard_map/ppermute | solution.py:356
  62.9 0.0 collective-permute-start.8
  62.9 0.1 collective-permute-done.11.rest_1_
  63.0 0.7 collective-permute-start.13
  63.7 1.3 %collective-permute-start.14 = (bf16[1536,128]{1,0:T(8,128)(2,1)S(1)}, bf16[1536,128]{1,0:T(8,128)(2,1)S(1)}, u32[]{:S(2)}, u32[]{:S(2)}) collective-permute-start(bf16[1536,128]{1,0:T(8,128)(2,1)S(1)} %collective-permute-done.12.rest_2_), channel_id=1, source_target_pairs={{1,0},{2,3},{5,4},{6,7},{9,8},{10,11},{13,12},{14,15},{17,16},{18,... | collective-permute-start | bytes 1179656 | tf_op jit(solution)/shard_map/ppermute | solution.py:360
  65.0 0.0 slice-start.1
  65.0 0.0 slice-start.2
  65.0 0.0 slice-start.3
  65.0 9.3 %early.3.rest_4_ = bf16[1536,512]{1,0:T(8,128)(2,1)S(1)} custom-call(s32[2]{0:T(128)S(1)} %pad_add_fusion.here, bf16[1536,128]{1,0:T(8,128)(2,1)S(1)} %get-tuple-element.41.rest_0_, bf16[1536,128]{1,0:T(8,128)(2,1)S(1)} %collective-permute-done.11.rest_1_, bf16[1536,128]{1,0:T(8,128)(2,1)S(1)} %collective-permute-done.12.rest_2_, ...), custom_call_target="tpu_custom_call" | custom-call | flops 64000000000 | bytes 1000000 | tf_op jit(solution)/shard_map/early/pallas_call | solution.py:388
  74.3 0.0 collective-permute-done.6.rest_3_
  74.3 1.6 %collective-permute-start.4 = (bf16[48,1536]{1,0:T(8,128)(2,1)S(1)}, bf16[48,1536]{1,0:T(8,128)(2,1)S(1)}, u32[]{:S(2)}, u32[]{:S(2)}) collective-permute-start(bf16[48,1536]{1,0:T(8,128)(2,1)S(1)} %get-tuple-element.32), channel_id=1, source_target_pairs={{0,4},{4,0},{8,12},{12,8},{16,20},{20,16},{24,28},{28,24},{1,5},{5... | collective-permute-start | bytes 442376 | tf_op jit(solution)/shard_map/ppermute | solution.py:419
  76.0 1.9 %collective-permute-start.9 = (bf16[48,1536]{1,0:T(8,128)(2,1)S(1)}, bf16[48,1536]{1,0:T(8,128)(2,1)S(1)}, u32[]{:S(2)}, u32[]{:S(2)}) collective-permute-start(bf16[48,1536]{1,0:T(8,128)(2,1)S(1)} %get-tuple-element.37), channel_id=1, source_target_pairs={{0,24},{4,28},{8,16},{12,20},{16,8},{20,12},{24,0},{28,4},{1,25},{... | collective-permute-start | bytes 442376 | tf_op jit(solution)/shard_map/ppermute | solution.py:419
  77.9 0.4 collective-permute-start.10
  78.3 5.2 %late.3 = (bf16[48,1536]{1,0:T(8,128)(2,1)S(1)}, bf16[48,1536]{1,0:T(8,128)(2,1)S(1)}, bf16[48,1536]{1,0:T(8,128)(2,1)S(1)}, bf16[48,1536]{1,0:T(8,128)(2,1)S(1)...) custom-call(s32[2]{0:T(128)S(1)} %pad_add_fusion.here, ...), custom_call_target="tpu_custom_call" | custom-call | flops 3200000000 | bytes 1000000 | tf_op jit(solution)/shard_map/late/pallas_call | solution.py:400
  83.5 0.8 collective-permute-start.15
  84.3 0.8 collective-permute-start.16
  85.2 0.6 collective-permute-start.17
  85.7 1.1 collective-permute-start.18
  86.8 1.0 collective-permute-start.19
  87.8 1.9 %collective-permute-start.20 = (bf16[48,1536]{1,0:T(8,128)(2,1)S(1)}, bf16[48,1536]{1,0:T(8,128)(2,1)S(1)}, u32[]{:S(2)}, u32[]{:S(2)}) collective-permute-start(bf16[48,1536]{1,0:T(8,128)(2,1)S(1)} %get-tuple-element.51), channel_id=1, source_target_pairs={{0,24},{4,28},{8,16},{12,20},{16,8},{20,12},{24,0},{28,4},{1,25},{... | collective-permute-start | bytes 442376 | tf_op jit(solution)/shard_map/ppermute | solution.py:419
  89.7 1.3 %collective-permute-done.16.rest_2_ = bf16[48,1536]{1,0:T(8,128)(2,1)S(1)} collective-permute-done((bf16[48,1536]{1,0:T(8,128)(2,1)S(1)}, bf16[48,1536]{1,0:T(8,128)(2,1)S(1)}, u32[]{:S(2)}, u32[]{:S(2)}) %collective-permute-start.16) | collective-permute-done | bytes 147488 | tf_op jit(solution)/shard_map/ppermute | solution.py:419
  91.0 1.0 collect.1.early
  92.0 0.5 collective-permute-done.17.rest_3_
  92.5 8.9 %collective-permute-done.19.rest_5_ = bf16[48,1536]{1,0:T(8,128)(2,1)S(1)} collective-permute-done((bf16[48,1536]{1,0:T(8,128)(2,1)S(1)}, bf16[48,1536]{1,0:T(8,128)(2,1)S(1)}, u32[]{:S(2)}, u32[]{:S(2)}) %collective-permute-start.19) | collective-permute-done | bytes 147488 | tf_op jit(solution)/shard_map/ppermute | solution.py:419
  101.5 9.4 %final.1 = f32[48,768,128]{2,1,0:T(8,128)} custom-call(s32[2]{0:T(128)S(1)} %pad_add_fusion.here, bf16[48,192,768]{2,1,0:T(8,128)(2,1)S(1)} %bitcast.10, f32[9216,128]{1,0:T(8,128)S(1)} %collect.1.early, bf16[48,1536]{1,0:T(8,128)(2,1)S(1)} %get-tuple-element.45.rest_0_, bf16[48,1536]{1,0:T(8,128)(2,1)S(1)} %collective-permute-done.15.rest_1_, ...), custom_call_target="tpu_custom_call" | custom-call | tf_op jit(solution)/shard_map/final/pallas_call | solution.py:435
  (23 shorter events, 0.1 us)
Async XLA Ops:
  0.7 1.1 %copy-start = (bf16[24,128,128]{2,1,0:T(8,128)(2,1)S(1)}, bf16[24,128,128]{2,1,0:T(8,128)(2,1)}, u32[]{:S(2)}) copy-start(bf16[24,128,128]{2,1,0:T(8,128)(2,1)} %param.7) | copy-start | bytes 2359300
  1.9 0.8 copy-start.1
  2.7 0.8 copy-start.2
  3.4 0.7 copy-start.3
  5.9 23.9 %collective-permute-start.1 = (bf16[1728,128]{1,0:T(8,128)(2,1)S(1)}, bf16[1728,128]{1,0:T(8,128)(2,1)S(1)}, u32[]{:S(2)}, u32[]{:S(2)}) collective-permute-start(bf16[1728,128]{1,0:T(8,128)(2,1)S(1)} %get-tuple-element.30.rest_0_), channel_id=1, source_target_pairs={{0,2},{1,3},{2,0},{3,1},{4,6},{5,7},{6,4},{7,5},{8,10},{9,11},{10,... | collective-permute-start | bytes 1327112 | tf_op jit(solution)/shard_map/ppermute | solution.py:356
  10.0 19.9 %collective-permute-start = (bf16[1728,128]{1,0:T(8,128)(2,1)S(1)}, bf16[1728,128]{1,0:T(8,128)(2,1)S(1)}, u32[]{:S(2)}, u32[]{:S(2)}) collective-permute-start(bf16[1728,128]{1,0:T(8,128)(2,1)S(1)} %get-tuple-element.30.rest_0_), channel_id=1, source_target_pairs={{0,1},{1,0},{2,3},{3,2},{4,5},{5,4},{6,7},{7,6},{8,9},{9,8},{10,11... | collective-permute-start | bytes 1327112 | tf_op jit(solution)/shard_map/ppermute | solution.py:356
  29.9 14.2 %collective-permute-start.2 = (bf16[1728,128]{1,0:T(8,128)(2,1)S(1)}, bf16[1728,128]{1,0:T(8,128)(2,1)S(1)}, u32[]{:S(2)}, u32[]{:S(2)}) collective-permute-start(bf16[1728,128]{1,0:T(8,128)(2,1)S(1)} %get-tuple-element.30.rest_0_), channel_id=1, source_target_pairs={{1,2},{2,1},{5,6},{6,5},{9,10},{10,9},{13,14},{14,13},{17,18},{18,... | collective-permute-start | bytes 1327112 | tf_op jit(solution)/shard_map/ppermute | solution.py:356
  30.6 13.5 %collective-permute-start.3 = (bf16[1728,128]{1,0:T(8,128)(2,1)S(1)}, bf16[1728,128]{1,0:T(8,128)(2,1)S(1)}, u32[]{:S(2)}, u32[]{:S(2)}) collective-permute-start(bf16[1728,128]{1,0:T(8,128)(2,1)S(1)} %collective-permute-done.1.rest_2_), channel_id=1, source_target_pairs={{1,0},{2,3},{5,4},{6,7},{9,8},{10,11},{13,12},{14,15},{17,16},{18,... | collective-permute-start | bytes 1327112 | tf_op jit(solution)/shard_map/ppermute | solution.py:360
  44.1 18.8 %collective-permute-start.12 = (bf16[1536,128]{1,0:T(8,128)(2,1)S(1)}, bf16[1536,128]{1,0:T(8,128)(2,1)S(1)}, u32[]{:S(2)}, u32[]{:S(2)}) collective-permute-start(bf16[1536,128]{1,0:T(8,128)(2,1)S(1)} %get-tuple-element.41.rest_0_), channel_id=1, source_target_pairs={{0,2},{1,3},{2,0},{3,1},{4,6},{5,7},{6,4},{7,5},{8,10},{9,11},{10,... | collective-permute-start | bytes 1179656 | tf_op jit(solution)/shard_map/ppermute | solution.py:356
  45.9 17.1 %collective-permute-start.11 = (bf16[1536,128]{1,0:T(8,128)(2,1)S(1)}, bf16[1536,128]{1,0:T(8,128)(2,1)S(1)}, u32[]{:S(2)}, u32[]{:S(2)}) collective-permute-start(bf16[1536,128]{1,0:T(8,128)(2,1)S(1)} %get-tuple-element.41.rest_0_), channel_id=1, source_target_pairs={{0,1},{1,0},{2,3},{3,2},{4,5},{5,4},{6,7},{7,6},{8,9},{9,8},{10,11... | collective-permute-start | bytes 1179656 | tf_op jit(solution)/shard_map/ppermute | solution.py:356
  48.4 53.0 %slice-start = ((s8[14155776]{0:T(1024)(128)(4,1)}), s8[4194304]{0:T(1024)(128)(4,1)S(1)}, s32[]{:S(2)}) async-start(s8[14155776]{0:T(1024)(128)(4,1)} %bitcast.9), calls=%async_computation | async-start | bytes 8388608
  55.9 7.8 %collective-permute-start.5 = (bf16[48,1536]{1,0:T(8,128)(2,1)S(1)}, bf16[48,1536]{1,0:T(8,128)(2,1)S(1)}, u32[]{:S(2)}, u32[]{:S(2)}) collective-permute-start(bf16[48,1536]{1,0:T(8,128)(2,1)S(1)} %get-tuple-element.33), channel_id=1, source_target_pairs={{0,8},{4,12},{8,0},{12,4},{16,24},{20,28},{24,16},{28,20},{1,9},{5... | collective-permute-start | bytes 442376 | tf_op jit(solution)/shard_map/ppermute | solution.py:419
  56.6 17.6 %collective-permute-start.6 = (bf16[48,1536]{1,0:T(8,128)(2,1)S(1)}, bf16[48,1536]{1,0:T(8,128)(2,1)S(1)}, u32[]{:S(2)}, u32[]{:S(2)}) collective-permute-start(bf16[48,1536]{1,0:T(8,128)(2,1)S(1)} %get-tuple-element.34), channel_id=1, source_target_pairs={{0,12},{4,8},{8,4},{12,0},{16,28},{20,24},{24,20},{28,16},{1,13},{... | collective-permute-start | bytes 442376 | tf_op jit(solution)/shard_map/ppermute | solution.py:419
  56.6 19.3 %collective-permute-start.7 = (bf16[48,1536]{1,0:T(8,128)(2,1)S(1)}, bf16[48,1536]{1,0:T(8,128)(2,1)S(1)}, u32[]{:S(2)}, u32[]{:S(2)}) collective-permute-start(bf16[48,1536]{1,0:T(8,128)(2,1)S(1)} %get-tuple-element.35), channel_id=1, source_target_pairs={{0,16},{4,20},{8,24},{12,28},{16,0},{20,4},{24,8},{28,12},{1,17},{... | collective-permute-start | bytes 442376 | tf_op jit(solution)/shard_map/ppermute | solution.py:419
  62.9 15.0 %collective-permute-start.8 = (bf16[48,1536]{1,0:T(8,128)(2,1)S(1)}, bf16[48,1536]{1,0:T(8,128)(2,1)S(1)}, u32[]{:S(2)}, u32[]{:S(2)}) collective-permute-start(bf16[48,1536]{1,0:T(8,128)(2,1)S(1)} %get-tuple-element.36), channel_id=1, source_target_pairs={{0,20},{4,16},{8,28},{12,24},{16,4},{20,0},{24,12},{28,8},{1,21},{... | collective-permute-start | bytes 442376 | tf_op jit(solution)/shard_map/ppermute | solution.py:419
  63.0 15.3 %collective-permute-start.13 = (bf16[1536,128]{1,0:T(8,128)(2,1)S(1)}, bf16[1536,128]{1,0:T(8,128)(2,1)S(1)}, u32[]{:S(2)}, u32[]{:S(2)}) collective-permute-start(bf16[1536,128]{1,0:T(8,128)(2,1)S(1)} %get-tuple-element.41.rest_0_), channel_id=1, source_target_pairs={{1,2},{2,1},{5,6},{6,5},{9,10},{10,9},{13,14},{14,13},{17,18},{18,... | collective-permute-start | bytes 1179656 | tf_op jit(solution)/shard_map/ppermute | solution.py:356
  63.7 14.6 %collective-permute-start.14 = (bf16[1536,128]{1,0:T(8,128)(2,1)S(1)}, bf16[1536,128]{1,0:T(8,128)(2,1)S(1)}, u32[]{:S(2)}, u32[]{:S(2)}) collective-permute-start(bf16[1536,128]{1,0:T(8,128)(2,1)S(1)} %collective-permute-done.12.rest_2_), channel_id=1, source_target_pairs={{1,0},{2,3},{5,4},{6,7},{9,8},{10,11},{13,12},{14,15},{17,16},{18,... | collective-permute-start | bytes 1179656 | tf_op jit(solution)/shard_map/ppermute | solution.py:360
  65.0 36.4 %slice-start.1 = ((s8[14155776]{0:T(1024)(128)(4,1)}), s8[4194304]{0:T(1024)(128)(4,1)S(1)}, s32[]{:S(2)}) async-start(s8[14155776]{0:T(1024)(128)(4,1)} %bitcast.9), calls=%async_computation.1 | async-start | bytes 8388608
  65.0 36.4 %slice-start.2 = ((s8[14155776]{0:T(1024)(128)(4,1)}), s8[4194304]{0:T(1024)(128)(4,1)S(1)}, s32[]{:S(2)}) async-start(s8[14155776]{0:T(1024)(128)(4,1)} %bitcast.9), calls=%async_computation.2 | async-start | bytes 8388608
  65.0 36.4 %slice-start.3 = ((s8[14155776]{0:T(1024)(128)(4,1)}), s8[1572864]{0:T(1024)(128)(4,1)S(1)}, s32[]{:S(2)}) async-start(s8[14155776]{0:T(1024)(128)(4,1)} %bitcast.9), calls=%async_computation.3 | async-start | bytes 3145728
  74.3 10.9 %collective-permute-start.4 = (bf16[48,1536]{1,0:T(8,128)(2,1)S(1)}, bf16[48,1536]{1,0:T(8,128)(2,1)S(1)}, u32[]{:S(2)}, u32[]{:S(2)}) collective-permute-start(bf16[48,1536]{1,0:T(8,128)(2,1)S(1)} %get-tuple-element.32), channel_id=1, source_target_pairs={{0,4},{4,0},{8,12},{12,8},{16,20},{20,16},{24,28},{28,24},{1,5},{5... | collective-permute-start | bytes 442376 | tf_op jit(solution)/shard_map/ppermute | solution.py:419
  76.0 9.8 %collective-permute-start.9 = (bf16[48,1536]{1,0:T(8,128)(2,1)S(1)}, bf16[48,1536]{1,0:T(8,128)(2,1)S(1)}, u32[]{:S(2)}, u32[]{:S(2)}) collective-permute-start(bf16[48,1536]{1,0:T(8,128)(2,1)S(1)} %get-tuple-element.37), channel_id=1, source_target_pairs={{0,24},{4,28},{8,16},{12,20},{16,8},{20,12},{24,0},{28,4},{1,25},{... | collective-permute-start | bytes 442376 | tf_op jit(solution)/shard_map/ppermute | solution.py:419
  77.9 8.9 %collective-permute-start.10 = (bf16[48,1536]{1,0:T(8,128)(2,1)S(1)}, bf16[48,1536]{1,0:T(8,128)(2,1)S(1)}, u32[]{:S(2)}, u32[]{:S(2)}) collective-permute-start(bf16[48,1536]{1,0:T(8,128)(2,1)S(1)} %get-tuple-element.38), channel_id=1, source_target_pairs={{0,28},{4,24},{8,20},{12,16},{16,12},{20,8},{24,4},{28,0},{1,29},{... | collective-permute-start | bytes 442376 | tf_op jit(solution)/shard_map/ppermute | solution.py:419
  83.5 4.3 %collective-permute-start.15 = (bf16[48,1536]{1,0:T(8,128)(2,1)S(1)}, bf16[48,1536]{1,0:T(8,128)(2,1)S(1)}, u32[]{:S(2)}, u32[]{:S(2)}) collective-permute-start(bf16[48,1536]{1,0:T(8,128)(2,1)S(1)} %get-tuple-element.46), channel_id=1, source_target_pairs={{0,4},{4,0},{8,12},{12,8},{16,20},{20,16},{24,28},{28,24},{1,5},{5... | collective-permute-start | bytes 442376 | tf_op jit(solution)/shard_map/ppermute | solution.py:419
  84.3 6.7 %collective-permute-start.16 = (bf16[48,1536]{1,0:T(8,128)(2,1)S(1)}, bf16[48,1536]{1,0:T(8,128)(2,1)S(1)}, u32[]{:S(2)}, u32[]{:S(2)}) collective-permute-start(bf16[48,1536]{1,0:T(8,128)(2,1)S(1)} %get-tuple-element.47), channel_id=1, source_target_pairs={{0,8},{4,12},{8,0},{12,4},{16,24},{20,28},{24,16},{28,20},{1,9},{5... | collective-permute-start | bytes 442376 | tf_op jit(solution)/shard_map/ppermute | solution.py:419
  85.2 7.4 %collective-permute-start.17 = (bf16[48,1536]{1,0:T(8,128)(2,1)S(1)}, bf16[48,1536]{1,0:T(8,128)(2,1)S(1)}, u32[]{:S(2)}, u32[]{:S(2)}) collective-permute-start(bf16[48,1536]{1,0:T(8,128)(2,1)S(1)} %get-tuple-element.48), channel_id=1, source_target_pairs={{0,12},{4,8},{8,4},{12,0},{16,28},{20,24},{24,20},{28,16},{1,13},{... | collective-permute-start | bytes 442376 | tf_op jit(solution)/shard_map/ppermute | solution.py:419
  85.7 6.8 %collective-permute-start.18 = (bf16[48,1536]{1,0:T(8,128)(2,1)S(1)}, bf16[48,1536]{1,0:T(8,128)(2,1)S(1)}, u32[]{:S(2)}, u32[]{:S(2)}) collective-permute-start(bf16[48,1536]{1,0:T(8,128)(2,1)S(1)} %get-tuple-element.49), channel_id=1, source_target_pairs={{0,16},{4,20},{8,24},{12,28},{16,0},{20,4},{24,8},{28,12},{1,17},{... | collective-permute-start | bytes 442376 | tf_op jit(solution)/shard_map/ppermute | solution.py:419
  86.8 14.6 %collective-permute-start.19 = (bf16[48,1536]{1,0:T(8,128)(2,1)S(1)}, bf16[48,1536]{1,0:T(8,128)(2,1)S(1)}, u32[]{:S(2)}, u32[]{:S(2)}) collective-permute-start(bf16[48,1536]{1,0:T(8,128)(2,1)S(1)} %get-tuple-element.50), channel_id=1, source_target_pairs={{0,20},{4,16},{8,28},{12,24},{16,4},{20,0},{24,12},{28,8},{1,21},{... | collective-permute-start | bytes 442376 | tf_op jit(solution)/shard_map/ppermute | solution.py:419
  87.8 13.6 %collective-permute-start.20 = (bf16[48,1536]{1,0:T(8,128)(2,1)S(1)}, bf16[48,1536]{1,0:T(8,128)(2,1)S(1)}, u32[]{:S(2)}, u32[]{:S(2)}) collective-permute-start(bf16[48,1536]{1,0:T(8,128)(2,1)S(1)} %get-tuple-element.51), channel_id=1, source_target_pairs={{0,24},{4,28},{8,16},{12,20},{16,8},{20,12},{24,0},{28,4},{1,25},{... | collective-permute-start | bytes 442376 | tf_op jit(solution)/shard_map/ppermute | solution.py:419
  91.0 10.4 %collective-permute-start.21 = (bf16[48,1536]{1,0:T(8,128)(2,1)S(1)}, bf16[48,1536]{1,0:T(8,128)(2,1)S(1)}, u32[]{:S(2)}, u32[]{:S(2)}) collective-permute-start(bf16[48,1536]{1,0:T(8,128)(2,1)S(1)} %get-tuple-element.52), channel_id=1, source_target_pairs={{0,28},{4,24},{8,20},{12,16},{16,12},{20,8},{24,4},{28,0},{1,29},{... | collective-permute-start | bytes 442376 | tf_op jit(solution)/shard_map/ppermute | solution.py:419

commit v4 on v3

--- a/solution.py
+++ b/solution.py
@@ -269,7 +269,7 @@
             gathered[pl.ds(start, waves), :] = total
 
 
-def final_body(last, bands, lat_rows, per_step, here, legendre, early, *rest):
+def final_body(last, bands, lat_rows, per_step, per_copy, here, legendre, early, *rest):
     pieces, (out, gathered, factor, staged, done) = rest[:bands], rest[bands:]
     waves, lat_total, degrees = legendre.shape
     first, width = last
@@ -291,8 +291,9 @@
                 legendre[wave], column, (((0,), (0,)), ((), ())), preferred_element_type=F32
             )
             staged[wave] = projected * factor[...]
-        rows = pl.ds(number * per_step, per_step)
-        pltpu.make_async_copy(staged.at[rows], out.at[rows], done).start()
+            if (inner + 1) % per_copy == 0:
+                rows = pl.ds(wave + 1 - per_copy, per_copy)
+                pltpu.make_async_copy(staged.at[rows], out.at[rows], done).start()
         return 0
 
     lax.fori_loop(0, waves // per_step, step, 0)
@@ -343,7 +344,7 @@
             pltpu.VMEM(req_frac.shape[2:], jnp.int32),
             pltpu.SemaphoreType.DMA((5,)),
         ],
-        compiler_params=limit(48),
+        compiler_params=limit(63),
         name="pack",
     )(req_count[0, 0], fields.reshape(cells, channels), req_block[0, 0], req_stencil[0, 0], req_frac[0, 0])
 
@@ -431,9 +432,9 @@
         cost_estimate=cost(10**9),
         name="collect",
     )(here, *early)
-    per_step = math.gcd(waves, 8)
+    per_step = math.gcd(waves, 16)
     return pl.pallas_call(
-        functools.partial(final_body, chunks[-1], bands, lat_rows, per_step),
+        functools.partial(final_body, chunks[-1], bands, lat_rows, per_step, math.gcd(per_step, 4)),
         out_shape=jax.ShapeDtypeStruct((waves, degrees, channels), F32),
         in_specs=[SMEM] + [VMEM] * (bands + 2),
         out_specs=ANY,

time: 112 us -> 110 us (0.982)
  local copies, waits for them, and re-layouts: 5.13 us -> 3.42 us
    unnamed x17 -> x13, local copies, waits for them, and re-layouts: 4.11 us -> 2.35 us
    pallas_call x1, Pallas kernels: 1.8 us -> 3.25 us  [gathering(): pl.pallas_call(functools.partial(pack_body, chunks, blocks), out_shape=[j...]
  transfers between devices with their start and end apart: 22 -> 22, of which waited for: 8 -> 9; matrix products, arithmetic and copies ran while one was open for 1% -> 1% of each run, Pallas kernels for 28% -> 29%
where the time goes in v4:
time: 110 us; the launch traced here: 109 us
  Pallas kernels  42.7 us (39%)
  waiting for transfers between devices  35.7 us (32%)
  starting transfers between devices  26.5 us (24%)
  local copies, waits for them, and re-layouts  3.42 us (3%)
    pallas_call x4, Pallas kernels, gathering(): pl.pallas_call(functools.partial(interp_body, count, bands, width, blocks...  30.1 us
    ppermute x6, waiting for transfers between devices, exchange(): lax.ppermute(after(tile, others), 'lon', [pair for pair in near if pair[0...  21.9 us
    ppermute x14, starting transfers between devices, gathering(): lax.ppermute(results[shift], 'lat', [(i, i ^ shift) for i in range(bands)])  12.6 us
    ppermute x6, starting transfers between devices, exchange(): lax.ppermute(after(tile, others), 'lon', [pair for pair in near if pair[0...  11.3 us
    ppermute x14, waiting for transfers between devices, gathering(): lax.ppermute(results[shift], 'lat', [(i, i ^ shift) for i in range(bands)])  10.9 us
    pallas_call x1, Pallas kernels, gathering(): pl.pallas_call(functools.partial(final_body, chunks[-1], bands, lat_rows,...  8.35 us
    pallas_call x1, Pallas kernels, gathering(): pl.pallas_call(functools.partial(pack_body, chunks, blocks), out_shape=[j...  3.25 us
    ppermute x2, waiting for transfers between devices, relay(): return lax.ppermute(tile, 'lon', pairs)  2.92 us
  transfers between devices with their start and end apart: 22, of which 9 were waited for; matrix products, arithmetic and copies ran while one was open for 1% of the time, Pallas kernels for 29%

profile of v4, /device:TPU:0, one launch (start us, length us, event | category | flops | bytes accessed | tf_op | source)
XLA Modules:
  0.0 108.8 jit_solution(14663428338031415636)
XLA Ops:
  0.0 1.3 %copy.10 = s32[1,1,3,1280]{3,2,1,0:T(4,128)} copy(s32[1,1,3,1280]{3,1,2,0:T(1,128)} %param.8) | data formatting | bytes 30720
  1.3 3.2 %pack.1 = (bf16[1728,128]{1,0:T(8,128)(2,1)}, bf16[1536,128]{1,0:T(8,128)(2,1)}) custom-call(s32[3]{0:T(128)} %bitcast.15, bf16[3072,128]{1,0:T(8,128)(2,1)} %bitcast.11, s32[3,1280]{1,0:T(4,128)} %bitcast.12, s32[3,4,1280]{2,1,0:T(4,128)} %bitcast.13, s32[3,2,1280]{2,1,0:T(2,128)} %bitcast.14), custom_call_target="tpu_custom_call" | custom-call | tf_op jit(solution)/shard_map/pack/pallas_call | solution.py:333
  4.6 4.1 %collective-permute-start.1 = (bf16[1728,128]{1,0:T(8,128)(2,1)}, bf16[1728,128]{1,0:T(8,128)(2,1)S(1)}, u32[]{:S(2)}, u32[]{:S(2)}) collective-permute-start(bf16[1728,128]{1,0:T(8,128)(2,1)} %get-tuple-element.30.rest_0_), channel_id=1, source_target_pairs={{0,2},{1,3},{2,0},{3,1},{4,6},{5,7},{6,4},{7,5},{8,10},{9,11},{10,... | collective-permute-start | bytes 1327112 | tf_op jit(solution)/shard_map/ppermute | solution.py:357
  8.7 1.6 %collective-permute-start = (bf16[1728,128]{1,0:T(8,128)(2,1)}, bf16[1728,128]{1,0:T(8,128)(2,1)S(1)}, u32[]{:S(2)}, u32[]{:S(2)}) collective-permute-start(bf16[1728,128]{1,0:T(8,128)(2,1)} %get-tuple-element.30.rest_0_), channel_id=1, source_target_pairs={{0,1},{1,0},{2,3},{3,2},{4,5},{5,4},{6,7},{7,6},{8,9},{9,8},{10,11... | collective-permute-start | bytes 1327112 | tf_op jit(solution)/shard_map/ppermute | solution.py:357
  10.3 0.1 pad_add_fusion.here
  10.3 1.1 constant_dynamic-slice_fusion.rest_6_.rest_5_
  11.4 17.2 %collective-permute-done.1.rest_2_ = bf16[1728,128]{1,0:T(8,128)(2,1)S(1)} collective-permute-done((bf16[1728,128]{1,0:T(8,128)(2,1)}, bf16[1728,128]{1,0:T(8,128)(2,1)S(1)}, u32[]{:S(2)}, u32[]{:S(2)}) %collective-permute-start.1) | collective-permute-done | bytes 442400 | tf_op jit(solution)/shard_map/ppermute | solution.py:357
  28.6 0.2 collective-permute-done.rest_1_
  28.8 0.7 collective-permute-start.2
  29.5 1.3 %collective-permute-start.3 = (bf16[1728,128]{1,0:T(8,128)(2,1)S(1)}, bf16[1728,128]{1,0:T(8,128)(2,1)S(1)}, u32[]{:S(2)}, u32[]{:S(2)}) collective-permute-start(bf16[1728,128]{1,0:T(8,128)(2,1)S(1)} %collective-permute-done.1.rest_2_), channel_id=1, source_target_pairs={{1,0},{2,3},{5,4},{6,7},{9,8},{10,11},{13,12},{14,15},{17,16},{18,... | collective-permute-start | bytes 1327112 | tf_op jit(solution)/shard_map/ppermute | solution.py:361
  30.8 0.0 copy-start
  30.8 1.0 copy-done
  31.8 8.3 %early.2.rest_5_ = bf16[1536,512]{1,0:T(8,128)(2,1)S(1)} custom-call(s32[2]{0:T(128)S(1)} %pad_add_fusion.here, bf16[1728,128]{1,0:T(8,128)(2,1)S(1)} %copy-done, bf16[1728,128]{1,0:T(8,128)(2,1)S(1)} %collective-permute-done.rest_1_, bf16[1728,128]{1,0:T(8,128)(2,1)S(1)} %collective-permute-done.1.rest_2_), custom_call_target="tpu_custom_call" | custom-call | flops 64000000000 | bytes 1000000 | tf_op jit(solution)/shard_map/early/pallas_call | solution.py:389
  40.1 2.9 %collective-permute-done.3.rest_4_ = bf16[1728,128]{1,0:T(8,128)(2,1)S(1)} collective-permute-done((bf16[1728,128]{1,0:T(8,128)(2,1)S(1)}, bf16[1728,128]{1,0:T(8,128)(2,1)S(1)}, u32[]{:S(2)}, u32[]{:S(2)}) %collective-permute-start.3) | collective-permute-done | bytes 442400 | tf_op jit(solution)/shard_map/ppermute | solution.py:361
  43.0 0.0 collective-permute-done.2.rest_3_
  43.0 1.8 %collective-permute-start.12 = (bf16[1536,128]{1,0:T(8,128)(2,1)S(1)}, bf16[1536,128]{1,0:T(8,128)(2,1)S(1)}, u32[]{:S(2)}, u32[]{:S(2)}) collective-permute-start(bf16[1536,128]{1,0:T(8,128)(2,1)S(1)} %copy-done.1), channel_id=1, source_target_pairs={{0,2},{1,3},{2,0},{3,1},{4,6},{5,7},{6,4},{7,5},{8,10},{9,11},{10,... | collective-permute-start | bytes 1179656 | tf_op jit(solution)/shard_map/ppermute | solution.py:357
  44.8 2.5 %collective-permute-start.11 = (bf16[1536,128]{1,0:T(8,128)(2,1)S(1)}, bf16[1536,128]{1,0:T(8,128)(2,1)S(1)}, u32[]{:S(2)}, u32[]{:S(2)}) collective-permute-start(bf16[1536,128]{1,0:T(8,128)(2,1)S(1)} %copy-done.1), channel_id=1, source_target_pairs={{0,1},{1,0},{2,3},{3,2},{4,5},{5,4},{6,7},{7,6},{8,9},{9,8},{10,11... | collective-permute-start | bytes 1179656 | tf_op jit(solution)/shard_map/ppermute | solution.py:357
  47.3 7.4 %late.2 = (bf16[48,1536]{1,0:T(8,128)(2,1)S(1)}, bf16[48,1536]{1,0:T(8,128)(2,1)S(1)}, bf16[48,1536]{1,0:T(8,128)(2,1)S(1)}, bf16[48,1536]{1,0:T(8,128)(2,1)S(1)...) custom-call(s32[2]{0:T(128)S(1)} %pad_add_fusion.here, ...), custom_call_target="tpu_custom_call" | custom-call | flops 3200000000 | bytes 1000000 | tf_op jit(solution)/shard_map/late/pallas_call | solution.py:401
  54.7 0.8 collective-permute-start.5
  55.6 0.0 collective-permute-start.6
  55.6 2.3 %collective-permute-start.7 = (bf16[48,1536]{1,0:T(8,128)(2,1)S(1)}, bf16[48,1536]{1,0:T(8,128)(2,1)S(1)}, u32[]{:S(2)}, u32[]{:S(2)}) collective-permute-start(bf16[48,1536]{1,0:T(8,128)(2,1)S(1)} %get-tuple-element.35), channel_id=1, source_target_pairs={{0,16},{4,20},{8,24},{12,28},{16,0},{20,4},{24,8},{28,12},{1,17},{... | collective-permute-start | bytes 442376 | tf_op jit(solution)/shard_map/ppermute | solution.py:420
  57.8 4.4 %collective-permute-done.12.rest_2_ = bf16[1536,128]{1,0:T(8,128)(2,1)S(1)} collective-permute-done((bf16[1536,128]{1,0:T(8,128)(2,1)S(1)}, bf16[1536,128]{1,0:T(8,128)(2,1)S(1)}, u32[]{:S(2)}, u32[]{:S(2)}) %collective-permute-start.12) | collective-permute-done | bytes 393248 | tf_op jit(solution)/shard_map/ppermute | solution.py:357
  62.2 0.1 collective-permute-done.11.rest_1_
  62.3 0.7 collective-permute-start.13
  63.0 1.3 %collective-permute-start.14 = (bf16[1536,128]{1,0:T(8,128)(2,1)S(1)}, bf16[1536,128]{1,0:T(8,128)(2,1)S(1)}, u32[]{:S(2)}, u32[]{:S(2)}) collective-permute-start(bf16[1536,128]{1,0:T(8,128)(2,1)S(1)} %collective-permute-done.12.rest_2_), channel_id=1, source_target_pairs={{1,0},{2,3},{5,4},{6,7},{9,8},{10,11},{13,12},{14,15},{17,16},{18,... | collective-permute-start | bytes 1179656 | tf_op jit(solution)/shard_map/ppermute | solution.py:361
  64.3 0.0 slice-start.1
  64.3 0.0 slice-start.2
  64.3 9.2 %early.3.rest_4_ = bf16[1536,512]{1,0:T(8,128)(2,1)S(1)} custom-call(s32[2]{0:T(128)S(1)} %pad_add_fusion.here, bf16[1536,128]{1,0:T(8,128)(2,1)S(1)} %copy-done.1, bf16[1536,128]{1,0:T(8,128)(2,1)S(1)} %collective-permute-done.11.rest_1_, bf16[1536,128]{1,0:T(8,128)(2,1)S(1)} %collective-permute-done.12.rest_2_, ...), custom_call_target="tpu_custom_call" | custom-call | flops 64000000000 | bytes 1000000 | tf_op jit(solution)/shard_map/early/pallas_call | solution.py:389
  73.6 0.0 collective-permute-done.6.rest_3_
  73.6 2.1 %collective-permute-start.4 = (bf16[48,1536]{1,0:T(8,128)(2,1)S(1)}, bf16[48,1536]{1,0:T(8,128)(2,1)S(1)}, u32[]{:S(2)}, u32[]{:S(2)}) collective-permute-start(bf16[48,1536]{1,0:T(8,128)(2,1)S(1)} %get-tuple-element.32), channel_id=1, source_target_pairs={{0,4},{4,0},{8,12},{12,8},{16,20},{20,16},{24,28},{28,24},{1,5},{5... | collective-permute-start | bytes 442376 | tf_op jit(solution)/shard_map/ppermute | solution.py:420
  75.7 0.6 collective-permute-start.9
  76.3 0.0 collective-permute-done.8.rest_5_
  76.3 1.7 %collective-permute-start.10 = (bf16[48,1536]{1,0:T(8,128)(2,1)S(1)}, bf16[48,1536]{1,0:T(8,128)(2,1)S(1)}, u32[]{:S(2)}, u32[]{:S(2)}) collective-permute-start(bf16[48,1536]{1,0:T(8,128)(2,1)S(1)} %get-tuple-element.38), channel_id=1, source_target_pairs={{0,28},{4,24},{8,20},{12,16},{16,12},{20,8},{24,4},{28,0},{1,29},{... | collective-permute-start | bytes 442376 | tf_op jit(solution)/shard_map/ppermute | solution.py:420
  78.0 5.2 %late.3 = (bf16[48,1536]{1,0:T(8,128)(2,1)S(1)}, bf16[48,1536]{1,0:T(8,128)(2,1)S(1)}, bf16[48,1536]{1,0:T(8,128)(2,1)S(1)}, bf16[48,1536]{1,0:T(8,128)(2,1)S(1)...) custom-call(s32[2]{0:T(128)S(1)} %pad_add_fusion.here, ...), custom_call_target="tpu_custom_call" | custom-call | flops 3200000000 | bytes 1000000 | tf_op jit(solution)/shard_map/late/pallas_call | solution.py:401
  83.2 0.1 collective-permute-start.15
  83.3 1.7 %collective-permute-start.16 = (bf16[48,1536]{1,0:T(8,128)(2,1)S(1)}, bf16[48,1536]{1,0:T(8,128)(2,1)S(1)}, u32[]{:S(2)}, u32[]{:S(2)}) collective-permute-start(bf16[48,1536]{1,0:T(8,128)(2,1)S(1)} %get-tuple-element.47), channel_id=1, source_target_pairs={{0,8},{4,12},{8,0},{12,4},{16,24},{20,28},{24,16},{28,20},{1,9},{5... | collective-permute-start | bytes 442376 | tf_op jit(solution)/shard_map/ppermute | solution.py:420
  85.0 0.0 collective-permute-done.4.rest_1_
  85.0 0.1 collective-permute-start.17
  85.2 0.0 collective-permute-done.9.rest_6_
  85.2 0.1 collective-permute-start.18
  85.3 1.6 %collective-permute-start.19 = (bf16[48,1536]{1,0:T(8,128)(2,1)S(1)}, bf16[48,1536]{1,0:T(8,128)(2,1)S(1)}, u32[]{:S(2)}, u32[]{:S(2)}) collective-permute-start(bf16[48,1536]{1,0:T(8,128)(2,1)S(1)} %get-tuple-element.50), channel_id=1, source_target_pairs={{0,20},{4,16},{8,28},{12,24},{16,4},{20,0},{24,12},{28,8},{1,21},{... | collective-permute-start | bytes 442376 | tf_op jit(solution)/shard_map/ppermute | solution.py:420
  86.9 1.4 %collective-permute-start.20 = (bf16[48,1536]{1,0:T(8,128)(2,1)S(1)}, bf16[48,1536]{1,0:T(8,128)(2,1)S(1)}, u32[]{:S(2)}, u32[]{:S(2)}) collective-permute-start(bf16[48,1536]{1,0:T(8,128)(2,1)S(1)} %get-tuple-element.51), channel_id=1, source_target_pairs={{0,24},{4,28},{8,16},{12,20},{16,8},{20,12},{24,0},{28,4},{1,25},{... | collective-permute-start | bytes 442376 | tf_op jit(solution)/shard_map/ppermute | solution.py:420
  88.3 1.7 %collective-permute-done.16.rest_2_ = bf16[48,1536]{1,0:T(8,128)(2,1)S(1)} collective-permute-done((bf16[48,1536]{1,0:T(8,128)(2,1)S(1)}, bf16[48,1536]{1,0:T(8,128)(2,1)S(1)}, u32[]{:S(2)}, u32[]{:S(2)}) %collective-permute-start.16) | collective-permute-done | bytes 147488 | tf_op jit(solution)/shard_map/ppermute | solution.py:420
  90.0 1.0 collect.1.early
  91.0 1.4 %collective-permute-done.17.rest_3_ = bf16[48,1536]{1,0:T(8,128)(2,1)S(1)} collective-permute-done((bf16[48,1536]{1,0:T(8,128)(2,1)S(1)}, bf16[48,1536]{1,0:T(8,128)(2,1)S(1)}, u32[]{:S(2)}, u32[]{:S(2)}) %collective-permute-start.17) | collective-permute-done | bytes 147488 | tf_op jit(solution)/shard_map/ppermute | solution.py:420
  92.4 0.1 collective-permute-done.18.rest_4_
  92.5 7.7 %collective-permute-done.19.rest_5_ = bf16[48,1536]{1,0:T(8,128)(2,1)S(1)} collective-permute-done((bf16[48,1536]{1,0:T(8,128)(2,1)S(1)}, bf16[48,1536]{1,0:T(8,128)(2,1)S(1)}, u32[]{:S(2)}, u32[]{:S(2)}) %collective-permute-start.19) | collective-permute-done | bytes 147488 | tf_op jit(solution)/shard_map/ppermute | solution.py:420
  100.3 8.3 %final.1 = f32[48,768,128]{2,1,0:T(8,128)} custom-call(s32[2]{0:T(128)S(1)} %pad_add_fusion.here, bf16[48,192,768]{2,1,0:T(8,128)(2,1)S(1)} %bitcast.10, f32[9216,128]{1,0:T(8,128)S(1)} %collect.1.early, bf16[48,1536]{1,0:T(8,128)(2,1)S(1)} %get-tuple-element.45.rest_0_, bf16[48,1536]{1,0:T(8,128)(2,1)S(1)} %collective-permute-done.15.rest_1_, ...), custom_call_target="tpu_custom_call" | custom-call | tf_op jit(solution)/shard_map/final/pallas_call | solution.py:436
  (19 shorter events, 0.0 us)
Async XLA Ops:
  4.6 24.1 %collective-permute-start.1 = (bf16[1728,128]{1,0:T(8,128)(2,1)}, bf16[1728,128]{1,0:T(8,128)(2,1)S(1)}, u32[]{:S(2)}, u32[]{:S(2)}) collective-permute-start(bf16[1728,128]{1,0:T(8,128)(2,1)} %get-tuple-element.30.rest_0_), channel_id=1, source_target_pairs={{0,2},{1,3},{2,0},{3,1},{4,6},{5,7},{6,4},{7,5},{8,10},{9,11},{10,... | collective-permute-start | bytes 1327112 | tf_op jit(solution)/shard_map/ppermute | solution.py:357
  8.7 20.2 %collective-permute-start = (bf16[1728,128]{1,0:T(8,128)(2,1)}, bf16[1728,128]{1,0:T(8,128)(2,1)S(1)}, u32[]{:S(2)}, u32[]{:S(2)}) collective-permute-start(bf16[1728,128]{1,0:T(8,128)(2,1)} %get-tuple-element.30.rest_0_), channel_id=1, source_target_pairs={{0,1},{1,0},{2,3},{3,2},{4,5},{5,4},{6,7},{7,6},{8,9},{9,8},{10,11... | collective-permute-start | bytes 1327112 | tf_op jit(solution)/shard_map/ppermute | solution.py:357
  10.3 32.7 %copy-start.1 = (bf16[1536,128]{1,0:T(8,128)(2,1)S(1)}, bf16[1536,128]{1,0:T(8,128)(2,1)}, u32[]{:S(2)}) copy-start(bf16[1536,128]{1,0:T(8,128)(2,1)} %get-tuple-element.41.rest_0_) | copy-start | bytes 1179652
  28.8 14.2 %collective-permute-start.2 = (bf16[1728,128]{1,0:T(8,128)(2,1)}, bf16[1728,128]{1,0:T(8,128)(2,1)S(1)}, u32[]{:S(2)}, u32[]{:S(2)}) collective-permute-start(bf16[1728,128]{1,0:T(8,128)(2,1)} %get-tuple-element.30.rest_0_), channel_id=1, source_target_pairs={{1,2},{2,1},{5,6},{6,5},{9,10},{10,9},{13,14},{14,13},{17,18},{18,... | collective-permute-start | bytes 1327112 | tf_op jit(solution)/shard_map/ppermute | solution.py:357
  29.5 13.5 %collective-permute-start.3 = (bf16[1728,128]{1,0:T(8,128)(2,1)S(1)}, bf16[1728,128]{1,0:T(8,128)(2,1)S(1)}, u32[]{:S(2)}, u32[]{:S(2)}) collective-permute-start(bf16[1728,128]{1,0:T(8,128)(2,1)S(1)} %collective-permute-done.1.rest_2_), channel_id=1, source_target_pairs={{1,0},{2,3},{5,4},{6,7},{9,8},{10,11},{13,12},{14,15},{17,16},{18,... | collective-permute-start | bytes 1327112 | tf_op jit(solution)/shard_map/ppermute | solution.py:361
  30.8 1.0 copy-start
  43.0 19.2 %collective-permute-start.12 = (bf16[1536,128]{1,0:T(8,128)(2,1)S(1)}, bf16[1536,128]{1,0:T(8,128)(2,1)S(1)}, u32[]{:S(2)}, u32[]{:S(2)}) collective-permute-start(bf16[1536,128]{1,0:T(8,128)(2,1)S(1)} %copy-done.1), channel_id=1, source_target_pairs={{0,2},{1,3},{2,0},{3,1},{4,6},{5,7},{6,4},{7,5},{8,10},{9,11},{10,... | collective-permute-start | bytes 1179656 | tf_op jit(solution)/shard_map/ppermute | solution.py:357
  44.8 17.4 %collective-permute-start.11 = (bf16[1536,128]{1,0:T(8,128)(2,1)S(1)}, bf16[1536,128]{1,0:T(8,128)(2,1)S(1)}, u32[]{:S(2)}, u32[]{:S(2)}) collective-permute-start(bf16[1536,128]{1,0:T(8,128)(2,1)S(1)} %copy-done.1), channel_id=1, source_target_pairs={{0,1},{1,0},{2,3},{3,2},{4,5},{5,4},{6,7},{7,6},{8,9},{9,8},{10,11... | collective-permute-start | bytes 1179656 | tf_op jit(solution)/shard_map/ppermute | solution.py:357
  47.3 52.9 %slice-start = ((s8[14155776]{0:T(1024)(128)(4,1)}), s8[4194304]{0:T(1024)(128)(4,1)S(1)}, s32[]{:S(2)}) async-start(s8[14155776]{0:T(1024)(128)(4,1)} %bitcast.9), calls=%async_computation | async-start | bytes 8388608
  54.7 8.2 %collective-permute-start.5 = (bf16[48,1536]{1,0:T(8,128)(2,1)S(1)}, bf16[48,1536]{1,0:T(8,128)(2,1)S(1)}, u32[]{:S(2)}, u32[]{:S(2)}) collective-permute-start(bf16[48,1536]{1,0:T(8,128)(2,1)S(1)} %get-tuple-element.33), channel_id=1, source_target_pairs={{0,8},{4,12},{8,0},{12,4},{16,24},{20,28},{24,16},{28,20},{1,9},{5... | collective-permute-start | bytes 442376 | tf_op jit(solution)/shard_map/ppermute | solution.py:420
  55.6 18.0 %collective-permute-start.6 = (bf16[48,1536]{1,0:T(8,128)(2,1)S(1)}, bf16[48,1536]{1,0:T(8,128)(2,1)S(1)}, u32[]{:S(2)}, u32[]{:S(2)}) collective-permute-start(bf16[48,1536]{1,0:T(8,128)(2,1)S(1)} %get-tuple-element.34), channel_id=1, source_target_pairs={{0,12},{4,8},{8,4},{12,0},{16,28},{20,24},{24,20},{28,16},{1,13},{... | collective-permute-start | bytes 442376 | tf_op jit(solution)/shard_map/ppermute | solution.py:420
  55.6 20.1 %collective-permute-start.7 = (bf16[48,1536]{1,0:T(8,128)(2,1)S(1)}, bf16[48,1536]{1,0:T(8,128)(2,1)S(1)}, u32[]{:S(2)}, u32[]{:S(2)}) collective-permute-start(bf16[48,1536]{1,0:T(8,128)(2,1)S(1)} %get-tuple-element.35), channel_id=1, source_target_pairs={{0,16},{4,20},{8,24},{12,28},{16,0},{20,4},{24,8},{28,12},{1,17},{... | collective-permute-start | bytes 442376 | tf_op jit(solution)/shard_map/ppermute | solution.py:420
  62.2 14.1 %collective-permute-start.8 = (bf16[48,1536]{1,0:T(8,128)(2,1)S(1)}, bf16[48,1536]{1,0:T(8,128)(2,1)S(1)}, u32[]{:S(2)}, u32[]{:S(2)}) collective-permute-start(bf16[48,1536]{1,0:T(8,128)(2,1)S(1)} %get-tuple-element.36), channel_id=1, source_target_pairs={{0,20},{4,16},{8,28},{12,24},{16,4},{20,0},{24,12},{28,8},{1,21},{... | collective-permute-start | bytes 442376 | tf_op jit(solution)/shard_map/ppermute | solution.py:420
  62.3 15.7 %collective-permute-start.13 = (bf16[1536,128]{1,0:T(8,128)(2,1)S(1)}, bf16[1536,128]{1,0:T(8,128)(2,1)S(1)}, u32[]{:S(2)}, u32[]{:S(2)}) collective-permute-start(bf16[1536,128]{1,0:T(8,128)(2,1)S(1)} %copy-done.1), channel_id=1, source_target_pairs={{1,2},{2,1},{5,6},{6,5},{9,10},{10,9},{13,14},{14,13},{17,18},{18,... | collective-permute-start | bytes 1179656 | tf_op jit(solution)/shard_map/ppermute | solution.py:357
  63.0 15.0 %collective-permute-start.14 = (bf16[1536,128]{1,0:T(8,128)(2,1)S(1)}, bf16[1536,128]{1,0:T(8,128)(2,1)S(1)}, u32[]{:S(2)}, u32[]{:S(2)}) collective-permute-start(bf16[1536,128]{1,0:T(8,128)(2,1)S(1)} %collective-permute-done.12.rest_2_), channel_id=1, source_target_pairs={{1,0},{2,3},{5,4},{6,7},{9,8},{10,11},{13,12},{14,15},{17,16},{18,... | collective-permute-start | bytes 1179656 | tf_op jit(solution)/shard_map/ppermute | solution.py:361
  64.3 35.9 %slice-start.1 = ((s8[14155776]{0:T(1024)(128)(4,1)}), s8[4194304]{0:T(1024)(128)(4,1)S(1)}, s32[]{:S(2)}) async-start(s8[14155776]{0:T(1024)(128)(4,1)} %bitcast.9), calls=%async_computation.1 | async-start | bytes 8388608
  64.3 35.9 %slice-start.2 = ((s8[14155776]{0:T(1024)(128)(4,1)}), s8[4194304]{0:T(1024)(128)(4,1)S(1)}, s32[]{:S(2)}) async-start(s8[14155776]{0:T(1024)(128)(4,1)} %bitcast.9), calls=%async_computation.2 | async-start | bytes 8388608
  64.3 35.9 %slice-start.3 = ((s8[14155776]{0:T(1024)(128)(4,1)}), s8[1572864]{0:T(1024)(128)(4,1)S(1)}, s32[]{:S(2)}) async-start(s8[14155776]{0:T(1024)(128)(4,1)} %bitcast.9), calls=%async_computation.3 | async-start | bytes 3145728
  73.6 11.5 %collective-permute-start.4 = (bf16[48,1536]{1,0:T(8,128)(2,1)S(1)}, bf16[48,1536]{1,0:T(8,128)(2,1)S(1)}, u32[]{:S(2)}, u32[]{:S(2)}) collective-permute-start(bf16[48,1536]{1,0:T(8,128)(2,1)S(1)} %get-tuple-element.32), channel_id=1, source_target_pairs={{0,4},{4,0},{8,12},{12,8},{16,20},{20,16},{24,28},{28,24},{1,5},{5... | collective-permute-start | bytes 442376 | tf_op jit(solution)/shard_map/ppermute | solution.py:420
  75.7 9.5 %collective-permute-start.9 = (bf16[48,1536]{1,0:T(8,128)(2,1)S(1)}, bf16[48,1536]{1,0:T(8,128)(2,1)S(1)}, u32[]{:S(2)}, u32[]{:S(2)}) collective-permute-start(bf16[48,1536]{1,0:T(8,128)(2,1)S(1)} %get-tuple-element.37), channel_id=1, source_target_pairs={{0,24},{4,28},{8,16},{12,20},{16,8},{20,12},{24,0},{28,4},{1,25},{... | collective-permute-start | bytes 442376 | tf_op jit(solution)/shard_map/ppermute | solution.py:420
  76.3 9.0 %collective-permute-start.10 = (bf16[48,1536]{1,0:T(8,128)(2,1)S(1)}, bf16[48,1536]{1,0:T(8,128)(2,1)S(1)}, u32[]{:S(2)}, u32[]{:S(2)}) collective-permute-start(bf16[48,1536]{1,0:T(8,128)(2,1)S(1)} %get-tuple-element.38), channel_id=1, source_target_pairs={{0,28},{4,24},{8,20},{12,16},{16,12},{20,8},{24,4},{28,0},{1,29},{... | collective-permute-start | bytes 442376 | tf_op jit(solution)/shard_map/ppermute | solution.py:420
  83.2 3.7 %collective-permute-start.15 = (bf16[48,1536]{1,0:T(8,128)(2,1)S(1)}, bf16[48,1536]{1,0:T(8,128)(2,1)S(1)}, u32[]{:S(2)}, u32[]{:S(2)}) collective-permute-start(bf16[48,1536]{1,0:T(8,128)(2,1)S(1)} %get-tuple-element.46), channel_id=1, source_target_pairs={{0,4},{4,0},{8,12},{12,8},{16,20},{20,16},{24,28},{28,24},{1,5},{5... | collective-permute-start | bytes 442376 | tf_op jit(solution)/shard_map/ppermute | solution.py:420
  83.3 6.7 %collective-permute-start.16 = (bf16[48,1536]{1,0:T(8,128)(2,1)S(1)}, bf16[48,1536]{1,0:T(8,128)(2,1)S(1)}, u32[]{:S(2)}, u32[]{:S(2)}) collective-permute-start(bf16[48,1536]{1,0:T(8,128)(2,1)S(1)} %get-tuple-element.47), channel_id=1, source_target_pairs={{0,8},{4,12},{8,0},{12,4},{16,24},{20,28},{24,16},{28,20},{1,9},{5... | collective-permute-start | bytes 442376 | tf_op jit(solution)/shard_map/ppermute | solution.py:420
  85.0 7.4 %collective-permute-start.17 = (bf16[48,1536]{1,0:T(8,128)(2,1)S(1)}, bf16[48,1536]{1,0:T(8,128)(2,1)S(1)}, u32[]{:S(2)}, u32[]{:S(2)}) collective-permute-start(bf16[48,1536]{1,0:T(8,128)(2,1)S(1)} %get-tuple-element.48), channel_id=1, source_target_pairs={{0,12},{4,8},{8,4},{12,0},{16,28},{20,24},{24,20},{28,16},{1,13},{... | collective-permute-start | bytes 442376 | tf_op jit(solution)/shard_map/ppermute | solution.py:420
  85.2 7.3 %collective-permute-start.18 = (bf16[48,1536]{1,0:T(8,128)(2,1)S(1)}, bf16[48,1536]{1,0:T(8,128)(2,1)S(1)}, u32[]{:S(2)}, u32[]{:S(2)}) collective-permute-start(bf16[48,1536]{1,0:T(8,128)(2,1)S(1)} %get-tuple-element.49), channel_id=1, source_target_pairs={{0,16},{4,20},{8,24},{12,28},{16,0},{20,4},{24,8},{28,12},{1,17},{... | collective-permute-start | bytes 442376 | tf_op jit(solution)/shard_map/ppermute | solution.py:420
  85.3 14.9 %collective-permute-start.19 = (bf16[48,1536]{1,0:T(8,128)(2,1)S(1)}, bf16[48,1536]{1,0:T(8,128)(2,1)S(1)}, u32[]{:S(2)}, u32[]{:S(2)}) collective-permute-start(bf16[48,1536]{1,0:T(8,128)(2,1)S(1)} %get-tuple-element.50), channel_id=1, source_target_pairs={{0,20},{4,16},{8,28},{12,24},{16,4},{20,0},{24,12},{28,8},{1,21},{... | collective-permute-start | bytes 442376 | tf_op jit(solution)/shard_map/ppermute | solution.py:420
  86.9 13.3 %collective-permute-start.20 = (bf16[48,1536]{1,0:T(8,128)(2,1)S(1)}, bf16[48,1536]{1,0:T(8,128)(2,1)S(1)}, u32[]{:S(2)}, u32[]{:S(2)}) collective-permute-start(bf16[48,1536]{1,0:T(8,128)(2,1)S(1)} %get-tuple-element.51), channel_id=1, source_target_pairs={{0,24},{4,28},{8,16},{12,20},{16,8},{20,12},{24,0},{28,4},{1,25},{... | collective-permute-start | bytes 442376 | tf_op jit(solution)/shard_map/ppermute | solution.py:420
  90.0 10.2 %collective-permute-start.21 = (bf16[48,1536]{1,0:T(8,128)(2,1)S(1)}, bf16[48,1536]{1,0:T(8,128)(2,1)S(1)}, u32[]{:S(2)}, u32[]{:S(2)}) collective-permute-start(bf16[48,1536]{1,0:T(8,128)(2,1)S(1)} %get-tuple-element.52), channel_id=1, source_target_pairs={{0,28},{4,24},{8,20},{12,16},{16,12},{20,8},{24,4},{28,0},{1,29},{... | collective-permute-start | bytes 442376 | tf_op jit(solution)/shard_map/ppermute | solution.py:420

commit v5 on v4

--- a/solution.py
+++ b/solution.py
@@ -14,7 +14,7 @@
 SLOTS = 3
 LANES = 128
 SPAN = 2 * LANES
-UNROLL = 4
+UNROLL = 5
 F32 = jnp.float32
 BF16 = jnp.bfloat16
 

time: 110 us -> 110 us (level)
  waiting for transfers between devices: 35.7 us -> 37.5 us
  starting transfers between devices: 26.5 us -> 24.9 us
    ppermute x14, starting transfers between devices: 12.6 us -> 10.9 us  [gathering(): lax.ppermute(results[shift], 'lat', [(i, i ^ shift) for i in range(bands)])]
    ppermute x6, waiting for transfers between devices: 21.9 us -> 23 us  [exchange(): lax.ppermute(after(tile, others), 'lon', [pair for pair in near if pair[0...]
  transfers between devices with their start and end apart: 22 -> 22, of which waited for: 9 -> 9; matrix products, arithmetic and copies ran while one was open for 1% -> 1% of each run, Pallas kernels for 29% -> 28%
where the time goes in v5:
time: 110 us; the launch traced here: 108 us
  Pallas kernels  42.2 us (38%)
  waiting for transfers between devices  37.5 us (34%)
  starting transfers between devices  24.9 us (23%)
  local copies, waits for them, and re-layouts  3.42 us (3%)
    pallas_call x4, Pallas kernels, gathering(): pl.pallas_call(functools.partial(interp_body, count, bands, width, blocks...  29.6 us
    ppermute x6, waiting for transfers between devices, exchange(): lax.ppermute(after(tile, others), 'lon', [pair for pair in near if pair[0...  23 us
    ppermute x6, starting transfers between devices, exchange(): lax.ppermute(after(tile, others), 'lon', [pair for pair in near if pair[0...  11.3 us
    ppermute x14, starting transfers between devices, gathering(): lax.ppermute(results[shift], 'lat', [(i, i ^ shift) for i in range(bands)])  10.9 us
    ppermute x14, waiting for transfers between devices, gathering(): lax.ppermute(results[shift], 'lat', [(i, i ^ shift) for i in range(bands)])  10.6 us
    pallas_call x1, Pallas kernels, gathering(): pl.pallas_call(functools.partial(final_body, chunks[-1], bands, lat_rows,...  8.35 us
    ppermute x2, waiting for transfers between devices, relay(): return lax.ppermute(tile, 'lon', pairs)  3.9 us
    pallas_call x1, Pallas kernels, gathering(): pl.pallas_call(functools.partial(pack_body, chunks, blocks), out_shape=[j...  3.25 us
  transfers between devices with their start and end apart: 22, of which 9 were waited for; matrix products, arithmetic and copies ran while one was open for 1% of the time, Pallas kernels for 28%

profile of v5, /device:TPU:0, one launch (start us, length us, event | category | flops | bytes accessed | tf_op | source)
XLA Modules:
  0.0 108.4 jit_solution(1814793422247132263)
XLA Ops:
  0.0 1.3 %copy.10 = s32[1,1,3,1280]{3,2,1,0:T(4,128)} copy(s32[1,1,3,1280]{3,1,2,0:T(1,128)} %param.8) | data formatting | bytes 30720
  1.3 3.2 %pack.1 = (bf16[1728,128]{1,0:T(8,128)(2,1)}, bf16[1536,128]{1,0:T(8,128)(2,1)}) custom-call(s32[3]{0:T(128)} %bitcast.15, bf16[3072,128]{1,0:T(8,128)(2,1)} %bitcast.11, s32[3,1280]{1,0:T(4,128)} %bitcast.12, s32[3,4,1280]{2,1,0:T(4,128)} %bitcast.13, s32[3,2,1280]{2,1,0:T(2,128)} %bitcast.14), custom_call_target="tpu_custom_call" | custom-call | tf_op jit(solution)/shard_map/pack/pallas_call | solution.py:333
  4.6 4.1 %collective-permute-start.1 = (bf16[1728,128]{1,0:T(8,128)(2,1)}, bf16[1728,128]{1,0:T(8,128)(2,1)S(1)}, u32[]{:S(2)}, u32[]{:S(2)}) collective-permute-start(bf16[1728,128]{1,0:T(8,128)(2,1)} %get-tuple-element.30.rest_0_), channel_id=1, source_target_pairs={{0,2},{1,3},{2,0},{3,1},{4,6},{5,7},{6,4},{7,5},{8,10},{9,11},{10,... | collective-permute-start | bytes 1327112 | tf_op jit(solution)/shard_map/ppermute | solution.py:357
  8.7 1.6 %collective-permute-start = (bf16[1728,128]{1,0:T(8,128)(2,1)}, bf16[1728,128]{1,0:T(8,128)(2,1)S(1)}, u32[]{:S(2)}, u32[]{:S(2)}) collective-permute-start(bf16[1728,128]{1,0:T(8,128)(2,1)} %get-tuple-element.30.rest_0_), channel_id=1, source_target_pairs={{0,1},{1,0},{2,3},{3,2},{4,5},{5,4},{6,7},{7,6},{8,9},{9,8},{10,11... | collective-permute-start | bytes 1327112 | tf_op jit(solution)/shard_map/ppermute | solution.py:357
  10.3 0.1 pad_add_fusion.here
  10.3 1.1 constant_dynamic-slice_fusion.rest_6_.rest_5_
  11.4 17.2 %collective-permute-done.1.rest_2_ = bf16[1728,128]{1,0:T(8,128)(2,1)S(1)} collective-permute-done((bf16[1728,128]{1,0:T(8,128)(2,1)}, bf16[1728,128]{1,0:T(8,128)(2,1)S(1)}, u32[]{:S(2)}, u32[]{:S(2)}) %collective-permute-start.1) | collective-permute-done | bytes 442400 | tf_op jit(solution)/shard_map/ppermute | solution.py:357
  28.6 0.2 collective-permute-done.rest_1_
  28.8 0.7 collective-permute-start.2
  29.5 1.3 %collective-permute-start.3 = (bf16[1728,128]{1,0:T(8,128)(2,1)S(1)}, bf16[1728,128]{1,0:T(8,128)(2,1)S(1)}, u32[]{:S(2)}, u32[]{:S(2)}) collective-permute-start(bf16[1728,128]{1,0:T(8,128)(2,1)S(1)} %collective-permute-done.1.rest_2_), channel_id=1, source_target_pairs={{1,0},{2,3},{5,4},{6,7},{9,8},{10,11},{13,12},{14,15},{17,16},{18,... | collective-permute-start | bytes 1327112 | tf_op jit(solution)/shard_map/ppermute | solution.py:361
  30.8 0.0 copy-start
  30.8 1.0 copy-done
  31.8 7.5 %early.2.rest_5_ = bf16[1536,512]{1,0:T(8,128)(2,1)S(1)} custom-call(s32[2]{0:T(128)S(1)} %pad_add_fusion.here, bf16[1728,128]{1,0:T(8,128)(2,1)S(1)} %copy-done, bf16[1728,128]{1,0:T(8,128)(2,1)S(1)} %collective-permute-done.rest_1_, bf16[1728,128]{1,0:T(8,128)(2,1)S(1)} %collective-permute-done.1.rest_2_), custom_call_target="tpu_custom_call" | custom-call | flops 64000000000 | bytes 1000000 | tf_op jit(solution)/shard_map/early/pallas_call | solution.py:389
  39.4 3.6 %collective-permute-done.3.rest_4_ = bf16[1728,128]{1,0:T(8,128)(2,1)S(1)} collective-permute-done((bf16[1728,128]{1,0:T(8,128)(2,1)S(1)}, bf16[1728,128]{1,0:T(8,128)(2,1)S(1)}, u32[]{:S(2)}, u32[]{:S(2)}) %collective-permute-start.3) | collective-permute-done | bytes 442400 | tf_op jit(solution)/shard_map/ppermute | solution.py:361
  43.0 1.9 %collective-permute-start.12 = (bf16[1536,128]{1,0:T(8,128)(2,1)S(1)}, bf16[1536,128]{1,0:T(8,128)(2,1)S(1)}, u32[]{:S(2)}, u32[]{:S(2)}) collective-permute-start(bf16[1536,128]{1,0:T(8,128)(2,1)S(1)} %copy-done.1), channel_id=1, source_target_pairs={{0,2},{1,3},{2,0},{3,1},{4,6},{5,7},{6,4},{7,5},{8,10},{9,11},{10,... | collective-permute-start | bytes 1179656 | tf_op jit(solution)/shard_map/ppermute | solution.py:357
  44.9 2.4 %collective-permute-start.11 = (bf16[1536,128]{1,0:T(8,128)(2,1)S(1)}, bf16[1536,128]{1,0:T(8,128)(2,1)S(1)}, u32[]{:S(2)}, u32[]{:S(2)}) collective-permute-start(bf16[1536,128]{1,0:T(8,128)(2,1)S(1)} %copy-done.1), channel_id=1, source_target_pairs={{0,1},{1,0},{2,3},{3,2},{4,5},{5,4},{6,7},{7,6},{8,9},{9,8},{10,11... | collective-permute-start | bytes 1179656 | tf_op jit(solution)/shard_map/ppermute | solution.py:357
  47.3 7.4 %late.2 = (bf16[48,1536]{1,0:T(8,128)(2,1)S(1)}, bf16[48,1536]{1,0:T(8,128)(2,1)S(1)}, bf16[48,1536]{1,0:T(8,128)(2,1)S(1)}, bf16[48,1536]{1,0:T(8,128)(2,1)S(1)...) custom-call(s32[2]{0:T(128)S(1)} %pad_add_fusion.here, ...), custom_call_target="tpu_custom_call" | custom-call | flops 3200000000 | bytes 1000000 | tf_op jit(solution)/shard_map/late/pallas_call | solution.py:401
  54.8 1.5 %collective-permute-start.5 = (bf16[48,1536]{1,0:T(8,128)(2,1)S(1)}, bf16[48,1536]{1,0:T(8,128)(2,1)S(1)}, u32[]{:S(2)}, u32[]{:S(2)}) collective-permute-start(bf16[48,1536]{1,0:T(8,128)(2,1)S(1)} %get-tuple-element.33), channel_id=1, source_target_pairs={{0,8},{4,12},{8,0},{12,4},{16,24},{20,28},{24,16},{28,20},{1,9},{5... | collective-permute-start | bytes 442376 | tf_op jit(solution)/shard_map/ppermute | solution.py:420
  56.3 0.0 collective-permute-start.6
  56.3 0.6 collective-permute-start.7
  56.9 5.5 %collective-permute-done.12.rest_2_ = bf16[1536,128]{1,0:T(8,128)(2,1)S(1)} collective-permute-done((bf16[1536,128]{1,0:T(8,128)(2,1)S(1)}, bf16[1536,128]{1,0:T(8,128)(2,1)S(1)}, u32[]{:S(2)}, u32[]{:S(2)}) %collective-permute-start.12) | collective-permute-done | bytes 393248 | tf_op jit(solution)/shard_map/ppermute | solution.py:357
  62.4 0.1 collective-permute-done.11.rest_1_
  62.5 0.7 collective-permute-start.13
  63.2 0.0 collective-permute-done.5.rest_2_
  63.2 1.3 %collective-permute-start.14 = (bf16[1536,128]{1,0:T(8,128)(2,1)S(1)}, bf16[1536,128]{1,0:T(8,128)(2,1)S(1)}, u32[]{:S(2)}, u32[]{:S(2)}) collective-permute-start(bf16[1536,128]{1,0:T(8,128)(2,1)S(1)} %collective-permute-done.12.rest_2_), channel_id=1, source_target_pairs={{1,0},{2,3},{5,4},{6,7},{9,8},{10,11},{13,12},{14,15},{17,16},{18,... | collective-permute-start | bytes 1179656 | tf_op jit(solution)/shard_map/ppermute | solution.py:361
  64.5 0.0 slice-start.1
  64.5 0.0 slice-start.2
  64.5 0.0 slice-start.3
  64.5 8.8 %early.3.rest_4_ = bf16[1536,512]{1,0:T(8,128)(2,1)S(1)} custom-call(s32[2]{0:T(128)S(1)} %pad_add_fusion.here, bf16[1536,128]{1,0:T(8,128)(2,1)S(1)} %copy-done.1, bf16[1536,128]{1,0:T(8,128)(2,1)S(1)} %collective-permute-done.11.rest_1_, bf16[1536,128]{1,0:T(8,128)(2,1)S(1)} %collective-permute-done.12.rest_2_, ...), custom_call_target="tpu_custom_call" | custom-call | flops 64000000000 | bytes 1000000 | tf_op jit(solution)/shard_map/early/pallas_call | solution.py:389
  73.4 0.0 collective-permute-done.6.rest_3_
  73.4 1.0 collective-permute-start.4
  74.4 0.0 collective-permute-done.7.rest_4_
  74.4 2.4 %collective-permute-start.9 = (bf16[48,1536]{1,0:T(8,128)(2,1)S(1)}, bf16[48,1536]{1,0:T(8,128)(2,1)S(1)}, u32[]{:S(2)}, u32[]{:S(2)}) collective-permute-start(bf16[48,1536]{1,0:T(8,128)(2,1)S(1)} %get-tuple-element.37), channel_id=1, source_target_pairs={{0,24},{4,28},{8,16},{12,20},{16,8},{20,12},{24,0},{28,4},{1,25},{... | collective-permute-start | bytes 442376 | tf_op jit(solution)/shard_map/ppermute | solution.py:420
  76.8 0.0 collective-permute-done.8.rest_5_
  76.8 0.0 collective-permute-start.10
  76.8 0.3 collective-permute-done.14.rest_1_
  77.1 5.8 %late.3 = (bf16[48,1536]{1,0:T(8,128)(2,1)S(1)}, bf16[48,1536]{1,0:T(8,128)(2,1)S(1)}, bf16[48,1536]{1,0:T(8,128)(2,1)S(1)}, bf16[48,1536]{1,0:T(8,128)(2,1)S(1)...) custom-call(s32[2]{0:T(128)S(1)} %pad_add_fusion.here, ...), custom_call_target="tpu_custom_call" | custom-call | flops 3200000000 | bytes 1000000 | tf_op jit(solution)/shard_map/late/pallas_call | solution.py:401
  82.9 0.1 collective-permute-start.15
  82.9 1.2 %collective-permute-start.16 = (bf16[48,1536]{1,0:T(8,128)(2,1)S(1)}, bf16[48,1536]{1,0:T(8,128)(2,1)S(1)}, u32[]{:S(2)}, u32[]{:S(2)}) collective-permute-start(bf16[48,1536]{1,0:T(8,128)(2,1)S(1)} %get-tuple-element.47), channel_id=1, source_target_pairs={{0,8},{4,12},{8,0},{12,4},{16,24},{20,28},{24,16},{28,20},{1,9},{5... | collective-permute-start | bytes 442376 | tf_op jit(solution)/shard_map/ppermute | solution.py:420
  84.2 0.6 collective-permute-start.17
  84.8 0.6 collective-permute-start.18
  85.4 1.1 %collective-permute-start.19 = (bf16[48,1536]{1,0:T(8,128)(2,1)S(1)}, bf16[48,1536]{1,0:T(8,128)(2,1)S(1)}, u32[]{:S(2)}, u32[]{:S(2)}) collective-permute-start(bf16[48,1536]{1,0:T(8,128)(2,1)S(1)} %get-tuple-element.50), channel_id=1, source_target_pairs={{0,20},{4,16},{8,28},{12,24},{16,4},{20,0},{24,12},{28,8},{1,21},{... | collective-permute-start | bytes 442376 | tf_op jit(solution)/shard_map/ppermute | solution.py:420
  86.5 1.8 %collective-permute-start.20 = (bf16[48,1536]{1,0:T(8,128)(2,1)S(1)}, bf16[48,1536]{1,0:T(8,128)(2,1)S(1)}, u32[]{:S(2)}, u32[]{:S(2)}) collective-permute-start(bf16[48,1536]{1,0:T(8,128)(2,1)S(1)} %get-tuple-element.51), channel_id=1, source_target_pairs={{0,24},{4,28},{8,16},{12,20},{16,8},{20,12},{24,0},{28,4},{1,25},{... | collective-permute-start | bytes 442376 | tf_op jit(solution)/shard_map/ppermute | solution.py:420
  88.3 1.4 %collective-permute-done.16.rest_2_ = bf16[48,1536]{1,0:T(8,128)(2,1)S(1)} collective-permute-done((bf16[48,1536]{1,0:T(8,128)(2,1)S(1)}, bf16[48,1536]{1,0:T(8,128)(2,1)S(1)}, u32[]{:S(2)}, u32[]{:S(2)}) %collective-permute-start.16) | collective-permute-done | bytes 147488 | tf_op jit(solution)/shard_map/ppermute | solution.py:420
  89.7 1.0 collect.1.early
  90.7 1.3 %collective-permute-done.17.rest_3_ = bf16[48,1536]{1,0:T(8,128)(2,1)S(1)} collective-permute-done((bf16[48,1536]{1,0:T(8,128)(2,1)S(1)}, bf16[48,1536]{1,0:T(8,128)(2,1)S(1)}, u32[]{:S(2)}, u32[]{:S(2)}) %collective-permute-start.17) | collective-permute-done | bytes 147488 | tf_op jit(solution)/shard_map/ppermute | solution.py:420
  91.9 7.9 %collective-permute-done.19.rest_5_ = bf16[48,1536]{1,0:T(8,128)(2,1)S(1)} collective-permute-done((bf16[48,1536]{1,0:T(8,128)(2,1)S(1)}, bf16[48,1536]{1,0:T(8,128)(2,1)S(1)}, u32[]{:S(2)}, u32[]{:S(2)}) %collective-permute-start.19) | collective-permute-done | bytes 147488 | tf_op jit(solution)/shard_map/ppermute | solution.py:420
  99.9 8.3 %final.1 = f32[48,768,128]{2,1,0:T(8,128)} custom-call(s32[2]{0:T(128)S(1)} %pad_add_fusion.here, bf16[48,192,768]{2,1,0:T(8,128)(2,1)S(1)} %bitcast.10, f32[9216,128]{1,0:T(8,128)S(1)} %collect.1.early, bf16[48,1536]{1,0:T(8,128)(2,1)S(1)} %get-tuple-element.45.rest_0_, bf16[48,1536]{1,0:T(8,128)(2,1)S(1)} %collective-permute-done.15.rest_1_, ...), custom_call_target="tpu_custom_call" | custom-call | tf_op jit(solution)/shard_map/final/pallas_call | solution.py:436
  (19 shorter events, 0.0 us)
Async XLA Ops:
  4.6 24.1 %collective-permute-start.1 = (bf16[1728,128]{1,0:T(8,128)(2,1)}, bf16[1728,128]{1,0:T(8,128)(2,1)S(1)}, u32[]{:S(2)}, u32[]{:S(2)}) collective-permute-start(bf16[1728,128]{1,0:T(8,128)(2,1)} %get-tuple-element.30.rest_0_), channel_id=1, source_target_pairs={{0,2},{1,3},{2,0},{3,1},{4,6},{5,7},{6,4},{7,5},{8,10},{9,11},{10,... | collective-permute-start | bytes 1327112 | tf_op jit(solution)/shard_map/ppermute | solution.py:357
  8.7 20.2 %collective-permute-start = (bf16[1728,128]{1,0:T(8,128)(2,1)}, bf16[1728,128]{1,0:T(8,128)(2,1)S(1)}, u32[]{:S(2)}, u32[]{:S(2)}) collective-permute-start(bf16[1728,128]{1,0:T(8,128)(2,1)} %get-tuple-element.30.rest_0_), channel_id=1, source_target_pairs={{0,1},{1,0},{2,3},{3,2},{4,5},{5,4},{6,7},{7,6},{8,9},{9,8},{10,11... | collective-permute-start | bytes 1327112 | tf_op jit(solution)/shard_map/ppermute | solution.py:357
  10.3 32.7 %copy-start.1 = (bf16[1536,128]{1,0:T(8,128)(2,1)S(1)}, bf16[1536,128]{1,0:T(8,128)(2,1)}, u32[]{:S(2)}) copy-start(bf16[1536,128]{1,0:T(8,128)(2,1)} %get-tuple-element.41.rest_0_) | copy-start | bytes 1179652
  28.8 14.2 %collective-permute-start.2 = (bf16[1728,128]{1,0:T(8,128)(2,1)}, bf16[1728,128]{1,0:T(8,128)(2,1)S(1)}, u32[]{:S(2)}, u32[]{:S(2)}) collective-permute-start(bf16[1728,128]{1,0:T(8,128)(2,1)} %get-tuple-element.30.rest_0_), channel_id=1, source_target_pairs={{1,2},{2,1},{5,6},{6,5},{9,10},{10,9},{13,14},{14,13},{17,18},{18,... | collective-permute-start | bytes 1327112 | tf_op jit(solution)/shard_map/ppermute | solution.py:357
  29.5 13.5 %collective-permute-start.3 = (bf16[1728,128]{1,0:T(8,128)(2,1)S(1)}, bf16[1728,128]{1,0:T(8,128)(2,1)S(1)}, u32[]{:S(2)}, u32[]{:S(2)}) collective-permute-start(bf16[1728,128]{1,0:T(8,128)(2,1)S(1)} %collective-permute-done.1.rest_2_), channel_id=1, source_target_pairs={{1,0},{2,3},{5,4},{6,7},{9,8},{10,11},{13,12},{14,15},{17,16},{18,... | collective-permute-start | bytes 1327112 | tf_op jit(solution)/shard_map/ppermute | solution.py:361
  30.8 1.0 copy-start
  43.0 19.4 %collective-permute-start.12 = (bf16[1536,128]{1,0:T(8,128)(2,1)S(1)}, bf16[1536,128]{1,0:T(8,128)(2,1)S(1)}, u32[]{:S(2)}, u32[]{:S(2)}) collective-permute-start(bf16[1536,128]{1,0:T(8,128)(2,1)S(1)} %copy-done.1), channel_id=1, source_target_pairs={{0,2},{1,3},{2,0},{3,1},{4,6},{5,7},{6,4},{7,5},{8,10},{9,11},{10,... | collective-permute-start | bytes 1179656 | tf_op jit(solution)/shard_map/ppermute | solution.py:357
  44.9 17.6 %collective-permute-start.11 = (bf16[1536,128]{1,0:T(8,128)(2,1)S(1)}, bf16[1536,128]{1,0:T(8,128)(2,1)S(1)}, u32[]{:S(2)}, u32[]{:S(2)}) collective-permute-start(bf16[1536,128]{1,0:T(8,128)(2,1)S(1)} %copy-done.1), channel_id=1, source_target_pairs={{0,1},{1,0},{2,3},{3,2},{4,5},{5,4},{6,7},{7,6},{8,9},{9,8},{10,11... | collective-permute-start | bytes 1179656 | tf_op jit(solution)/shard_map/ppermute | solution.py:357
  47.3 52.5 %slice-start = ((s8[14155776]{0:T(1024)(128)(4,1)}), s8[4194304]{0:T(1024)(128)(4,1)S(1)}, s32[]{:S(2)}) async-start(s8[14155776]{0:T(1024)(128)(4,1)} %bitcast.9), calls=%async_computation | async-start | bytes 8388608
  54.8 8.4 %collective-permute-start.5 = (bf16[48,1536]{1,0:T(8,128)(2,1)S(1)}, bf16[48,1536]{1,0:T(8,128)(2,1)S(1)}, u32[]{:S(2)}, u32[]{:S(2)}) collective-permute-start(bf16[48,1536]{1,0:T(8,128)(2,1)S(1)} %get-tuple-element.33), channel_id=1, source_target_pairs={{0,8},{4,12},{8,0},{12,4},{16,24},{20,28},{24,16},{28,20},{1,9},{5... | collective-permute-start | bytes 442376 | tf_op jit(solution)/shard_map/ppermute | solution.py:420
  56.3 17.1 %collective-permute-start.6 = (bf16[48,1536]{1,0:T(8,128)(2,1)S(1)}, bf16[48,1536]{1,0:T(8,128)(2,1)S(1)}, u32[]{:S(2)}, u32[]{:S(2)}) collective-permute-start(bf16[48,1536]{1,0:T(8,128)(2,1)S(1)} %get-tuple-element.34), channel_id=1, source_target_pairs={{0,12},{4,8},{8,4},{12,0},{16,28},{20,24},{24,20},{28,16},{1,13},{... | collective-permute-start | bytes 442376 | tf_op jit(solution)/shard_map/ppermute | solution.py:420
  56.3 18.1 %collective-permute-start.7 = (bf16[48,1536]{1,0:T(8,128)(2,1)S(1)}, bf16[48,1536]{1,0:T(8,128)(2,1)S(1)}, u32[]{:S(2)}, u32[]{:S(2)}) collective-permute-start(bf16[48,1536]{1,0:T(8,128)(2,1)S(1)} %get-tuple-element.35), channel_id=1, source_target_pairs={{0,16},{4,20},{8,24},{12,28},{16,0},{20,4},{24,8},{28,12},{1,17},{... | collective-permute-start | bytes 442376 | tf_op jit(solution)/shard_map/ppermute | solution.py:420
  62.4 14.4 %collective-permute-start.8 = (bf16[48,1536]{1,0:T(8,128)(2,1)S(1)}, bf16[48,1536]{1,0:T(8,128)(2,1)S(1)}, u32[]{:S(2)}, u32[]{:S(2)}) collective-permute-start(bf16[48,1536]{1,0:T(8,128)(2,1)S(1)} %get-tuple-element.36), channel_id=1, source_target_pairs={{0,20},{4,16},{8,28},{12,24},{16,4},{20,0},{24,12},{28,8},{1,21},{... | collective-permute-start | bytes 442376 | tf_op jit(solution)/shard_map/ppermute | solution.py:420
  62.5 14.6 %collective-permute-start.13 = (bf16[1536,128]{1,0:T(8,128)(2,1)S(1)}, bf16[1536,128]{1,0:T(8,128)(2,1)S(1)}, u32[]{:S(2)}, u32[]{:S(2)}) collective-permute-start(bf16[1536,128]{1,0:T(8,128)(2,1)S(1)} %copy-done.1), channel_id=1, source_target_pairs={{1,2},{2,1},{5,6},{6,5},{9,10},{10,9},{13,14},{14,13},{17,18},{18,... | collective-permute-start | bytes 1179656 | tf_op jit(solution)/shard_map/ppermute | solution.py:357
  63.2 13.9 %collective-permute-start.14 = (bf16[1536,128]{1,0:T(8,128)(2,1)S(1)}, bf16[1536,128]{1,0:T(8,128)(2,1)S(1)}, u32[]{:S(2)}, u32[]{:S(2)}) collective-permute-start(bf16[1536,128]{1,0:T(8,128)(2,1)S(1)} %collective-permute-done.12.rest_2_), channel_id=1, source_target_pairs={{1,0},{2,3},{5,4},{6,7},{9,8},{10,11},{13,12},{14,15},{17,16},{18,... | collective-permute-start | bytes 1179656 | tf_op jit(solution)/shard_map/ppermute | solution.py:361
  64.5 35.4 %slice-start.1 = ((s8[14155776]{0:T(1024)(128)(4,1)}), s8[4194304]{0:T(1024)(128)(4,1)S(1)}, s32[]{:S(2)}) async-start(s8[14155776]{0:T(1024)(128)(4,1)} %bitcast.9), calls=%async_computation.1 | async-start | bytes 8388608
  64.5 35.4 %slice-start.2 = ((s8[14155776]{0:T(1024)(128)(4,1)}), s8[4194304]{0:T(1024)(128)(4,1)S(1)}, s32[]{:S(2)}) async-start(s8[14155776]{0:T(1024)(128)(4,1)} %bitcast.9), calls=%async_computation.2 | async-start | bytes 8388608
  64.5 35.4 %slice-start.3 = ((s8[14155776]{0:T(1024)(128)(4,1)}), s8[1572864]{0:T(1024)(128)(4,1)S(1)}, s32[]{:S(2)}) async-start(s8[14155776]{0:T(1024)(128)(4,1)} %bitcast.9), calls=%async_computation.3 | async-start | bytes 3145728
  73.4 10.8 %collective-permute-start.4 = (bf16[48,1536]{1,0:T(8,128)(2,1)S(1)}, bf16[48,1536]{1,0:T(8,128)(2,1)S(1)}, u32[]{:S(2)}, u32[]{:S(2)}) collective-permute-start(bf16[48,1536]{1,0:T(8,128)(2,1)S(1)} %get-tuple-element.32), channel_id=1, source_target_pairs={{0,4},{4,0},{8,12},{12,8},{16,20},{20,16},{24,28},{28,24},{1,5},{5... | collective-permute-start | bytes 442376 | tf_op jit(solution)/shard_map/ppermute | solution.py:420
  74.4 10.4 %collective-permute-start.9 = (bf16[48,1536]{1,0:T(8,128)(2,1)S(1)}, bf16[48,1536]{1,0:T(8,128)(2,1)S(1)}, u32[]{:S(2)}, u32[]{:S(2)}) collective-permute-start(bf16[48,1536]{1,0:T(8,128)(2,1)S(1)} %get-tuple-element.37), channel_id=1, source_target_pairs={{0,24},{4,28},{8,16},{12,20},{16,8},{20,12},{24,0},{28,4},{1,25},{... | collective-permute-start | bytes 442376 | tf_op jit(solution)/shard_map/ppermute | solution.py:420
  76.8 8.6 %collective-permute-start.10 = (bf16[48,1536]{1,0:T(8,128)(2,1)S(1)}, bf16[48,1536]{1,0:T(8,128)(2,1)S(1)}, u32[]{:S(2)}, u32[]{:S(2)}) collective-permute-start(bf16[48,1536]{1,0:T(8,128)(2,1)S(1)} %get-tuple-element.38), channel_id=1, source_target_pairs={{0,28},{4,24},{8,20},{12,16},{16,12},{20,8},{24,4},{28,0},{1,29},{... | collective-permute-start | bytes 442376 | tf_op jit(solution)/shard_map/ppermute | solution.py:420
  82.9 3.7 %collective-permute-start.15 = (bf16[48,1536]{1,0:T(8,128)(2,1)S(1)}, bf16[48,1536]{1,0:T(8,128)(2,1)S(1)}, u32[]{:S(2)}, u32[]{:S(2)}) collective-permute-start(bf16[48,1536]{1,0:T(8,128)(2,1)S(1)} %get-tuple-element.46), channel_id=1, source_target_pairs={{0,4},{4,0},{8,12},{12,8},{16,20},{20,16},{24,28},{28,24},{1,5},{5... | collective-permute-start | bytes 442376 | tf_op jit(solution)/shard_map/ppermute | solution.py:420
  82.9 6.7 %collective-permute-start.16 = (bf16[48,1536]{1,0:T(8,128)(2,1)S(1)}, bf16[48,1536]{1,0:T(8,128)(2,1)S(1)}, u32[]{:S(2)}, u32[]{:S(2)}) collective-permute-start(bf16[48,1536]{1,0:T(8,128)(2,1)S(1)} %get-tuple-element.47), channel_id=1, source_target_pairs={{0,8},{4,12},{8,0},{12,4},{16,24},{20,28},{24,16},{28,20},{1,9},{5... | collective-permute-start | bytes 442376 | tf_op jit(solution)/shard_map/ppermute | solution.py:420
  84.2 7.7 %collective-permute-start.17 = (bf16[48,1536]{1,0:T(8,128)(2,1)S(1)}, bf16[48,1536]{1,0:T(8,128)(2,1)S(1)}, u32[]{:S(2)}, u32[]{:S(2)}) collective-permute-start(bf16[48,1536]{1,0:T(8,128)(2,1)S(1)} %get-tuple-element.48), channel_id=1, source_target_pairs={{0,12},{4,8},{8,4},{12,0},{16,28},{20,24},{24,20},{28,16},{1,13},{... | collective-permute-start | bytes 442376 | tf_op jit(solution)/shard_map/ppermute | solution.py:420
  84.8 7.1 %collective-permute-start.18 = (bf16[48,1536]{1,0:T(8,128)(2,1)S(1)}, bf16[48,1536]{1,0:T(8,128)(2,1)S(1)}, u32[]{:S(2)}, u32[]{:S(2)}) collective-permute-start(bf16[48,1536]{1,0:T(8,128)(2,1)S(1)} %get-tuple-element.49), channel_id=1, source_target_pairs={{0,16},{4,20},{8,24},{12,28},{16,0},{20,4},{24,8},{28,12},{1,17},{... | collective-permute-start | bytes 442376 | tf_op jit(solution)/shard_map/ppermute | solution.py:420
  85.4 14.4 %collective-permute-start.19 = (bf16[48,1536]{1,0:T(8,128)(2,1)S(1)}, bf16[48,1536]{1,0:T(8,128)(2,1)S(1)}, u32[]{:S(2)}, u32[]{:S(2)}) collective-permute-start(bf16[48,1536]{1,0:T(8,128)(2,1)S(1)} %get-tuple-element.50), channel_id=1, source_target_pairs={{0,20},{4,16},{8,28},{12,24},{16,4},{20,0},{24,12},{28,8},{1,21},{... | collective-permute-start | bytes 442376 | tf_op jit(solution)/shard_map/ppermute | solution.py:420
  86.5 13.3 %collective-permute-start.20 = (bf16[48,1536]{1,0:T(8,128)(2,1)S(1)}, bf16[48,1536]{1,0:T(8,128)(2,1)S(1)}, u32[]{:S(2)}, u32[]{:S(2)}) collective-permute-start(bf16[48,1536]{1,0:T(8,128)(2,1)S(1)} %get-tuple-element.51), channel_id=1, source_target_pairs={{0,24},{4,28},{8,16},{12,20},{16,8},{20,12},{24,0},{28,4},{1,25},{... | collective-permute-start | bytes 442376 | tf_op jit(solution)/shard_map/ppermute | solution.py:420
  89.7 10.2 %collective-permute-start.21 = (bf16[48,1536]{1,0:T(8,128)(2,1)S(1)}, bf16[48,1536]{1,0:T(8,128)(2,1)S(1)}, u32[]{:S(2)}, u32[]{:S(2)}) collective-permute-start(bf16[48,1536]{1,0:T(8,128)(2,1)S(1)} %get-tuple-element.52), channel_id=1, source_target_pairs={{0,28},{4,24},{8,20},{12,16},{16,12},{20,8},{24,4},{28,0},{1,29},{... | collective-permute-start | bytes 442376 | tf_op jit(solution)/shard_map/ppermute | solution.py:420
